TPU v7x, 32 devices: a whole 2x2x4 slice. The times are simulated.
32 devices in a mesh: seq: 8 (over z, x), tp: 4 (over y, core).
Axes of the slice: x: 2, y: 2, z: 4, core: 2. Of those that a mesh axis runs over, the one named last changes fastest.
Arguments:
- tokens: bfloat16 [2, 2048, 2048], P(None, 'seq', 'tp'), may hold values from -6 to 6
- norm_gain: bfloat16 [2, 2048], P(None, 'tp'), may hold values from 0.5 to 1.5
- input_weight: bfloat16 [2, 2048, 2, 4096], P(None, None, None, 'tp'), may hold values from -0.125 to 0.125
- conv_weight: bfloat16 [2, 4, 4096], P(None, None, 'tp'), may hold values from -3 to 3
- conv_bias: bfloat16 [2, 4096], P(None, 'tp'), may hold values from -3 to 3
- select_weight: bfloat16 [2, 4096, 160], P(None, 'tp'), may hold values from -0.09375 to 0.09375
- step_weight: bfloat16 [2, 128, 4096], P(None, None, 'tp'), may hold values from -0.5 to 0.5
- step_bias: float32 [2, 4096], P(None, 'tp'), may hold values from -9 to -2.3
- skip_gain: bfloat16 [2, 4096], P(None, 'tp'), may hold values from 0.5 to 1.5
- out_weight: bfloat16 [2, 4096, 2048], P(None, 'tp'), may hold values from -0.25 to 0.25
- cotangent: bfloat16 [2, 2048, 2048], P(None, 'seq', 'tp'), may hold values from -6 to 6
- doc_lengths: int32 [2, 64], replicated, may hold values from 0 to 2048, as said below
- doc_offsets: int32 [2, 64], replicated, may hold values from 0 to 2048, as said below
Outputs:
- layer_out: bfloat16 [2, 2048, 2048], P(None, 'seq', 'tp')
- tokens_grad: bfloat16 [2, 2048, 2048], P(None, 'seq', 'tp')
- gain_grad: float32 [2, 2048], P(None, 'tp')
- inweight_grad: float32 [2, 2048, 2, 4096], P(None, 'seq', None, 'tp')
- convweight_grad: float32 [2, 4, 4096], P(None, None, 'tp')
- convbias_grad: float32 [2, 4096], P(None, 'tp')
- select_grad: float32 [2, 4096, 128], P(None, 'tp', 'seq')
- keyquery_grad: float32 [2, 4096, 32], P(None, 'tp')
- step_grad: float32 [2, 128, 4096], P(None, 'seq', 'tp')
- stepbias_grad: float32 [2, 4096], P(None, 'tp')
- skip_grad: float32 [2, 4096], P(None, 'tp')
- outweight_grad: float32 [2, 4096, 2048], P(None, 'tp', 'seq')
Inputs may be any that keep to these rules, and one draw needn't show every extreme that they name: `doc_offsets`: in each micro-batch the slots' offsets do not fall and start at 0; a document fills positions offset to offset + length - 1, before the next slot's offset, and positions between documents are padding. Slots that hold no document have offset 2048 and length 0. In one micro-batch, drawn from the seed, a single document fills all 2048 positions; in the others documents are 64 to 1024 positions long, except one cut by the stream's end. `doc_lengths`: lengths of the slots described with doc_offsets.
All inputs are finite; a program needn't handle non-finite values.
Results may differ from a plain program's by a relative error of at most 0.03.
Values may be sent and summed in bfloat16 or wider, within the bound.
No kernel may reach another device: no remote copies, remote signals or barrier semaphores. Data moves between devices by JAX's collectives and lax.ppermute only.
A program may use at most 320 MiB of HBM per device.

v0:
```python
import math

import jax
import jax.numpy as jnp
from jax import lax
from jax.sharding import PartitionSpec as P

norm_epsilon = 1e-05


def shifted(value, axis, steps):
    count = lax.axis_size(axis)
    leading, last = (max(0, -steps), min(count, count - steps))
    return lax.ppermute(value, axis, [(source, source + steps) for source in range(leading, last)])


def prefix(value, axis, join, neutral):
    place = lax.axis_index(axis)
    gathered = jax.tree.map(
        lambda a, kind: lax.all_gather(a.astype(kind), axis), value, (jnp.bfloat16, jnp.bfloat16)
    )
    state = jax.tree.map(lambda a, e: jnp.zeros_like(a) + jnp.asarray(e, a.dtype), value, neutral)

    def one(turn, state):
        return join(
            state,
            jax.tree.map(
                lambda a, own: lax.dynamic_index_in_dim(a, turn, 0, False).astype(own.dtype),
                gathered,
                value,
            ),
        )

    return lax.fori_loop(0, place, one, state)


def prefix_2(value, axis, combine, identity):
    size, place = (lax.axis_size(axis), lax.axis_index(axis))
    everything = jax.tree.map(
        lambda part, kind: lax.all_gather(part.astype(kind), axis),
        value,
        jax.tree.map(lambda a: jnp.bfloat16 if a.dtype == jnp.float32 else a.dtype, value),
    )
    start = jax.tree.map(
        lambda part, zero: jnp.broadcast_to(jnp.asarray(zero, part.dtype), part.shape),
        value,
        identity,
    )

    def turn(k, before):
        at = size - 1 - k
        reached = at > place
        new = combine(
            before, jax.tree.map(lambda part, own: part[at].astype(own.dtype), everything, value)
        )
        return jax.tree.map(lambda a, b: jnp.where(reached, a, b), new, before)

    return lax.fori_loop(0, size, turn, start)


def gated_silu(argument):
    return argument * jax.nn.sigmoid(argument)


def silu_slope(argument):
    logistic = jax.nn.sigmoid(argument)
    return logistic * (1.0 + argument * (1.0 - logistic))


def link(earlier, latter):
    return (earlier[0] * latter[0], latter[0] * earlier[1] + latter[1])


def block_pass(carry_pair, pieces):
    decay_total, carry_state = carry_pair
    write_rate, key_state, query_state, conv_act, keep_mask = pieces
    outputs = []
    for row in range(write_rate.shape[1]):
        key_row = key_state[:, row]
        rate_row = write_rate[:, row]
        decay = (1.0 - rate_row[:, None, :] * (key_row * key_row)[:, :, None]) * keep_mask[:, row][
            :, None, None
        ]
        carry_state = (
            decay * carry_state + (rate_row * conv_act[:, row])[:, None, :] * key_row[:, :, None]
        )
        decay_total = decay_total * decay
        outputs.append(jnp.sum(carry_state * query_state[:, row][:, :, None], axis=1))
    return ((decay_total, carry_state), jnp.stack(outputs, axis=1))


def to_blocks(argument, block_rows):
    array_shape = argument.shape
    reshaped = argument.reshape(
        (array_shape[0], array_shape[1] // block_rows, block_rows) + array_shape[2:]
    )
    return jnp.moveaxis(reshaped, 1, 0)


def run_blocks(write_rate, key_state, query_state, conv_act, keep_mask, carry_state):
    block_rows = math.gcd(write_rate.shape[1], 16)
    pieces = tuple(
        (
            to_blocks(member, block_rows)
            for member in (write_rate, key_state, query_state, conv_act, keep_mask)
        )
    )
    start_pair = (jnp.ones_like(carry_state), carry_state)
    final_pair, output = lax.scan(jax.checkpoint(block_pass), start_pair, pieces)
    output = jnp.moveaxis(output, 0, 1).reshape(write_rate.shape)
    return (output, final_pair)


def doc_masks(doc_lengths, doc_offsets, positions):
    before = doc_offsets[:, None, :] <= positions[None, :, None]
    starts = jnp.max(jnp.where(before, doc_offsets[:, None, :], 0), axis=2)
    doc_ends = jnp.max(
        jnp.where(before, doc_offsets[:, None, :] + doc_lengths[:, None, :], 0), axis=2
    )
    return (starts, (positions[None, :] < doc_ends).astype(jnp.float32))


def conv_forward(projected_rows, previous, conv_weight, conv_bias, tap_masks):
    edge_rows = conv_weight.shape[0] - 1
    row_count = projected_rows.shape[1]
    extended = jnp.concatenate(
        [previous.astype(jnp.float32), projected_rows[:, :, 0, :].astype(jnp.float32)], axis=1
    )
    running = jnp.broadcast_to(conv_bias.astype(jnp.float32), extended[:, edge_rows:].shape)
    for shift_back in range(edge_rows + 1):
        window = extended[:, edge_rows - shift_back : edge_rows - shift_back + row_count]
        running = (
            running
            + conv_weight[shift_back].astype(jnp.float32)
            * window
            * tap_masks[shift_back][:, :, None]
        )
    return (extended, running)


def forward_layer(hidden, layer_weights, valid_mask, keep_mask, tap_masks):
    (
        norm_gain,
        input_weight,
        conv_weight,
        conv_bias,
        select_weight,
        step_weight,
        step_bias,
        skip_gain,
        out_weight,
    ) = layer_weights
    square_sums = lax.psum(jnp.sum(hidden * hidden, axis=2), "tp")
    model_width = input_weight.shape[0]
    inverse_norm = lax.rsqrt(square_sums / model_width + norm_epsilon)
    normalized_rows = (hidden * inverse_norm[:, :, None] * norm_gain.astype(jnp.float32)).astype(
        jnp.bfloat16
    )
    complete_rows = lax.all_gather(normalized_rows, "tp", axis=2, tiled=True)
    projected_rows = jnp.einsum(
        "pbh,htg->pbtg", complete_rows, input_weight, preferred_element_type=jnp.float32
    ).astype(jnp.bfloat16)
    edge_rows = conv_weight.shape[0] - 1
    row_count = hidden.shape[1]
    previous = shifted(projected_rows[:, row_count - edge_rows :, 0, :], "seq", 1)
    extended, conv_out = conv_forward(projected_rows, previous, conv_weight, conv_bias, tap_masks)
    conv_act = gated_silu(conv_out).astype(jnp.bfloat16)
    selection = lax.psum(
        jnp.einsum(
            "mri,ic->mrc", conv_act, select_weight, preferred_element_type=jnp.float32
        ).astype(jnp.bfloat16),
        "tp",
    ).astype(jnp.float32)
    rank_count = step_weight.shape[0]
    state_count = (selection.shape[2] - rank_count) // 2
    low_rank = selection[:, :, :rank_count].astype(jnp.bfloat16)
    key_state = selection[:, :, rank_count : rank_count + state_count]
    query_state = selection[:, :, rank_count + state_count :]
    pre_step = jnp.einsum("mrk,ki->mri", low_rank, step_weight, preferred_element_type=jnp.float32)
    step_size = jax.nn.softplus(pre_step + step_bias)
    key_norm = jnp.sum(key_state * key_state, axis=2)
    write_rate = step_size / (1.0 + step_size * key_norm[:, :, None])
    act_float = conv_act.astype(jnp.float32)
    start_state = jnp.zeros((hidden.shape[0], state_count, write_rate.shape[2]), jnp.float32)
    _, summary = run_blocks(write_rate, key_state, query_state, act_float, keep_mask, start_state)
    incoming = prefix(
        (summary[0], summary[1]), "seq", link, (jnp.ones_like(start_state), start_state)
    )[1]
    recurrent, _ = run_blocks(write_rate, key_state, query_state, act_float, keep_mask, incoming)
    mixed_out = recurrent + skip_gain.astype(jnp.float32) * act_float
    gated_out = (mixed_out * gated_silu(projected_rows[:, :, 1, :].astype(jnp.float32))).astype(
        jnp.bfloat16
    )
    branch = lax.psum_scatter(
        jnp.einsum("mri,id->mrd", gated_out, out_weight, preferred_element_type=jnp.float32),
        "tp",
        scatter_dimension=2,
        tiled=True,
    )
    new_hidden = hidden + valid_mask[:, :, None] * branch
    kept = (
        hidden,
        inverse_norm,
        complete_rows,
        projected_rows,
        extended,
        conv_out,
        conv_act,
        selection,
        pre_step,
        write_rate,
        incoming,
        summary[0],
        mixed_out,
        gated_out,
    )
    return (new_hidden, kept)


def backward_layer(grad_new, layer_weights, kept, valid_mask, keep_mask, tap_masks):
    (
        norm_gain,
        input_weight,
        conv_weight,
        conv_bias,
        select_weight,
        step_weight,
        step_bias,
        skip_gain,
        out_weight,
    ) = layer_weights
    (
        hidden,
        inverse_norm,
        complete_rows,
        projected_rows,
        extended,
        conv_out,
        conv_act,
        selection,
        pre_step,
        write_rate,
        incoming,
        decay_total,
        mixed_out,
        gated_out,
    ) = kept
    grad_branch = (grad_new * valid_mask[:, :, None]).astype(jnp.bfloat16)
    branch_rows = lax.all_gather(grad_branch, "tp", axis=2, tiled=True)
    grad_gated = jnp.einsum(
        "mrd,id->mri", branch_rows, out_weight, preferred_element_type=jnp.float32
    )
    outweight_grad = jnp.einsum(
        "mri,mrd->id", gated_out, branch_rows, preferred_element_type=jnp.float32
    )
    gate_in = projected_rows[:, :, 1, :].astype(jnp.float32)
    grad_mixed = grad_gated * gated_silu(gate_in)
    grad_gate = grad_gated * mixed_out * silu_slope(gate_in)
    act_float = conv_act.astype(jnp.float32)
    skip_grad = jnp.sum(grad_mixed * act_float, axis=(0, 1))
    rank_count = step_weight.shape[0]
    state_count = (selection.shape[2] - rank_count) // 2
    key_state = selection[:, :, rank_count : rank_count + state_count]
    query_state = selection[:, :, rank_count + state_count :]

    def recurrence(rate_in, key_in, query_in, act_in, state_in):
        output, final_pair = run_blocks(rate_in, key_in, query_in, act_in, keep_mask, state_in)
        return (output, final_pair[1])

    _, pullback = jax.vjp(recurrence, write_rate, key_state, query_state, act_float, incoming)
    first_pass = pullback((grad_mixed, jnp.zeros_like(incoming)))
    carried = prefix_2(
        (decay_total, first_pass[4]),
        "seq",
        link,
        (jnp.ones_like(incoming), jnp.zeros_like(incoming)),
    )[1]
    second = pullback((jnp.zeros_like(grad_mixed), carried))
    grad_rate = first_pass[0] + second[0]
    grad_key = first_pass[1] + second[1]
    grad_query = first_pass[2] + second[2]
    grad_act = first_pass[3] + second[3] + grad_mixed * skip_gain.astype(jnp.float32)
    biased = pre_step + step_bias
    step_size = jax.nn.softplus(biased)
    key_norm = jnp.sum(key_state * key_state, axis=2)
    denominator = 1.0 + step_size * key_norm[:, :, None]
    grad_step = grad_rate / (denominator * denominator)
    grad_norm_key = -jnp.sum(grad_step * step_size * step_size, axis=2)
    grad_key = grad_key + 2.0 * key_state * grad_norm_key[:, :, None]
    grad_pre = grad_step * jax.nn.sigmoid(biased)
    stepbias_grad = jnp.sum(grad_pre, axis=(0, 1))
    grad_pre_low = grad_pre.astype(jnp.bfloat16)
    low_rank = selection[:, :, :rank_count].astype(jnp.bfloat16)
    step_grad = jnp.einsum(
        "mrk,mri->ki", low_rank, grad_pre_low, preferred_element_type=jnp.float32
    )
    grad_rank = jnp.einsum(
        "mri,ki->mrk", grad_pre_low, step_weight, preferred_element_type=jnp.float32
    )
    grad_selection = lax.psum(
        jnp.concatenate([grad_rank, grad_key, grad_query], axis=2).astype(jnp.bfloat16), "tp"
    )
    select_full = jnp.einsum(
        "mri,mrc->ic", conv_act, grad_selection, preferred_element_type=jnp.float32
    )
    rank_select = select_full[:, :rank_count]
    keyquery_part = select_full[:, rank_count:]
    grad_act = grad_act + jnp.einsum(
        "mrc,ic->mri", grad_selection, select_weight, preferred_element_type=jnp.float32
    )
    grad_conv = grad_act * silu_slope(conv_out)
    convbias_grad = jnp.sum(grad_conv, axis=(0, 1))
    edge_rows = conv_weight.shape[0] - 1
    row_count = grad_conv.shape[1]
    tap_grads = []
    grad_extended = jnp.zeros(extended.shape, jnp.float32)
    for shift_back in range(edge_rows + 1):
        masked = grad_conv * tap_masks[shift_back][:, :, None]
        window = extended[:, edge_rows - shift_back : edge_rows - shift_back + row_count]
        tap_grads.append(jnp.sum(masked * window, axis=(0, 1)))
        grad_extended = grad_extended + jnp.pad(
            masked * conv_weight[shift_back].astype(jnp.float32),
            ((0, 0), (edge_rows - shift_back, shift_back), (0, 0)),
        )
    convweight_grad = jnp.stack(tap_grads, axis=0)
    returned = shifted(grad_extended[:, :edge_rows], "seq", -1)
    grad_conv_in = grad_extended[:, edge_rows:] + jnp.pad(
        returned, ((0, 0), (row_count - edge_rows, 0), (0, 0))
    )
    projection_gradient = jnp.stack([grad_conv_in, grad_gate], axis=2).astype(jnp.bfloat16)
    inweight_grad = jnp.einsum(
        "bsz,bsjk->zjk", complete_rows, projection_gradient, preferred_element_type=jnp.float32
    )
    grad_normed = lax.psum_scatter(
        jnp.einsum(
            "paqe,xqe->pax", projection_gradient, input_weight, preferred_element_type=jnp.float32
        ).astype(jnp.bfloat16),
        "tp",
        scatter_dimension=2,
        tiled=True,
    ).astype(jnp.float32)
    gain_float = norm_gain.astype(jnp.float32)
    gain_grad = jnp.sum(grad_normed * hidden * inverse_norm[:, :, None], axis=(0, 1))
    scaled = grad_normed * gain_float
    inner_sum = lax.psum(jnp.sum(scaled * hidden, axis=2), "tp")
    model_width = input_weight.shape[0]
    cubed = inverse_norm * inverse_norm * inverse_norm
    grad_hidden = (
        grad_new
        + inverse_norm[:, :, None] * scaled
        - hidden * (cubed * inner_sum / model_width)[:, :, None]
    )
    return (
        grad_hidden,
        (inweight_grad, rank_select, step_grad, outweight_grad),
        (gain_grad, convweight_grad, convbias_grad, stepbias_grad, skip_grad, keyquery_part),
    )


def reduce_weights(inweight_grad, select_grad, step_grad, outweight_grad):
    return (
        lax.psum_scatter(
            inweight_grad.astype(jnp.bfloat16), "seq", scatter_dimension=1, tiled=True
        ).astype(jnp.float32),
        lax.psum_scatter(
            select_grad.astype(jnp.bfloat16), "seq", scatter_dimension=2, tiled=True
        ).astype(jnp.float32),
        lax.psum_scatter(
            step_grad.astype(jnp.bfloat16), "seq", scatter_dimension=1, tiled=True
        ).astype(jnp.float32),
        lax.psum_scatter(
            outweight_grad.astype(jnp.bfloat16), "seq", scatter_dimension=2, tiled=True
        ).astype(jnp.float32),
    )


def on_device(
    tokens,
    norm_gain,
    input_weight,
    conv_weight,
    conv_bias,
    select_weight,
    step_weight,
    step_bias,
    skip_gain,
    out_weight,
    cotangent,
    doc_lengths,
    doc_offsets,
):
    row_count = tokens.shape[1]
    positions = lax.axis_index("seq") * row_count + jnp.arange(row_count, dtype=jnp.int32)
    starts, valid_mask = doc_masks(doc_lengths, doc_offsets, positions)
    keep_mask = (positions[None, :] != starts).astype(jnp.float32)
    tap_masks = [
        (positions[None, :] - shift_back >= starts).astype(jnp.float32)
        for shift_back in range(conv_weight.shape[1])
    ]
    weights = (
        norm_gain,
        input_weight,
        conv_weight,
        conv_bias,
        select_weight,
        step_weight,
        step_bias,
        skip_gain,
        out_weight,
    )
    layers_count = input_weight.shape[0]
    hidden = tokens.astype(jnp.float32)
    saved = []
    for layer_index in range(layers_count):
        layer_weights = tuple((member[layer_index] for member in weights))
        hidden, kept = forward_layer(hidden, layer_weights, valid_mask, keep_mask, tap_masks)
        saved.append(kept)
    layer_out = hidden.astype(jnp.bfloat16)
    grad_hidden = cotangent.astype(jnp.float32)
    reduced_layers = [None] * layers_count
    small_list = [None] * layers_count
    for layer_index in reversed(range(layers_count)):
        layer_weights = tuple((member[layer_index] for member in weights))
        grad_hidden, big_grads, small_grads = backward_layer(
            grad_hidden, layer_weights, saved[layer_index], valid_mask, keep_mask, tap_masks
        )
        small_list[layer_index] = small_grads
        reduced_layers[layer_index] = reduce_weights(
            big_grads[0][None], big_grads[1][None], big_grads[2][None], big_grads[3][None]
        )
    big_out = tuple(
        (
            jnp.concatenate([member[slot_index] for member in reduced_layers], axis=0)
            for slot_index in range(4)
        )
    )
    small_stacked = tuple(
        (
            jnp.stack([member[slot_index] for member in small_list], axis=0)
            for slot_index in range(6)
        )
    )
    small_out = (
        lax.psum(small_stacked[0].astype(jnp.bfloat16), "seq").astype(jnp.float32),
        lax.psum(small_stacked[1].astype(jnp.bfloat16), "seq").astype(jnp.float32),
        lax.psum(small_stacked[2].astype(jnp.bfloat16), "seq").astype(jnp.float32),
        lax.psum(small_stacked[3].astype(jnp.bfloat16), "seq").astype(jnp.float32),
        lax.psum(small_stacked[4].astype(jnp.bfloat16), "seq").astype(jnp.float32),
        lax.psum(small_stacked[5].astype(jnp.bfloat16), "seq").astype(jnp.float32),
    )
    tokens_grad = grad_hidden.astype(jnp.bfloat16)
    return (
        layer_out,
        tokens_grad,
        small_out[0],
        big_out[0],
        small_out[1],
        small_out[2],
        big_out[1],
        small_out[5],
        big_out[2],
        small_out[3],
        small_out[4],
        big_out[3],
    )


def solution(mesh):
    placed = (
        P(None, "seq", "tp"),
        P(None, "tp"),
        P(None, None, None, "tp"),
        P(None, None, "tp"),
        P(None, "tp"),
        P(None, "tp", None),
        P(None, None, "tp"),
        P(None, "tp"),
        P(None, "tp"),
        P(None, "tp", None),
        P(None, "seq", "tp"),
        P(),
        P(),
    )
    return jax.shard_map(
        on_device,
        mesh=mesh,
        in_specs=placed,
        out_specs=(
            P(None, "seq", "tp"),
            P(None, "seq", "tp"),
            P(None, "tp"),
            P(None, "seq", None, "tp"),
            P(None, None, "tp"),
            P(None, "tp"),
            P(None, "tp", "seq"),
            P(None, "tp", None),
            P(None, "seq", "tp"),
            P(None, "tp"),
            P(None, "tp"),
            P(None, "tp", "seq"),
        ),
        check_vma=False,
    )
```

profile of v0, /device:TPU:0, one launch (start us, length us, event | category | flops | bytes accessed | tf_op | source)
XLA Modules:
  0.0 2767.9 jit_solution(5416186018644158338)
XLA Ops:
  9.3 8.4 psum.98
  20.3 14.1 fusion.490
  34.4 8.3 all-gather.11.cloned.1.call-done
  42.7 8.6 fusion.409
  63.3 29.8 %all-reduce.273.cloned.1.call-done = bf16[2,256,160]{1,2,0:T(8,128)(2,1)} async-done(((bf16[2,256,160]{1,2,0:T(8,128)(2,1)}), bf16[2,256,160]{1,2,0:T(8,128)(2,1)}) %all-reduce.273.cloned.1.call-update) | async-done | bytes 163856 | tf_op jit(solution)/shard_map/psum | solution.py:168
  102.3 55.6 %while.228 = (s32[]{:T(128)}, f32[2,16,1024]{2,1,0:T(8,128)S(1)}, f32[2,16,1024]{2,1,0:T(8,128)S(1)}, f32[16,2,16,1024]{3,1,2,0:T(2,128)}, f32[16,2,16,16]{3,1,2...) while((s32[]{:T(128)}, f32[2,16,1024]{2,1,0:T(8,128)S(1)}, ...), condition=%wide.region_7.8_spmd.clone, body=%wide.region_6.7_spmd.clone.sunk | while | flops 5341699 | bytes 2108284 | solution.py:109
  158.0 31.4 %all-gather = bf16[16,16,1024]{2,1,0:T(8,128)(2,1)S(1)} all-gather(bf16[2,16,1024]{2,1,0:T(8,128)(2,1)S(1)} %convert_element_type.447), channel_id=2, replica_groups=mesh['seq'=8,'tp'=4] {'seq'}, dimensions={0}, use_global_device_ids=true | all-gather | bytes 589824 | tf_op jit(solution)/shard_map/all_gather | solution.py:20
  189.4 31.2 %all-gather.1 = bf16[16,16,1024]{2,1,0:T(8,128)(2,1)S(1)} all-gather(bf16[2,16,1024]{2,1,0:T(8,128)(2,1)S(1)} %convert_element_type.448), channel_id=3, replica_groups=mesh['seq'=8,'tp'=4] {'seq'}, dimensions={0}, use_global_device_ids=true | all-gather | bytes 589824 | tf_op jit(solution)/shard_map/all_gather | solution.py:20
  222.8 87.3 %while.221 = (s32[]{:T(128)}, f32[2,16,1024]{2,1,0:T(8,128)S(1)}, f32[16,2,16,1024]{3,2,1,0:T(8,128)}, f32[16,2,16,1024]{3,1,2,0:T(2,128)}, f32[16,2,16,16]{3,1,...) while((s32[]{:T(128)}, f32[2,16,1024]{2,1,0:T(8,128)S(1)}, ...), condition=%wide.region_27.28_spmd, body=%wide.region_10.27_spmd.sunk | while | flops 5767682 | bytes 4715317 | solution.py:109
  321.1 45.2 %reduce-scatter.13.cloned.1.call-done = f32[2,256,512]{2,1,0:T(8,128)} async-done(((f32[2,256,2048]{2,1,0:T(8,128)}), f32[2,256,512]{2,1,0:T(8,128)}) %reduce-scatter.13.cloned.1.call-update) | async-done | bytes 1048592 | tf_op jit(solution)/shard_map/reduce_scatter | solution.py:194
  376.0 23.2 all-gather.13.cloned.1.call-done
  399.2 8.6 fusion.406
  413.0 10.8 all-gather.15.cloned.1.call-done
  423.8 11.7 multiply_reduce_fusion.352
  444.6 24.8 all-reduce.275.cloned.1.call-done
  478.8 55.6 %while.229 = (s32[]{:T(128)}, f32[2,16,1024]{2,1,0:T(8,128)S(1)}, f32[2,16,1024]{2,1,0:T(8,128)S(1)}, f32[16,2,16,1024]{3,1,2,0:T(2,128)}, f32[16,2,16,16]{3,1,2...) while((s32[]{:T(128)}, f32[2,16,1024]{2,1,0:T(8,128)S(1)}, ...), condition=%wide.region_34.35_spmd.clone, body=%wide.region_33.34_spmd.clone.sunk | while | flops 5341699 | bytes 2108284 | solution.py:109
  534.5 33.3 %all-gather.2 = bf16[16,16,1024]{2,1,0:T(8,128)(2,1)} all-gather(bf16[2,16,1024]{2,1,0:T(8,128)(2,1)S(1)} %convert_element_type.467), channel_id=4, replica_groups=mesh['seq'=8,'tp'=4] {'seq'}, dimensions={0}, use_global_device_ids=true | all-gather | bytes 589824 | tf_op jit(solution)/shard_map/all_gather | solution.py:20
  567.8 33.2 %all-gather.3 = bf16[16,16,1024]{2,1,0:T(8,128)(2,1)} all-gather(bf16[2,16,1024]{2,1,0:T(8,128)(2,1)S(1)} %convert_element_type.468), channel_id=5, replica_groups=mesh['seq'=8,'tp'=4] {'seq'}, dimensions={0}, use_global_device_ids=true | all-gather | bytes 589824 | tf_op jit(solution)/shard_map/all_gather | solution.py:20
  603.7 87.3 %while.223 = (s32[]{:T(128)}, f32[2,16,1024]{2,1,0:T(8,128)S(1)}, f32[16,2,16,1024]{3,2,1,0:T(8,128)}, f32[16,2,16,1024]{3,1,2,0:T(2,128)}, f32[16,2,16,16]{3,1,...) while((s32[]{:T(128)}, f32[2,16,1024]{2,1,0:T(8,128)S(1)}, ...), condition=%wide.region_54.55_spmd, body=%wide.region_37.54_spmd.sunk | while | flops 5767682 | bytes 4715317 | solution.py:109
  695.7 58.9 %while.224 = (s32[]{:T(128)}, f32[2,16,1024]{2,1,0:T(8,128)S(1)}, f32[16,2,16,1024]{3,2,1,0:T(8,128)}, f32[16,2,16,1024]{3,1,2,0:T(2,128)}, f32[16,2,16,16]{3,1,...) while((s32[]{:T(128)}, f32[2,16,1024]{2,1,0:T(8,128)S(1)}, ...), condition=%wide.region_57.58_spmd, body=%wide.region_56.57_spmd.sunk | while | flops 3179010 | bytes 1975021 | solution.py:109
  760.6 198.5 %while.230 = (s32[]{:T(128)}, f32[2,16,1024]{2,1,0:T(8,128)S(1)}, f32[16,2,16,1024]{3,1,2,0:T(2,128)}, f32[16,2,16,16]{3,1,2,0:T(2,128)}, f32[16,2,16,16]{3,1,2,...) while((s32[]{:T(128)}, f32[2,16,1024]{2,1,0:T(8,128)S(1)}, ...), condition=%wide.region_139.140_spmd.clone, body=%wide.region_58.139_spmd.clone.sunk | while | flops 16858628 | bytes 11252991 | solution.py:109
  959.1 40.1 %all-gather.4 = bf16[16,16,1024]{2,1,0:T(8,128)(2,1)} all-gather(bf16[2,16,1024]{2,1,0:T(8,128)(2,1)S(1)} %convert_element_type.477), channel_id=6, replica_groups=mesh['seq'=8,'tp'=4] {'seq'}, dimensions={0}, use_global_device_ids=true | all-gather | bytes 589824 | tf_op jit(solution)/shard_map/all_gather | solution.py:40
  999.3 8.0 while.231
  1013.3 183.8 %while.225 = (s32[]{:T(128)}, f32[2,16,1024]{2,1,0:T(8,128)S(1)}, f32[16,2,16,1024]{3,1,2,0:T(2,128)}, f32[16,2,16,16]{3,1,2,0:T(2,128)}, f32[16,2,16,16]{3,1,2,...) while((s32[]{:T(128)}, f32[2,16,1024]{2,1,0:T(8,128)S(1)}, ...), condition=%wide.region_223.224_spmd, body=%wide.region_142.223_spmd.sunk | while | flops 16825860 | bytes 10859757 | solution.py:109
  1219.3 23.6 all-reduce.277.cloned.1.call-done
  1243.0 7.6 fusion.485
  1272.2 23.6 reduce-scatter.17.cloned.1.call-done
  1303.1 40.6 %reduce-scatter.15.cloned.1.call-done = f32[2,256,512]{2,1,0:T(8,128)} async-done(((f32[2,256,2048]{2,1,0:T(8,128)}), f32[2,256,512]{2,1,0:T(8,128)}) %reduce-scatter.15.cloned.1.call-update) | async-done | bytes 1048592 | tf_op jit(solution)/shard_map/reduce_scatter | solution.py:194
  1348.2 59.2 %while.226 = (s32[]{:T(128)}, f32[2,16,1024]{2,1,0:T(8,128)S(1)}, f32[16,2,16,1024]{3,2,1,0:T(8,128)}, f32[16,2,16,1024]{3,1,2,0:T(2,128)}, f32[16,2,16,16]{3,1,...) while((s32[]{:T(128)}, f32[2,16,1024]{2,1,0:T(8,128)S(1)}, ...), condition=%wide.region_230.231_spmd, body=%wide.region_229.230_spmd.sunk | while | flops 3179010 | bytes 1975021 | solution.py:109
  1409.7 8.1 multiply_reduce_fusion.353
  1426.7 198.7 %while.232 = (s32[]{:T(128)}, f32[2,16,1024]{2,1,0:T(8,128)S(1)}, f32[16,2,16,1024]{3,1,2,0:T(2,128)}, f32[16,2,16,16]{3,1,2,0:T(2,128)}, f32[16,2,16,16]{3,1,2,...) while((s32[]{:T(128)}, f32[2,16,1024]{2,1,0:T(8,128)S(1)}, ...), condition=%wide.region_312.313_spmd.clone, body=%wide.region_231.312_spmd.clone.sunk | while | flops 16858628 | bytes 11252991 | solution.py:109
  1625.4 33.9 %all-gather.5 = bf16[16,16,1024]{2,1,0:T(8,128)(2,1)} all-gather(bf16[2,16,1024]{2,1,0:T(8,128)(2,1)S(1)} %convert_element_type.482), channel_id=7, replica_groups=mesh['seq'=8,'tp'=4] {'seq'}, dimensions={0}, use_global_device_ids=true | all-gather | bytes 589824 | tf_op jit(solution)/shard_map/all_gather | solution.py:40
  1659.3 8.0 while.233
  1673.3 183.7 %while.227 = (s32[]{:T(128)}, f32[2,16,1024]{2,1,0:T(8,128)S(1)}, f32[16,2,16,1024]{3,1,2,0:T(2,128)}, f32[16,2,16,16]{3,1,2,0:T(2,128)}, f32[16,2,16,16]{3,1,2,...) while((s32[]{:T(128)}, f32[2,16,1024]{2,1,0:T(8,128)S(1)}, ...), condition=%wide.region_396.397_spmd, body=%wide.region_315.396_spmd.sunk | while | flops 16825860 | bytes 10859757 | solution.py:109
  1870.0 31.7 %all-reduce.279.cloned.1.call-done = bf16[2,256,160]{1,2,0:T(8,128)(2,1)} async-done(((bf16[2,256,160]{1,2,0:T(8,128)(2,1)}), bf16[2,256,160]{1,2,0:T(8,128)(2,1)}) %all-reduce.279.cloned.1.call-update) | async-done | bytes 163856 | tf_op jit(solution)/shard_map/psum | solution.py:300
  1931.4 10.1 bitcast_convert_fusion.4
  1957.0 9.6 fusion.349
  1967.9 9.6 fusion.348
  1980.3 59.2 %reduce-scatter.31.cloned.1.call-done = bf16[1,16,1024]{2,1,0:T(8,128)(2,1)} async-done(((bf16[1,128,1024]{2,1,0:T(8,128)(2,1)}), bf16[1,16,1024]{2,1,0:T(8,128)(2,1)}) %reduce-scatter.31.cloned.1.call-update) | async-done | bytes 32784 | tf_op jit(solution)/shard_map/reduce_scatter | solution.py:368
  2039.5 63.5 %reduce-scatter.29.cloned.1.call-done = bf16[1,16,1024]{2,1,0:T(8,128)(2,1)} async-done(((bf16[1,128,1024]{2,1,0:T(8,128)(2,1)}), bf16[1,16,1024]{2,1,0:T(8,128)(2,1)}) %reduce-scatter.29.cloned.1.call-update) | async-done | bytes 32784 | tf_op jit(solution)/shard_map/reduce_scatter | solution.py:368
  2104.5 62.0 %reduce-scatter.27.cloned.1.call-done = bf16[1,1024,16]{1,2,0:T(8,128)(2,1)} async-done(((bf16[1,1024,128]{1,2,0:T(8,128)(2,1)}), bf16[1,1024,16]{1,2,0:T(8,128)(2,1)}) %reduce-scatter.27.cloned.1.call-update) | async-done | bytes 32784 | tf_op jit(solution)/shard_map/reduce_scatter | solution.py:365
  2166.5 64.0 %reduce-scatter.25.cloned.1.call-done = bf16[1,1024,16]{1,2,0:T(8,128)(2,1)} async-done(((bf16[1,1024,128]{1,2,0:T(8,128)(2,1)}), bf16[1,1024,16]{1,2,0:T(8,128)(2,1)}) %reduce-scatter.25.cloned.1.call-update) | async-done | bytes 32784 | tf_op jit(solution)/shard_map/reduce_scatter | solution.py:365
  2232.0 32.0 %reduce-scatter.19.cloned.1.call-done = bf16[2,256,512]{2,1,0:T(8,128)(2,1)} async-done(((bf16[2,256,2048]{2,1,0:T(8,128)(2,1)}), bf16[2,256,512]{2,1,0:T(8,128)(2,1)}) %reduce-scatter.19.cloned.1.call-update) | async-done | bytes 524304 | tf_op jit(solution)/shard_map/reduce_scatter | solution.py:334
  2265.6 38.5 %all-reduce.266 = (bf16[2,512]{1,0:T(2,128)(2,1)S(1)}, bf16[2,4,1024]{2,1,0:T(4,128)(2,1)S(1)}, bf16[2,1024]{1,0:T(2,128)(2,1)S(1)}, bf16[2,1024]{1,0:T(2,128)(2,1)S(1)}, bf16[2,1024]{1,0:T(2,128)(2,1)S(1)}) all-reduce(bf16[2,512]{1,0:T(2,128)(2,1)S(1)} %pad_maximum_fusion.15, ...), channel_id=1, replica_groups=mesh['seq'=8,'tp'=4] {'seq'}, use_global_device_ids=true, to_apply=%region_404.405 | all-reduce | flops 15360 | bytes 61440 | tf_op jit(solution)/shard_map/psum | solution.py:444
  2315.6 41.8 %reduce-scatter.35.cloned.1.call-done = bf16[1,1024,256]{2,1,0:T(8,128)(2,1)} async-done(((bf16[1,1024,2048]{2,1,0:T(8,128)(2,1)}), bf16[1,1024,256]{2,1,0:T(8,128)(2,1)}) %reduce-scatter.35.cloned.1.call-update) | async-done | bytes 524304 | tf_op jit(solution)/shard_map/reduce_scatter | solution.py:371
  2357.4 91.7 %reduce-scatter.33.cloned.1.call-done = bf16[1,1024,256]{2,1,0:T(8,128)(2,1)} async-done(((bf16[1,1024,2048]{2,1,0:T(8,128)(2,1)}), bf16[1,1024,256]{2,1,0:T(8,128)(2,1)}) %reduce-scatter.33.cloned.1.call-update) | async-done | bytes 524304 | tf_op jit(solution)/shard_map/reduce_scatter | solution.py:371
  2451.7 150.1 %reduce-scatter.23.cloned.1.call-done = bf16[1,256,2,1024]{3,1,2,0:T(8,128)(2,1)} async-done(((bf16[1,2048,2,1024]{3,1,2,0:T(8,128)(2,1)}), bf16[1,256,2,1024]{3,1,2,0:T(8,128)(2,1)}) %reduce-scatter.23.cloned.1.call-update) | async-done | bytes 1048592 | tf_op jit(solution)/shard_map/reduce_scatter | solution.py:362
  2601.8 151.7 %reduce-scatter.21.cloned.1.call-done = bf16[1,256,2,1024]{3,1,2,0:T(8,128)(2,1)} async-done(((bf16[1,2048,2,1024]{3,1,2,0:T(8,128)(2,1)}), bf16[1,256,2,1024]{3,1,2,0:T(8,128)(2,1)}) %reduce-scatter.21.cloned.1.call-update) | async-done | bytes 1048592 | tf_op jit(solution)/shard_map/reduce_scatter | solution.py:362
  (5028 shorter events, 1414.8 us)
Async XLA Ops:
  7.2 35.5 %all-gather.11.cloned.1.call-start = ((), (), s32[]{:S(2)}) async-start(), calls=%async_computation.12 | async-start | bytes 2621440 | tf_op jit(solution)/shard_map/all_gather | solution.py:159
  19.7 73.3 %all-reduce.273.cloned.1.call-start = ((), (), s32[]{:S(2)}) async-start(), calls=%async_computation.13 | async-start | bytes 327680 | tf_op jit(solution)/shard_map/psum | solution.py:168
  20.1 76.1 %copy-start.60 = (f32[1,1024]{1,0:T(1,128)}, f32[1,1024]{1,0:T(1,128)S(1)}, u32[]{:S(2)}) copy-start(f32[1,1024]{1,0:T(1,128)S(1)} %get-tuple-element.4189) | copy-start | bytes 12292
  20.1 403.6 %copy-start.82 = (f32[2,256]{1,0:T(2,128)}, f32[2,256]{1,0:T(2,128)S(1)}, u32[]{:S(2)}) copy-start(f32[2,256]{1,0:T(2,128)S(1)} %get-tuple-element.4197) | copy-start | bytes 6148
  20.1 403.6 %copy-start.84 = (f32[2,256]{1,0:T(2,128)}, f32[2,256]{1,0:T(2,128)S(1)}, u32[]{:S(2)}) copy-start(f32[2,256]{1,0:T(2,128)S(1)} %get-tuple-element.4198) | copy-start | bytes 6148
  20.2 403.6 %copy-start.87 = (f32[2,256]{1,0:T(2,128)}, f32[2,256]{1,0:T(2,128)S(1)}, u32[]{:S(2)}) copy-start(f32[2,256]{1,0:T(2,128)S(1)} %get-tuple-element.4199) | copy-start | bytes 6148
  20.2 403.6 %copy-start.90 = (f32[2,256]{1,0:T(2,128)}, f32[2,256]{1,0:T(2,128)S(1)}, u32[]{:S(2)}) copy-start(f32[2,256]{1,0:T(2,128)S(1)} %get-tuple-element.4200) | copy-start | bytes 6148
  20.2 36.0 %copy-start.71 = (f32[1,1,1024]{2,1,0:T(1,128)}, f32[1,1,1024]{2,1,0:T(1,128)S(1)}, u32[]{:S(2)}) copy-start(f32[1,1,1024]{2,1,0:T(1,128)S(1)} %get-tuple-element.4182) | copy-start | bytes 12292
  20.3 403.5 %copy-start.94 = (f32[1,1,1024]{2,1,0:T(1,128)}, f32[1,1,1024]{2,1,0:T(1,128)S(1)}, u32[]{:S(2)}) copy-start(f32[1,1,1024]{2,1,0:T(1,128)S(1)} %get-tuple-element.4180) | copy-start | bytes 12292
  20.3 403.5 %copy-start.96 = (f32[1,1,1024]{2,1,0:T(1,128)}, f32[1,1,1024]{2,1,0:T(1,128)S(1)}, u32[]{:S(2)}) copy-start(f32[1,1,1024]{2,1,0:T(1,128)S(1)} %get-tuple-element.4181) | copy-start | bytes 12292
  20.3 403.5 %copy-start.98 = (f32[1,1,1024]{2,1,0:T(1,128)}, f32[1,1,1024]{2,1,0:T(1,128)S(1)}, u32[]{:S(2)}) copy-start(f32[1,1,1024]{2,1,0:T(1,128)S(1)} %get-tuple-element.4186) | copy-start | bytes 12292
  20.3 403.5 %copy-start.100 = (f32[1,1,1024]{2,1,0:T(1,128)}, f32[1,1,1024]{2,1,0:T(1,128)S(1)}, u32[]{:S(2)}) copy-start(f32[1,1,1024]{2,1,0:T(1,128)S(1)} %get-tuple-element.4187) | copy-start | bytes 12292
  51.4 4.8 collective-permute-start
  60.5 305.8 %reduce-scatter.13.cloned.1.call-start = ((), (), s32[]{:S(2)}) async-start(), calls=%async_computation.14 | async-start | bytes 5242880 | tf_op jit(solution)/shard_map/reduce_scatter | solution.py:194
  321.1 45.3 %copy-start.4 = (bf16[2,256,512]{2,1,0:T(8,128)(2,1)S(1)}, bf16[2,256,512]{2,1,0:T(8,128)(2,1)}, u32[]{:S(2)}) copy-start(bf16[2,256,512]{2,1,0:T(8,128)(2,1)} %param.41) | copy-start | bytes 1572868
  321.1 45.3 %copy-start.18 = (bf16[2,256,512]{2,1,0:T(8,128)(2,1)S(1)}, bf16[2,256,512]{2,1,0:T(8,128)(2,1)}, u32[]{:S(2)}) copy-start(bf16[2,256,512]{2,1,0:T(8,128)(2,1)} %param.51) | copy-start | bytes 1572868
  321.1 78.1 %all-gather.13.cloned.1.call-start = ((), (), s32[]{:S(2)}) async-start(), calls=%async_computation.15 | async-start | bytes 2621440 | tf_op jit(solution)/shard_map/all_gather | solution.py:159
  375.4 48.4 %all-gather.15.cloned.1.call-start = ((), (), s32[]{:S(2)}) async-start(), calls=%async_computation.18 | async-start | bytes 2621440 | tf_op jit(solution)/shard_map/all_gather | solution.py:249
  376.0 93.5 %all-reduce.275.cloned.1.call-start = ((), (), s32[]{:S(2)}) async-start(), calls=%async_computation.16 | async-start | bytes 327680 | tf_op jit(solution)/shard_map/psum | solution.py:168
  407.8 5.2 collective-permute-start.1
  437.7 805.2 %all-reduce.277.cloned.1.call-start = ((), (), s32[]{:S(2)}) async-start(), calls=%async_computation.19 | async-start | bytes 327680 | tf_op jit(solution)/shard_map/psum | solution.py:300
  1013.3 185.1 %copy-start.43 = (f32[16,2,16,16]{3,1,2,0:T(2,128)S(1)}, f32[16,2,16,16]{3,1,2,0:T(2,128)}, u32[]{:S(2)}) copy-start(f32[16,2,16,16]{3,1,2,0:T(2,128)} %get-tuple-element.1641) | copy-start | bytes 98308
  1210.6 85.2 %reduce-scatter.17.cloned.1.call-start = ((), (), s32[]{:S(2)}) async-start(), calls=%async_computation.20 | async-start | bytes 2621440 | tf_op jit(solution)/shard_map/reduce_scatter | solution.py:334
  1250.6 6.2 collective-permute-start.2
  1264.4 79.3 %reduce-scatter.15.cloned.1.call-start = ((), (), s32[]{:S(2)}) async-start(), calls=%async_computation.17 | async-start | bytes 5242880 | tf_op jit(solution)/shard_map/reduce_scatter | solution.py:194
  1272.1 71.5 %copy-start.19 = (bf16[2,256,512]{2,1,0:T(8,128)(2,1)S(1)}, bf16[2,256,512]{2,1,0:T(8,128)(2,1)}, u32[]{:S(2)}) copy-start(bf16[2,256,512]{2,1,0:T(8,128)(2,1)} %param.51) | copy-start | bytes 1572868
  1272.2 137.5 %all-gather.17.cloned.1.call-start = ((), (), s32[]{:S(2)}) async-start(), calls=%async_computation.21 | async-start | bytes 2621440 | tf_op jit(solution)/shard_map/all_gather | solution.py:249
  1346.5 555.3 %all-reduce.279.cloned.1.call-start = ((), (), s32[]{:S(2)}) async-start(), calls=%async_computation.22 | async-start | bytes 327680 | tf_op jit(solution)/shard_map/psum | solution.py:300
  1348.2 59.2 %copy-start.56 = (bf16[2,256,160]{1,2,0:T(8,128)(2,1)S(1)}, bf16[2,256,160]{1,2,0:T(8,128)(2,1)}, u32[]{:S(2)}) copy-start(bf16[2,256,160]{1,2,0:T(8,128)(2,1)} %all-reduce.277.cloned.1.call-done) | copy-start | bytes 491524
  1673.3 184.9 %copy-start.44 = (f32[16,2,16,16]{3,1,2,0:T(2,128)S(1)}, f32[16,2,16,16]{3,1,2,0:T(2,128)}, u32[]{:S(2)}) copy-start(f32[16,2,16,16]{3,1,2,0:T(2,128)} %get-tuple-element.1652) | copy-start | bytes 98308
  1868.0 36.5 %copy-start.35 = (bf16[2,256,160]{1,2,0:T(8,128)(2,1)S(1)}, bf16[2,256,160]{1,2,0:T(8,128)(2,1)}, u32[]{:S(2)}) copy-start(bf16[2,256,160]{1,2,0:T(8,128)(2,1)} %all-reduce.275.cloned.1.call-done) | copy-start | bytes 491524
  1869.9 36.9 %copy-start.34 = (bf16[2,256,160]{1,2,0:T(8,128)(2,1)S(1)}, bf16[2,256,160]{1,2,0:T(8,128)(2,1)}, u32[]{:S(2)}) copy-start(bf16[2,256,160]{1,2,0:T(8,128)(2,1)} %all-reduce.273.cloned.1.call-done) | copy-start | bytes 491524
  1870.0 108.7 %all-reduce.281.cloned.1.call-start = ((), (), s32[]{:S(2)}) async-start(), calls=%async_computation.28 | async-start | bytes 262144 | tf_op jit(solution)/shard_map/psum | solution.py:449
  1904.5 135.1 %reduce-scatter.31.cloned.1.call-start = ((), (), s32[]{:S(2)}) async-start(), calls=%async_computation.30 | async-start | bytes 294912 | tf_op jit(solution)/shard_map/reduce_scatter | solution.py:368
  1906.8 196.3 %reduce-scatter.29.cloned.1.call-start = ((), (), s32[]{:S(2)}) async-start(), calls=%async_computation.29 | async-start | bytes 294912 | tf_op jit(solution)/shard_map/reduce_scatter | solution.py:368
  1907.9 258.6 %reduce-scatter.27.cloned.1.call-start = ((), (), s32[]{:S(2)}) async-start(), calls=%async_computation.27 | async-start | bytes 294912 | tf_op jit(solution)/shard_map/reduce_scatter | solution.py:365
  1908.7 321.8 %reduce-scatter.25.cloned.1.call-start = ((), (), s32[]{:S(2)}) async-start(), calls=%async_computation.26 | async-start | bytes 294912 | tf_op jit(solution)/shard_map/reduce_scatter | solution.py:365
  1921.3 8.2 collective-permute-start.3
  1929.4 334.6 %reduce-scatter.19.cloned.1.call-start = ((), (), s32[]{:S(2)}) async-start(), calls=%async_computation.23 | async-start | bytes 2621440 | tf_op jit(solution)/shard_map/reduce_scatter | solution.py:334
  1941.5 415.9 %reduce-scatter.35.cloned.1.call-start = ((), (), s32[]{:S(2)}) async-start(), calls=%async_computation.32 | async-start | bytes 4718592 | tf_op jit(solution)/shard_map/reduce_scatter | solution.py:371
  1948.7 500.4 %reduce-scatter.33.cloned.1.call-start = ((), (), s32[]{:S(2)}) async-start(), calls=%async_computation.31 | async-start | bytes 4718592 | tf_op jit(solution)/shard_map/reduce_scatter | solution.py:371
  1955.8 646.0 %reduce-scatter.23.cloned.1.call-start = ((), (), s32[]{:S(2)}) async-start(), calls=%async_computation.25 | async-start | bytes 9437184 | tf_op jit(solution)/shard_map/reduce_scatter | solution.py:362
  1966.7 786.8 %reduce-scatter.21.cloned.1.call-start = ((), (), s32[]{:S(2)}) async-start(), calls=%async_computation.24 | async-start | bytes 9437184 | tf_op jit(solution)/shard_map/reduce_scatter | solution.py:362
  1977.6 286.4 %copy-start.5 = (bf16[2,256,512]{2,1,0:T(8,128)(2,1)S(1)}, bf16[2,256,512]{2,1,0:T(8,128)(2,1)}, u32[]{:S(2)}) copy-start(bf16[2,256,512]{2,1,0:T(8,128)(2,1)} %param.41) | copy-start | bytes 1572868
  1977.6 286.4 %copy-start.64 = (f32[1,512]{1,0:T(1,128)S(1)}, f32[1,512]{1,0:T(1,128)}, u32[]{:S(2)}) copy-start(f32[1,512]{1,0:T(1,128)} %copy-done.63) | copy-start | bytes 6148
  1977.6 286.4 %copy-start.66 = (f32[2,256]{1,0:T(2,128)S(1)}, f32[2,256]{1,0:T(2,128)}, u32[]{:S(2)}) copy-start(f32[2,256]{1,0:T(2,128)} %copy-done.65) | copy-start | bytes 6148
  1977.7 335.5 %copy-start.70 = (f32[2,256]{1,0:T(2,128)S(1)}, f32[2,256]{1,0:T(2,128)}, u32[]{:S(2)}) copy-start(f32[2,256]{1,0:T(2,128)} %copy-done.69) | copy-start | bytes 6148
  1977.7 335.5 %copy-start.17 = (bf16[2,256,512]{2,1,0:T(8,128)(2,1)S(1)}, bf16[2,256,512]{2,1,0:T(8,128)(2,1)}, u32[]{:S(2)}) copy-start(bf16[2,256,512]{2,1,0:T(8,128)(2,1)} %reduce-scatter.17.cloned.1.call-done) | copy-start | bytes 1572868
  (93 other events, 675.1 us)
Sparse Core Ops, SparseCore 0:
  19.8 22.8 all-gather.10
  60.6 32.3 all-reduce.272
  321.2 45.0 reduce-scatter.12
  375.5 23.6 all-gather.12
  401.2 22.5 all-gather.14
  437.9 31.5 all-reduce.274
  1210.7 32.1 all-reduce.276
  1264.5 31.2 reduce-scatter.16
  1299.1 44.5 reduce-scatter.14
  1346.6 22.5 all-gather.16
  1870.1 31.6 all-reduce.278
  1905.9 69.7 all-reduce.280
  1979.0 60.4 reduce-scatter.30
  2042.7 60.2 reduce-scatter.28
  2106.2 60.2 reduce-scatter.26
  2170.3 60.2 reduce-scatter.24
  2233.5 30.4 reduce-scatter.18
  2268.5 88.8 reduce-scatter.34
  2361.0 88.0 reduce-scatter.32
  2453.0 148.7 reduce-scatter.22
  2605.4 148.0 reduce-scatter.20
where the time goes:
time: 2800 us; the launch traced here: 2770 us
  waiting for transfers between devices  983 us (35%)
  other arithmetic  748 us (27%)
  local copies, waits for them, and re-layouts  597 us (21%)
  blocking collectives  268 us (10%)
  matrix products  122 us (4%)
    squeeze x608, local copies, waits for them, and re-layouts, run_blocks(): lax.scan(jax.checkpoint(block_pass), start_pair, pieces)  366 us
    reduce_scatter x2, waiting for transfers between devices, reduce_weights(): lax.psum_scatter(inweight_grad.astype(jnp.bfloat16), 'seq', scatter_dimen...  302 us
    reduce_sum x512, other arithmetic, block_pass(): rate_row[:, None, :] * (key_row * key_row)[:, :, None]  184 us
    dynamic_update_slice x256, other arithmetic, run_blocks(): lax.scan(jax.checkpoint(block_pass), start_pair, pieces)  164 us
    reduce_sum x448, other arithmetic, block_pass(): (rate_row * conv_act[:, row])[:, None, :] * key_row[:, :, None]  147 us
    reduce_scatter x2, waiting for transfers between devices, reduce_weights(): lax.psum_scatter(outweight_grad.astype(jnp.bfloat16), 'seq', scatter_dime...  134 us
    all_gather x4, blocking collectives, prefix(): lax.all_gather(a.astype(kind), axis)  129 us
    reduce_scatter x2, waiting for transfers between devices, reduce_weights(): lax.psum_scatter(select_grad.astype(jnp.bfloat16), 'seq', scatter_dimensi...  126 us

commit v1 on v0

v1 whole, which is shorter than its diff:
```python
import functools
import jax
import jax.numpy as jnp
import numpy as np
from jax import lax
from jax.experimental import pallas as pl
from jax.experimental.pallas import tpu as pltpu
from jax.sharding import PartitionSpec as P

CH = 16
LANES = 128
VMEM_BYTES = 40 * 1024 * 1024
norm_epsilon = 1e-05
BLOCK = 128
F32 = jnp.float32
LOW = jnp.bfloat16


def tables(states):
    wide = CH * states
    rows = np.arange(wide)
    lanes = np.arange(LANES)
    repeat = (rows[:, None] // states == np.arange(CH)[None, :]).astype(np.float32)
    picks = [lanes[:, None] == group * states + rows[None, :] % states for group in (0, 1, 3)]
    diagonal = (np.arange(CH)[:, None] == rows[None, :] // states).astype(np.float32)
    fold = (np.arange(3 * LANES)[:, None] // LANES == lanes[None, :] // states).astype(np.float32)
    fold_own = (rows[:, None] % states == lanes[None, :] % states).astype(np.float32)
    low = lambda value: jnp.asarray(value, LOW)
    return dict(
        pick=low(np.stack(picks).astype(np.float32)),
        diagonal=jnp.asarray(diagonal, F32),
        fold=low(fold),
        fold_own=jnp.asarray(fold_own, F32),
        gather=low(repeat.T),
    )


def dot(left, right):
    return jnp.dot(left, right, preferred_element_type=F32)


def spread_rows(table, row, states):
    wide = jnp.broadcast_to(table[:, row : row + 1], (table.shape[0], LANES))
    return [wide[at : at + states] for at in range(0, 4 * states, states)]


def groups(width):
    return [slice(at, at + LANES) for at in range(0, width, LANES)]


def row_of(ref, at, lanes):
    return ref[at : at + 1, lanes]


def summary_kernel(
    states, r_ref, act_ref, col_ref, out_ref, *scratch
):
    feed_refs = scratch[0:2]
    decay_ref, state_ref = scratch[2:]
    step = pl.program_id(1)
    r_ref, act_ref, col_ref = r_ref.at[0], act_ref.at[0], col_ref.at[0]
    count = r_ref.shape[0] // CH
    parts = groups(r_ref.shape[1])

    @pl.when(step == 0)
    def _():
        decay_ref[...] = jnp.ones_like(decay_ref)
        state_ref[...] = jnp.zeros_like(state_ref)

    def prepare(index, which):
        rows = pl.ds(pl.multiple_of(index * CH, CH), CH)
        feed_refs[which][...] = r_ref[rows, :] * act_ref[rows, :].astype(F32)

    def process(index, which, decays, values):
        base = pl.multiple_of(index * CH, CH)
        rates = r_ref.at[pl.ds(base, CH)]
        table, feeds = col_ref[pl.ds(base, CH), :].T[: 4 * states], feed_refs[which]
        for row in range(CH):
            mine = slice(row * states, (row + 1) * states)
            key, square, keep, _ = spread_rows(table, row, states)
            for at, lanes in enumerate(parts):
                decay = keep - row_of(rates, row, lanes) * square
                values[at] = decay * values[at] + row_of(feeds, row, lanes) * key
                decays[at] = decays[at] * decay

    prepare(0, 0)

    def pair(turn, carry):
        decays, values = list(carry[0]), list(carry[1])
        prepare(2 * turn + 1, 1)
        process(2 * turn, 0, decays, values)
        prepare(jnp.minimum(2 * turn + 2, count - 1), 0)
        process(2 * turn + 1, 1, decays, values)
        return (tuple(decays), tuple(values))

    start = (
        tuple(decay_ref[:, lanes] for lanes in parts),
        tuple(state_ref[:, lanes] for lanes in parts),
    )
    decays, values = lax.fori_loop(0, count // 2, pair, start)
    for at, lanes in enumerate(parts):
        decay_ref[:, lanes] = decays[at]
        state_ref[:, lanes] = values[at]

    @pl.when(step == pl.num_programs(1) - 1)
    def _():
        out_ref[0, :states] = decay_ref[...].astype(out_ref.dtype)
        out_ref[0, states:] = state_ref[...].astype(out_ref.dtype)


def forward_kernel(
    states,
    r_ref,
    act_ref,
    col_ref,
    gate_ref,
    skip_ref,
    in_ref,
    pick_ref,
    diagonal_ref,
    states_ref,
    mixed_ref,
    gated_ref,
    *scratch,
):
    feed_refs, value_refs, (state_ref,) = scratch[0:2], scratch[2:4], scratch[4:]
    step = pl.program_id(1)
    r_ref, act_ref, col_ref, gate_ref = r_ref.at[0], act_ref.at[0], col_ref.at[0], gate_ref.at[0]
    states_ref, mixed_ref, gated_ref = states_ref.at[0], mixed_ref.at[0], gated_ref.at[0]
    count = r_ref.shape[0] // CH
    parts = groups(r_ref.shape[1])

    @pl.when(step == 0)
    def _():
        state_ref[...] = in_ref[0].astype(F32)

    def prepare(index, which):
        rows = pl.ds(pl.multiple_of(index * CH, CH), CH)
        feed_refs[which][...] = r_ref[rows, :] * act_ref[rows, :].astype(F32)

    def process(index, which, values):
        base = pl.multiple_of(index * CH, CH)
        rates = r_ref.at[pl.ds(base, CH)]
        first = pl.multiple_of(index * (CH * states), CH * states)
        table, feeds = col_ref[pl.ds(base, CH), :].T[: 4 * states], feed_refs[which]
        for row in range(CH):
            mine = slice(row * states, (row + 1) * states)
            key, square, keep, _ = spread_rows(table, row, states)
            for at, lanes in enumerate(parts):
                decay = keep - row_of(rates, row, lanes) * square
                values[at] = decay * values[at] + row_of(feeds, row, lanes) * key
                low = values[at].astype(LOW)
                states_ref[pl.ds(first + row * states, states), lanes] = low
                value_refs[which][mine, lanes] = low

    def finish(index, which):
        rows = pl.ds(pl.multiple_of(index * CH, CH), CH)
        query = (dot(col_ref[rows, :].astype(LOW), pick_ref[2]) * diagonal_ref[...]).astype(LOW)
        recurrent = dot(query, value_refs[which][...])
        mixed = recurrent + skip_ref[...] * act_ref[rows, :].astype(F32)
        gate = gate_ref[rows, :].astype(F32)
        mixed_ref[rows, :] = mixed.astype(mixed_ref.dtype)
        gated_ref[rows, :] = (mixed * gate / (1.0 + jnp.exp(-gate))).astype(gated_ref.dtype)

    prepare(0, 0)

    def pair(turn, carry):
        values = list(carry)
        prepare(2 * turn + 1, 1)
        process(2 * turn, 0, values)
        finish(2 * turn, 0)
        prepare(jnp.minimum(2 * turn + 2, count - 1), 0)
        process(2 * turn + 1, 1, values)
        finish(2 * turn + 1, 1)
        return tuple(values)

    values = lax.fori_loop(0, count // 2, pair, tuple(state_ref[:, lanes] for lanes in parts))
    for at, lanes in enumerate(parts):
        state_ref[:, lanes] = values[at]


def adjoint_kernel(
    states, r_ref, gm_ref, col_ref, out_ref, *scratch
):
    (carry_ref,) = scratch
    step = pl.program_id(1)
    r_ref, gm_ref, col_ref = r_ref.at[0], gm_ref.at[0], col_ref.at[0]
    count = r_ref.shape[0] // CH
    parts = groups(r_ref.shape[1])

    @pl.when(step == 0)
    def _():
        carry_ref[...] = jnp.zeros_like(carry_ref)


    def process(index, which, values):
        base = pl.multiple_of(index * CH, CH)
        rates = r_ref.at[pl.ds(base, CH)]
        grads = gm_ref.at[pl.ds(base, CH)]
        table = col_ref[pl.ds(base, CH), :].T[: 4 * states]
        for row in reversed(range(CH)):
            mine = slice(row * states, (row + 1) * states)
            _, square, keep, query = spread_rows(table, row, states)
            for at, lanes in enumerate(parts):
                adjoint = query * row_of(grads, row, lanes) + values[at]
                values[at] = (keep - row_of(rates, row, lanes) * square) * adjoint


    def pair(turn, carry):
        values = list(carry)
        index = count - 1 - 2 * turn
        process(index, 0, values)
        process(index - 1, 1, values)
        return tuple(values)

    values = lax.fori_loop(0, count // 2, pair, tuple(carry_ref[:, lanes] for lanes in parts))
    for at, lanes in enumerate(parts):
        carry_ref[:, lanes] = values[at]

    @pl.when(step == pl.num_programs(1) - 1)
    def _():
        out_ref[0] = carry_ref[...].astype(out_ref.dtype)


def backward_kernel(
    states,
    r_ref,
    act_ref,
    gm_ref,
    col_ref,
    skip_ref,
    states_ref,
    before_ref,
    in_ref,
    carry_in_ref,
    pick_ref,
    diagonal_ref,
    fold_ref,
    fold_own_ref,
    gather_ref,
    rate_ref,
    gact_ref,
    sums_ref,
    *scratch,
):
    feed_refs, adjoint_refs, product_refs, part_refs = (
        scratch[2 * at : 2 * at + 2] for at in range(4)
    )
    first_ref, carry_ref = scratch[8:]
    step = pl.program_id(1)
    last = pl.num_programs(1) - 1
    r_ref, act_ref, gm_ref, col_ref = r_ref.at[0], act_ref.at[0], gm_ref.at[0], col_ref.at[0]
    states_ref, rate_ref, gact_ref, sums_ref = (
        states_ref.at[0],
        rate_ref.at[0],
        gact_ref.at[0],
        sums_ref.at[0],
    )
    count = r_ref.shape[0] // CH
    parts = groups(r_ref.shape[1])

    @pl.when(step == 0)
    def _():
        carry_ref[...] = carry_in_ref[0].astype(F32)

    @pl.when(step == last)
    def _():
        first_ref[...] = in_ref[0].astype(LOW)

    @pl.when(step != last)
    def _():
        first_ref[...] = before_ref[0]

    def prepare(index, which):
        rows = pl.ds(pl.multiple_of(index * CH, CH), CH)
        feed_refs[which][...] = r_ref[rows, :] * act_ref[rows, :].astype(F32)

    def process(index, which, values, held):
        base = pl.multiple_of(index * CH, CH)
        rates = r_ref.at[pl.ds(base, CH)]
        grads = gm_ref.at[pl.ds(base, CH)]
        first = pl.multiple_of(index * (CH * states), CH * states)
        table, feeds = col_ref[pl.ds(base, CH), :].T[: 4 * states], feed_refs[which]
        for row in reversed(range(CH)):
            mine = slice(row * states, (row + 1) * states)
            _, square, keep, query = spread_rows(table, row, states)
            sums = [None, None, None]
            for at, lanes in enumerate(parts):
                rate = row_of(rates, row, lanes)
                grad = row_of(grads, row, lanes)
                if row:
                    previous = states_ref[pl.ds(first + (row - 1) * states, states), lanes]
                else:
                    before = pl.multiple_of(jnp.maximum(first - states, 0), states)
                    previous = jnp.where(
                        index == 0, first_ref[:, lanes], states_ref[pl.ds(before, states), lanes]
                    )
                previous = previous.astype(F32)
                adjoint = query * grad + values[at]
                product = adjoint * previous
                values[at] = (keep - rate * square) * adjoint
                adjoint_refs[which][mine, lanes] = adjoint.astype(LOW)
                product_refs[which][mine, lanes] = product.astype(LOW)
                terms = (adjoint * row_of(feeds, row, lanes), product * rate, held[at] * grad)
                for kind, term in enumerate(terms):
                    sums[kind] = term if sums[kind] is None else sums[kind] + term
                held[at] = previous
            for kind in range(3):
                part_refs[which][mine, kind * LANES : (kind + 1) * LANES] = sums[kind].astype(LOW)

    def finish(index, which):
        rows = pl.ds(pl.multiple_of(index * CH, CH), CH)
        cols = col_ref[rows, :].astype(LOW)
        keys = (dot(cols, pick_ref[0]) * diagonal_ref[...]).astype(LOW)
        squares = (dot(cols, pick_ref[1]) * diagonal_ref[...]).astype(LOW)
        through_key = dot(keys, adjoint_refs[which][...])
        through_decay = dot(squares, product_refs[which][...])
        rate_ref[rows, :] = act_ref[rows, :].astype(F32) * through_key - through_decay
        gact_ref[rows, :] = r_ref[rows, :] * through_key + skip_ref[...] * gm_ref[rows, :]
        folded = dot(part_refs[which][...], fold_ref[...]) * fold_own_ref[...]
        high = folded.astype(LOW)
        rest = (folded - high.astype(F32)).astype(LOW)
        sums_ref[rows, :] = dot(gather_ref[...], high) + dot(gather_ref[...], rest)

    prepare(count - 1, 0)

    def pair(turn, carry):
        values, held = list(carry[0]), list(carry[1])
        index = count - 1 - 2 * turn
        prepare(index - 1, 1)
        process(index, 0, values, held)
        finish(index, 0)
        prepare(jnp.maximum(index - 2, 0), 0)
        process(index - 1, 1, values, held)
        finish(index - 1, 1)
        return (tuple(values), tuple(held))

    tail = pl.ds((count * CH - 1) * states, states)
    start = (
        tuple(carry_ref[:, lanes] for lanes in parts),
        tuple(states_ref[tail, lanes].astype(F32) for lanes in parts),
    )
    values, _ = lax.fori_loop(0, count // 2, pair, start)
    for at, lanes in enumerate(parts):
        carry_ref[:, lanes] = values[at]


def plan(rate):
    batch, rows, channels = rate.shape
    block = 128 if rows % 128 == 0 else rows
    return batch, rows, channels, block, (batch, rows // block)


def cost(rate, states, work):
    size = rate.shape[0] * rate.shape[1] * rate.shape[2] * states
    return pl.CostEstimate(flops=size * work, bytes_accessed=size * 2, transcendentals=0)


def params():
    return pltpu.CompilerParams(
        dimension_semantics=("arbitrary", "arbitrary"), vmem_limit_bytes=VMEM_BYTES
    )


def whole(value):
    return pl.BlockSpec(value.shape, lambda m, b: (0,) * value.ndim)


def run_summary(rate, act, cols, states):
    batch, rows, channels, block, grid = plan(rate)
    part = pl.BlockSpec((1, block, channels), lambda m, b: (m, b, 0))
    narrow = pl.BlockSpec((1, block, LANES), lambda m, b: (m, b, 0))
    return pl.pallas_call(
        functools.partial(summary_kernel, states),
        grid=grid,
        in_specs=[part, part, narrow],
        out_specs=pl.BlockSpec((1, 2 * states, channels), lambda m, b: (m, 0, 0)),
        out_shape=jax.ShapeDtypeStruct((batch, 2 * states, channels), LOW),
        scratch_shapes=[pltpu.VMEM((CH, channels), F32)] * 2
        + [pltpu.VMEM((states, channels), F32)] * 2,
        compiler_params=params(),
        cost_estimate=cost(rate, states, 6),
    )(rate, act, cols)


def run_forward(rate, act, cols, gate, skip, incoming, states, table):
    batch, rows, channels, block, grid = plan(rate)
    part = pl.BlockSpec((1, block, channels), lambda m, b: (m, b, 0))
    narrow = pl.BlockSpec((1, block, LANES), lambda m, b: (m, b, 0))
    edge = pl.BlockSpec((1, states, channels), lambda m, b: (m, 0, 0))
    consts = [table[name] for name in ("pick", "diagonal")]
    return pl.pallas_call(
        functools.partial(forward_kernel, states),
        grid=grid,
        in_specs=[part, part, narrow, part, whole(skip), edge] + [whole(value) for value in consts],
        out_specs=[
            pl.BlockSpec((1, block * states, channels), lambda m, b: (m, b, 0)),
            part,
            part,
        ],
        out_shape=[
            jax.ShapeDtypeStruct((batch, rows * states, channels), LOW),
            jax.ShapeDtypeStruct((batch, rows, channels), LOW),
            jax.ShapeDtypeStruct((batch, rows, channels), LOW),
        ],
        scratch_shapes=[pltpu.VMEM((CH, channels), F32)] * 2
        + [pltpu.VMEM((CH * states, channels), LOW)] * 2
        + [pltpu.VMEM((states, channels), F32)],
        compiler_params=params(),
        cost_estimate=cost(rate, states, 8),
    )(rate, act, cols, gate, skip, incoming, *consts)


def run_adjoint(rate, grad_mixed, cols, states):
    batch, rows, channels, block, grid = plan(rate)
    final = rows // block - 1
    part = pl.BlockSpec((1, block, channels), lambda m, b: (m, final - b, 0))
    narrow = pl.BlockSpec((1, block, LANES), lambda m, b: (m, final - b, 0))
    return pl.pallas_call(
        functools.partial(adjoint_kernel, states),
        grid=grid,
        in_specs=[part, part, narrow],
        out_specs=pl.BlockSpec((1, states, channels), lambda m, b: (m, 0, 0)),
        out_shape=jax.ShapeDtypeStruct((batch, states, channels), LOW),
        scratch_shapes=[pltpu.VMEM((states, channels), F32)],
        compiler_params=params(),
        cost_estimate=cost(rate, states, 5),
    )(rate, grad_mixed, cols)


def run_backward(rate, act, grad_mixed, cols, skip, kept_states, incoming, carry, states, table):
    batch, rows, channels, block, grid = plan(rate)
    final = rows // block - 1
    part = pl.BlockSpec((1, block, channels), lambda m, b: (m, final - b, 0))
    narrow = pl.BlockSpec((1, block, LANES), lambda m, b: (m, final - b, 0))
    edge = pl.BlockSpec((1, states, channels), lambda m, b: (m, 0, 0))
    names = ("pick", "diagonal", "fold", "fold_own", "gather")
    consts = [table[name] for name in names]
    return pl.pallas_call(
        functools.partial(backward_kernel, states),
        grid=grid,
        in_specs=[
            part,
            part,
            part,
            narrow,
            whole(skip),
            pl.BlockSpec((1, block * states, channels), lambda m, b: (m, final - b, 0)),
            pl.BlockSpec(
                (1, states, channels),
                lambda m, b: (m, jnp.maximum((final - b) * block - 1, 0), 0),
            ),
            edge,
            edge,
        ]
        + [whole(value) for value in consts],
        out_specs=[part, part, narrow],
        out_shape=[
            jax.ShapeDtypeStruct((batch, rows, channels), F32),
            jax.ShapeDtypeStruct((batch, rows, channels), F32),
            jax.ShapeDtypeStruct((batch, rows, LANES), F32),
        ],
        scratch_shapes=[pltpu.VMEM((CH, channels), F32)] * 2
        + [pltpu.VMEM((CH * states, channels), LOW)] * 4
        + [pltpu.VMEM((CH * states, 3 * LANES), LOW)] * 2
        + [pltpu.VMEM((states, channels), LOW), pltpu.VMEM((states, channels), F32)],
        compiler_params=params(),
        cost_estimate=cost(rate, states, 16),
    )(rate, act, grad_mixed, cols, skip, kept_states, kept_states, incoming, carry, *consts)


def columns(key, query, keep):
    kept = jnp.broadcast_to(keep[:, :, None], key.shape)
    parts = [key, kept * key * key, kept, query]
    blank = jnp.zeros(key.shape[:2] + (LANES - 4 * key.shape[2],), F32)
    return jnp.concatenate(parts + [blank], axis=2)


def shifted(value, axis, steps):
    count = lax.axis_size(axis)
    leading, last = (max(0, -steps), min(count, count - steps))
    return lax.ppermute(value, axis, [(source, source + steps) for source in range(leading, last)])


def swapped(value, axis, bit):
    count = lax.axis_size(axis)
    return lax.ppermute(value, axis, [(source, source ^ bit) for source in range(count)])


def odd(axis, bit):
    return (lax.axis_index(axis) // bit) % 2 == 1


def tp_bits():
    count = lax.axis_size("tp")
    return [1 << at for at in range(count.bit_length() - 1)]


def tp_sum(value, kind):
    for bit in tp_bits():
        value = value + swapped(value.astype(kind), "tp", bit).astype(F32)
    return value


def tp_gather(value):
    pieces = {0: value}
    for bit in reversed(tp_bits()):
        for at in list(pieces):
            pieces[at + bit] = swapped(pieces[at], "tp", bit)
    ordered = [pieces[at] for at in range(len(pieces))]
    for bit in tp_bits():
        flip = odd("tp", bit)
        ordered = [
            jnp.where(flip, ordered[at ^ bit], ordered[at]) for at in range(len(ordered))
        ]
    return jnp.concatenate(ordered, axis=-1)


def tp_scatter(value):
    count = lax.axis_size("tp")
    width = value.shape[-1] // count
    parts = [value[..., at * width : (at + 1) * width] for at in range(count)]
    for bit in tp_bits():
        flip = odd("tp", bit)
        pairs = [(parts[2 * at], parts[2 * at + 1]) for at in range(len(parts) // 2)]
        sent = [jnp.where(flip, even, other).astype(LOW) for even, other in pairs]
        mine = [jnp.where(flip, other, even) for even, other in pairs]
        parts = [
            here + swapped(there, "tp", bit).astype(F32) for here, there in zip(mine, sent)
        ]
    return parts[0]


def scan_exclusive(decay, value, direction):
    count = lax.axis_size("seq")
    states = decay.shape[1]
    outer = None
    step = 1
    while step < count:
        packed = jnp.concatenate([decay, value], axis=1).astype(LOW)
        final = 2 * step >= count
        got = shifted(packed[:, states:] if final else packed, "seq", direction * step).astype(F32)
        if final:
            got_value = got
        else:
            got_decay, got_value = got[:, :states], got[:, states:]
        if outer is None:
            outer = (got_decay, got_value) if not final else (None, got_value)
        else:
            total, held = outer
            outer = (None if final else total * got_decay, total * got_value + held)
        if not final:
            value = decay * got_value + value
            decay = decay * got_decay
        step *= 2
    return outer[1]


def halves(value):
    count = lax.axis_size("seq")
    batch, rows, width = value.shape
    parted = value.reshape(batch, rows, count // 2, 2, width // count)
    even, other = (
        parted[:, :, :, at, :].reshape(batch * rows, width // 2) for at in range(2)
    )
    flip = odd("seq", 1)
    mine = jnp.where(flip, other, even)
    theirs = swapped(jnp.where(flip, even, other), "seq", 1)
    return jnp.concatenate([mine, theirs], axis=0)


def paired(value):
    flat = value.reshape(-1, value.shape[-1])
    return jnp.concatenate([flat, swapped(flat, "seq", 1)], axis=0)


def line_reduce(value):
    long = lax.axis_size("seq") // 2
    place = lax.axis_index("seq") // 2
    pairs = lambda sources, move: [
        (2 * source + side, 2 * (source + move) + side) for source in sources for side in range(2)
    ]
    pick = lambda at: lax.dynamic_index_in_dim(value, jnp.clip(at, 0, long - 1), 0, False)
    right, left = None, None
    for step in range(1, long):
        ahead = pick(place + long - step)
        behind = pick(place - long + step)
        if right is not None:
            ahead = (ahead.astype(F32) + right.astype(F32)).astype(LOW)
            behind = (behind.astype(F32) + left.astype(F32)).astype(LOW)
        right = lax.ppermute(ahead, "seq", pairs(range(min(step, long - 1)), 1))
        left = lax.ppermute(behind, "seq", pairs(range(max(long - step, 1), long), -1))
    own = pick(place).astype(F32)
    if right is not None:
        own = own + right.astype(F32) + left.astype(F32)
    return own


def seq_scatter(value):
    count = lax.axis_size("seq")
    bit = count // 2
    while bit:
        flip = odd("seq", bit)
        low, high = value[: value.shape[0] // 2], value[value.shape[0] // 2 :]
        sent = jnp.where(flip, low, high).astype(LOW)
        value = jnp.where(flip, high, low).astype(F32) + swapped(sent, "seq", bit).astype(F32)
        bit //= 2
    return value


def seq_sum(value):
    count = lax.axis_size("seq")
    bit = 1
    while bit < count:
        value = value + swapped(value.astype(LOW), "seq", bit).astype(F32)
        bit *= 2
    return value


def gated_silu(argument):
    return argument * jax.nn.sigmoid(argument)


def silu_slope(argument):
    logistic = jax.nn.sigmoid(argument)
    return logistic * (1.0 + argument * (1.0 - logistic))


def doc_masks(doc_lengths, doc_offsets, positions):
    before = doc_offsets[:, None, :] <= positions[None, :, None]
    starts = jnp.max(jnp.where(before, doc_offsets[:, None, :], 0), axis=2)
    doc_ends = jnp.max(
        jnp.where(before, doc_offsets[:, None, :] + doc_lengths[:, None, :], 0), axis=2
    )
    return (starts, (positions[None, :] < doc_ends).astype(F32))


def matmul(left, right, dims):
    return jnp.einsum(dims, left, right, preferred_element_type=F32)


def conv_forward(conv_in, previous, conv_weight, conv_bias, tap_masks):
    edge = conv_weight.shape[0] - 1
    rows = conv_in.shape[1]
    extended = jnp.concatenate([previous, conv_in], axis=1).astype(F32)
    running = conv_bias.astype(F32)
    for back in range(edge + 1):
        window = extended[:, edge - back : edge - back + rows]
        running = running + conv_weight[back].astype(F32) * window * tap_masks[back][:, :, None]
    return (extended, running)


def forward_layer(hidden, weights, valid_mask, keep_mask, tap_masks, table):
    gain, conv_w, gate_w, conv_weight, conv_bias, select_w, step_w, step_bias, skip, out_w = weights
    width = conv_w.shape[0]
    scaled = (hidden * gain.astype(F32)).astype(LOW)
    square_sums = tp_sum(jnp.sum(hidden * hidden, axis=2), F32)
    inverse_norm = lax.rsqrt(square_sums / width + norm_epsilon)
    complete = tp_gather(scaled)
    conv_in = (matmul(complete, conv_w, "bph,hg->bpg") * inverse_norm[:, :, None]).astype(LOW)
    edge = conv_weight.shape[0] - 1
    rows = hidden.shape[1]
    previous = shifted(conv_in[:, rows - edge :], "seq", 1)
    extended, conv_out = conv_forward(conv_in, previous, conv_weight, conv_bias, tap_masks)
    conv_act = gated_silu(conv_out).astype(LOW)
    selection = tp_sum(matmul(conv_act, select_w, "mri,ic->mrc"), LOW)
    gate_in = (matmul(complete, gate_w, "bph,hg->bpg") * inverse_norm[:, :, None]).astype(LOW)
    rank = step_w.shape[0]
    states = (selection.shape[2] - rank) // 2
    low_rank = selection[:, :, :rank].astype(LOW)
    key_state = selection[:, :, rank : rank + states]
    query_state = selection[:, :, rank + states :]
    biased = matmul(low_rank, step_w, "mrk,ki->mri") + step_bias
    step_size = jax.nn.softplus(biased)
    key_norm = jnp.sum(key_state * key_state, axis=2)
    rate = step_size / (1.0 + step_size * key_norm[:, :, None])
    cols = columns(key_state, query_state, keep_mask)
    summary = run_summary(rate, conv_act, cols, states).astype(F32)
    decay_total, local_state = summary[:, :states], summary[:, states:]
    incoming = scan_exclusive(decay_total, local_state, 1)
    skip_row = skip.astype(F32)[None]
    kept_states, mixed, gated = run_forward(
        rate, conv_act, cols, gate_in, skip_row, incoming, states, table
    )
    branch = tp_scatter(matmul(gated, out_w, "mri,id->mrd"))
    new_hidden = hidden + valid_mask[:, :, None] * branch
    kept = dict(
        hidden=hidden,
        inverse_norm=inverse_norm,
        complete=complete,
        conv_in=conv_in,
        gate_in=gate_in,
        extended=extended,
        conv_out=conv_out,
        conv_act=conv_act,
        low_rank=low_rank,
        key_state=key_state,
        cols=cols,
        biased=biased,
        key_norm=key_norm,
        rate=rate,
        decay_total=decay_total,
        incoming=incoming,
        kept_states=kept_states,
        mixed=mixed,
        gated=gated,
    )
    return (new_hidden, kept)


def backward_layer(grad_new, weights, kept, valid_mask, keep_mask, tap_masks, table):
    gain, conv_w, gate_w, conv_weight, conv_bias, select_w, step_w, step_bias, skip, out_w = weights
    hidden, inverse_norm, rate, cols = (
        kept[name] for name in ("hidden", "inverse_norm", "rate", "cols")
    )
    conv_act, key_state = kept["conv_act"], kept["key_state"]
    width = conv_w.shape[0]
    states = key_state.shape[2]
    rank = step_w.shape[0]
    long = lax.axis_size("seq") // 2
    skip_row = skip.astype(F32)[None]
    branch_rows = tp_gather((grad_new * valid_mask[:, :, None]).astype(LOW))
    grad_gated = matmul(branch_rows, out_w, "mrd,id->mri")
    gate_in = kept["gate_in"].astype(F32)
    grad_mixed = grad_gated * gated_silu(gate_in)
    grad_gate = grad_gated * kept["mixed"].astype(F32) * silu_slope(gate_in)
    act_float = conv_act.astype(F32)
    skip_grad = jnp.sum(grad_mixed * act_float, axis=(0, 1))
    local_carry = run_adjoint(rate, grad_mixed, cols, states).astype(F32)
    carried = scan_exclusive(kept["decay_total"], local_carry, -1)
    grad_rate, grad_act, sums = run_backward(
        rate,
        conv_act,
        grad_mixed,
        cols,
        skip_row,
        kept["kept_states"],
        kept["incoming"],
        carried,
        states,
        table,
    )
    branch_half = halves(branch_rows)
    outweight_grad = matmul(branch_half, paired(kept["gated"]), "rd,ri->di").astype(LOW)
    outweight_grad = line_reduce(outweight_grad.reshape(long, -1, outweight_grad.shape[1]))
    normed_half = halves(kept["complete"])
    inverse = inverse_norm[:, :, None]
    grad_gate = (grad_gate * inverse).astype(LOW)
    gate_grad = matmul(normed_half, paired(grad_gate), "rd,ri->di").astype(LOW)
    gate_grad = line_reduce(gate_grad.reshape(long, -1, gate_grad.shape[1]))
    denominator = 1.0 + jax.nn.softplus(kept["biased"]) * kept["key_norm"][:, :, None]
    grad_step = grad_rate / (denominator * denominator)
    grad_norm_key = -jnp.sum(grad_rate * rate * rate, axis=2)
    grad_pre = grad_step * jax.nn.sigmoid(kept["biased"])
    stepbias_grad = jnp.sum(grad_pre, axis=(0, 1))
    grad_pre_low = grad_pre.astype(LOW)
    step_grad = matmul(kept["low_rank"], grad_pre_low, "mrk,mri->ki")
    grad_rank = matmul(grad_pre_low, step_w, "mri,ki->mrk")
    through_feed, through_decay, grad_query = (
        sums[:, :, at * states : (at + 1) * states] for at in range(3)
    )
    grad_key = (
        through_feed
        - 2.0 * keep_mask[:, :, None] * key_state * through_decay
        + 2.0 * key_state * grad_norm_key[:, :, None]
    )
    grad_selection = tp_sum(jnp.concatenate([grad_rank, grad_key, grad_query], axis=2), LOW)
    grad_selection = grad_selection.astype(LOW)
    select_full = matmul(grad_selection, conv_act, "mrc,mri->ci")
    grad_act = grad_act + matmul(grad_selection, select_w, "mrc,ic->mri")
    grad_conv = grad_act * silu_slope(kept["conv_out"])
    convbias_grad = jnp.sum(grad_conv, axis=(0, 1))
    edge = conv_weight.shape[0] - 1
    rows = grad_conv.shape[1]
    extended = kept["extended"]
    tap_grads = []
    grad_extended = jnp.zeros(extended.shape, F32)
    for back in range(edge + 1):
        masked = grad_conv * tap_masks[back][:, :, None]
        tap_grads.append(jnp.sum(masked * extended[:, edge - back : edge - back + rows], axis=(0, 1)))
        grad_extended = grad_extended + jnp.pad(
            masked * conv_weight[back].astype(F32), ((0, 0), (edge - back, back), (0, 0))
        )
    returned = shifted(grad_extended[:, :edge], "seq", -1)
    grad_conv_in = grad_extended[:, edge:] + jnp.pad(
        returned, ((0, 0), (rows - edge, 0), (0, 0))
    )
    grad_conv_in = (grad_conv_in * inverse).astype(LOW)
    grad_normed = matmul(grad_conv_in, conv_w, "bpg,hg->bph") + matmul(
        grad_gate, gate_w, "bpg,hg->bph"
    )
    grad_normed = tp_scatter(grad_normed)
    inner = tp_sum(
        jnp.sum(
            grad_conv_in.astype(F32) * kept["conv_in"].astype(F32)
            + grad_gate.astype(F32) * gate_in,
            axis=2,
        ),
        F32,
    )
    conv_grad = matmul(normed_half, paired(grad_conv_in), "rd,ri->di").astype(LOW)
    conv_grad = line_reduce(conv_grad.reshape(long, -1, conv_grad.shape[1]))
    gain_grad = jnp.sum(grad_normed * hidden, axis=(0, 1))
    grad_hidden = (
        grad_new
        + gain.astype(F32) * grad_normed
        - hidden * (inverse_norm * inner / width)[:, :, None]
    )
    count = lax.axis_size("seq")
    scattered = jnp.stack([select_full[:rank], step_grad], axis=0)
    scattered = scattered.reshape(2, count, rank // count, -1).swapaxes(0, 1)
    scattered = seq_scatter(scattered)[0]
    channels = conv_act.shape[2]
    summed = seq_sum(
        jnp.concatenate(
            [
                jnp.stack(tap_grads + [convbias_grad, stepbias_grad, skip_grad], axis=0),
                select_full[rank:],
                jnp.pad(gain_grad, (0, channels - gain_grad.shape[0]))[None],
            ],
            axis=0,
        )
    )
    grads = dict(
        inweight=jnp.stack([conv_grad, gate_grad], axis=1),
        outweight=outweight_grad.T,
        select=scattered[0].T,
        step=scattered[1],
        convweight=summed[: edge + 1],
        convbias=summed[edge + 1],
        stepbias=summed[edge + 2],
        skip=summed[edge + 3],
        keyquery=summed[edge + 4 : -1].T,
        gain=summed[-1, : gain_grad.shape[0]],
    )
    return (grad_hidden, grads)


def on_device(
    tokens,
    norm_gain,
    input_weight,
    conv_weight,
    conv_bias,
    select_weight,
    step_weight,
    step_bias,
    skip_gain,
    out_weight,
    cotangent,
    doc_lengths,
    doc_offsets,
):
    rows = tokens.shape[1]
    positions = lax.axis_index("seq") * rows + jnp.arange(rows, dtype=jnp.int32)
    starts, valid_mask = doc_masks(doc_lengths, doc_offsets, positions)
    keep_mask = (positions[None, :] != starts).astype(F32)
    tap_masks = [
        (positions[None, :] - back >= starts).astype(F32) for back in range(conv_weight.shape[1])
    ]
    layers = input_weight.shape[0]
    table = tables((select_weight.shape[2] - step_weight.shape[1]) // 2)
    weights = [
        (
            norm_gain[at],
            input_weight[at, :, 0],
            input_weight[at, :, 1],
            conv_weight[at],
            conv_bias[at],
            select_weight[at],
            step_weight[at],
            step_bias[at],
            skip_gain[at],
            out_weight[at],
        )
        for at in range(layers)
    ]
    hidden = tokens.astype(F32)
    saved = []
    for at in range(layers):
        hidden, kept = forward_layer(
            hidden, weights[at], valid_mask, keep_mask, tap_masks, table
        )
        saved.append(kept)
    layer_out = hidden.astype(LOW)
    grad = cotangent.astype(F32)
    grads = [None] * layers
    for at in reversed(range(layers)):
        grad, grads[at] = backward_layer(
            grad, weights[at], saved[at], valid_mask, keep_mask, tap_masks, table
        )
    stacked = lambda name: jnp.stack([member[name] for member in grads], axis=0)
    return (
        layer_out,
        grad.astype(LOW),
        stacked("gain"),
        stacked("inweight"),
        stacked("convweight"),
        stacked("convbias"),
        stacked("select"),
        stacked("keyquery"),
        stacked("step"),
        stacked("stepbias"),
        stacked("skip"),
        stacked("outweight"),
    )


def solution(mesh):
    placed = (
        P(None, "seq", "tp"),
        P(None, "tp"),
        P(None, None, None, "tp"),
        P(None, None, "tp"),
        P(None, "tp"),
        P(None, "tp", None),
        P(None, None, "tp"),
        P(None, "tp"),
        P(None, "tp"),
        P(None, "tp", None),
        P(None, "seq", "tp"),
        P(),
        P(),
    )
    return jax.shard_map(
        on_device,
        mesh=mesh,
        in_specs=placed,
        out_specs=(
            P(None, "seq", "tp"),
            P(None, "seq", "tp"),
            P(None, "tp"),
            P(None, "seq", None, "tp"),
            P(None, None, "tp"),
            P(None, "tp"),
            P(None, "tp", "seq"),
            P(None, "tp", None),
            P(None, "seq", "tp"),
            P(None, "tp"),
            P(None, "tp"),
            P(None, "tp", "seq"),
        ),
        check_vma=False,
    )
```

time: 2800 us -> 998 us (0.36)
  waiting for transfers between devices: 983 us -> 254 us
  other arithmetic: 748 us -> 138 us
  local copies, waits for them, and re-layouts: 597 us -> 157 us
  blocking collectives: 268 us -> 0 us
  starting transfers between devices: 11.6 us -> 186 us
  Pallas kernels: 0 us -> 147 us
    reduce_scatter x12 -> x0, waiting for transfers between devices: 825 us -> none  [the longest x2 302 us: reduce_weights(): lax.psum_scatter(inweight_grad.astype(jnp.bfloat16), 'seq', scatter_dimen...]
    reduce_sum x1254 -> x5, other arithmetic: 400 us -> 11.5 us  [the longest x2 5.48 us: backward_layer(): jnp.sum(grad_conv_in.astype(F32) * kept['conv_in'].astype(F32) + grad_gat...]
    squeeze x770 -> x4, local copies, waits for them, and re-layouts: 368 us -> 3.22 us  [line_reduce(): lax.dynamic_index_in_dim(value, jnp.clip(at, 0, long - 1), 0, False)]
    ppermute x0 -> x98, waiting for transfers between devices: none -> 230 us  [the longest x62 175 us: swapped(): lax.ppermute(value, axis, [(source, source ^ bit) for source in range(cou...]
    all_gather x6 -> x0, blocking collectives: 203 us -> none  [the longest x4 129 us: prefix(): lax.all_gather(a.astype(kind), axis)]
    dynamic_update_slice x256 -> x0, other arithmetic: 164 us -> none  [run_blocks(): lax.scan(jax.checkpoint(block_pass), start_pair, pieces)]
    ppermute x0 -> x98, starting transfers between devices: none -> 147 us  [the longest x18 73.7 us: line_reduce(): right = lax.ppermute(ahead, 'seq', pairs(range(min(step, long - 1)), 1))]
    pallas_call x0 -> x8, Pallas kernels: none -> 147 us  [the longest x2 72.2 us: run_backward(): pl.pallas_call(functools.partial(backward_kernel, states), grid=grid, in_...]
where the time goes in v1:
time: 998 us; the launch traced here: 986 us
  waiting for transfers between devices  254 us (25%)
  starting transfers between devices  186 us (19%)
  local copies, waits for them, and re-layouts  157 us (16%)
  Pallas kernels  147 us (15%)
  other arithmetic  138 us (14%)
  matrix products  99.6 us (10%)
    ppermute x62, waiting for transfers between devices, swapped(): lax.ppermute(value, axis, [(source, source ^ bit) for source in range(cou...  175 us
    dot_general x30, matrix products, matmul(): return jnp.einsum(dims, left, right, preferred_element_type=F32)  99.6 us
    ppermute x18, starting transfers between devices, line_reduce(): right = lax.ppermute(ahead, 'seq', pairs(range(min(step, long - 1)), 1))  73.7 us
    pallas_call x2, Pallas kernels, run_backward(): pl.pallas_call(functools.partial(backward_kernel, states), grid=grid, in_...  72.2 us
    ppermute x62, starting transfers between devices, swapped(): lax.ppermute(value, axis, [(source, source ^ bit) for source in range(cou...  52.3 us
    ppermute x18, waiting for transfers between devices, line_reduce(): right = lax.ppermute(ahead, 'seq', pairs(range(min(step, long - 1)), 1))  48.7 us
    unnamed x498, local copies, waits for them, and re-layouts  47.6 us
    ppermute x16, starting transfers between devices, shifted(): lax.ppermute(value, axis, [(source, source + steps) for source in range(l...  39 us
  transfers between devices with their start and end apart: 114, of which 47 were waited for; matrix products, arithmetic and copies ran while one was open for 33% of the time, Pallas kernels for 12%

profile of v1, /device:TPU:0, one launch (start us, length us, event | category | flops | bytes accessed | tf_op | source)
XLA Modules:
  0.0 986.3 jit_solution(9523136850768622088)
XLA Ops:
  6.8 33.2 %fusion.214 = (bf16[1,2048,1,1024]{3,2,1,0:T(2,128)(2,1)}, bf16[1,2048,1,1024]{3,2,1,0:T(2,128)(2,1)}, bf16[1,2048,1,1024]{3,2,1,0:T(2,128)(2,1)}, bf16[1,2048,1,1024]{3,2,1,0:T(2,128)(2,1)}) fusion(bf16[2,2048,2,1024]{3,2,1,0:T(2,128)(2,1)} %param.20), kind=kLoop, calls=%fused_computation.504 | loop fusion | bytes 33554432 | tf_op jit(solution)/shard_map/slice | solution.py:866
  46.9 6.5 multiply_convert_fusion.5
  65.1 7.2 collective-permute-done.7
  78.9 10.2 %shard_map.265 = bf16[2,32,1024]{2,1,0:T(8,128)(2,1)S(1)} custom-call(f32[2,256,1024]{2,1,0:T(8,128)S(1)} %fusion.71.r_ref, bf16[2,256,1024]{2,1,0:T(8,128)(2,1)S(1)} %get-tuple-element.82.act_ref, f32[2,256,128]{2,1,0:T(8,128)S(1)} %concatenate.104.col_ref), custom_call_target="tpu_custom_call" | custom-call | flops 50331648 | bytes 16777216 | tf_op jit(solution)/shard_map/pallas_call | solution.py:373
  96.2 6.5 collective-permute-start.9
  105.3 5.6 collective-permute-start.10
  110.9 5.9 multiply_convert_fusion.3.gate_ref
  117.0 17.8 %shard_map.266 = (bf16[2,4096,1024]{2,1,0:T(8,128)(2,1)}, bf16[2,256,1024]{2,1,0:T(8,128)(2,1)S(1)}, bf16[2,256,1024]{2,1,0:T(8,128)(2,1)}) custom-call(f32[2,256,1024]{2,1,0:T(8,128)S(1)} %fusion.71.r_ref, bf16[2,256,1024]{2,1,0:T(8,128)(2,1)S(1)} %get-tuple-element.82.act_ref, f32[2,256,128]{2,1,0:T(8,128)S(1)} %concatenate.104.col_ref, ...), custom_call_target="tpu_custom_call" | custom-call | flops 67108864 | bytes 16777216 | tf_op jit(solution)/shard_map/pallas_call | solution.py:392
  159.8 6.6 collective-permute-done.13
  174.4 10.2 %collective-permute-done.14 = bf16[2,256,512]{2,1,0:T(8,128)(2,1)} collective-permute-done((bf16[2,256,512]{2,1,0:T(8,128)(2,1)}, bf16[2,256,512]{2,1,0:T(8,128)(2,1)}, u32[]{:S(2)}, u32[]{:S(2)}) %collective-permute-start.14) | collective-permute-done | bytes 524320 | tf_op jit(solution)/shard_map/ppermute | solution.py:487
  188.5 5.7 collective-permute-done.18
  197.3 7.2 multiply_convert_fusion.gate_ref
  214.2 6.9 fusion.218
  225.1 9.7 multiply_reduce_fusion
  272.5 10.6 %shard_map.267 = bf16[2,32,1024]{2,1,0:T(8,128)(2,1)S(1)} custom-call(f32[2,256,1024]{2,1,0:T(8,128)S(1)} %copy-done, bf16[2,256,1024]{2,1,0:T(8,128)(2,1)S(1)} %copy-done.3, f32[2,256,128]{2,1,0:T(8,128)S(1)} %copy-done.8), custom_call_target="tpu_custom_call" | custom-call | flops 50331648 | bytes 16777216 | tf_op jit(solution)/shard_map/pallas_call | solution.py:373
  285.3 9.1 shard_map.269
  318.8 17.5 %shard_map.268 = (bf16[2,4096,1024]{2,1,0:T(8,128)(2,1)}, bf16[2,256,1024]{2,1,0:T(8,128)(2,1)S(1)}, bf16[2,256,1024]{2,1,0:T(8,128)(2,1)S(1)}) custom-call(f32[2,256,1024]{2,1,0:T(8,128)S(1)} %copy-done.1, bf16[2,256,1024]{2,1,0:T(8,128)(2,1)S(1)} %copy-done.4, f32[2,256,128]{2,1,0:T(8,128)S(1)} %copy-done.8, bf16[2,256,1024]{2,1,0:T(8,128)(2,1)S(1)} %copy-done.13, ...), custom_call_target="tpu_custom_call" | custom-call | flops 67108864 | bytes 16777216 | tf_op jit(solution)/shard_map/pallas_call | solution.py:392
  338.4 36.1 %shard_map.270 = (f32[2,256,1024]{2,1,0:T(8,128)S(1)}, f32[2,256,1024]{2,1,0:T(8,128)S(1)}, f32[2,256,128]{2,1,0:T(8,128)S(1)}) custom-call(f32[2,256,1024]{2,1,0:T(8,128)S(1)} %copy-done.1, bf16[2,256,1024]{2,1,0:T(8,128)(2,1)S(1)} %copy-done.4, f32[2,256,1024]{2,1,0:T(8,128)S(1)} %copy-done.6, f32[2,256,128]{2,1,0:T(8,128)S(1)} %copy-done.8, ...), custom_call_target="tpu_custom_call" | custom-call | flops 134217728 | bytes 16777216 | tf_op jit(solution)/shard_map/pallas_call | solution.py:439
  385.9 4.8 fusion.2
  414.5 5.8 fusion.95
  420.4 5.1 convolution_add_fusion.1
  443.1 14.7 %collective-permute-done.97 = bf16[1,2,16,1024]{3,2,1,0:T(8,128)(2,1)S(1)} collective-permute-done((bf16[1,2,16,1024]{3,2,1,0:T(8,128)(2,1)S(1)}, bf16[1,2,16,1024]{3,2,1,0:T(8,128)(2,1)S(1)}, u32[]{:S(2)}, u32[]{:S(2)}) %collective-permute-start.97) | collective-permute-done | bytes 65568 | tf_op jit(solution)/shard_map/ppermute | solution.py:487
  491.3 5.6 multiply_convert_fusion.6
  497.5 9.1 collective-permute-done.85
  512.8 15.2 %collective-permute-done.78 = bf16[512,1024]{1,0:T(8,128)(2,1)} collective-permute-done((bf16[512,1024]{1,0:T(8,128)(2,1)}, bf16[512,1024]{1,0:T(8,128)(2,1)}, u32[]{:S(2)}, u32[]{:S(2)}) %collective-permute-start.78) | collective-permute-done | bytes 1048608 | tf_op jit(solution)/shard_map/ppermute | solution.py:487
  549.8 5.8 collective-permute-done.79
  559.5 5.1 collective-permute-done.109
  567.1 5.3 collective-permute-start.87
  575.0 5.3 multiply_reduce_fusion.5
  586.3 5.6 fusion.215
  592.0 9.1 shard_map.271
  610.7 9.5 collective-permute-start.110
  628.6 9.8 collective-permute-start.88
  643.2 8.8 collective-permute-done.47
  652.1 36.1 %shard_map.272 = (f32[2,256,1024]{2,1,0:T(8,128)S(1)}, f32[2,256,1024]{2,1,0:T(8,128)S(1)}, f32[2,256,128]{2,1,0:T(8,128)S(1)}) custom-call(f32[2,256,1024]{2,1,0:T(8,128)S(1)} %fusion.71.r_ref, bf16[2,256,1024]{2,1,0:T(8,128)(2,1)S(1)} %get-tuple-element.82.act_ref, f32[2,256,1024]{2,1,0:T(8,128)S(1)} %copy-done.7, ...), custom_call_target="tpu_custom_call" | custom-call | flops 134217728 | bytes 16777216 | tf_op jit(solution)/shard_map/pallas_call | solution.py:439
  729.7 6.3 fusion.94
  749.2 5.5 collective-permute-done.61
  755.9 11.0 %collective-permute-done.92 = bf16[4,2,16,1024]{3,2,1,0:T(8,128)(2,1)S(1)} collective-permute-done((bf16[4,2,16,1024]{3,2,1,0:T(8,128)(2,1)S(1)}, bf16[4,2,16,1024]{3,2,1,0:T(8,128)(2,1)S(1)}, u32[]{:S(2)}, u32[]{:S(2)}) %collective-permute-start.92) | collective-permute-done | bytes 262176 | tf_op jit(solution)/shard_map/ppermute | solution.py:487
  777.1 19.3 %collective-permute-done.93 = bf16[2,2,16,1024]{3,2,1,0:T(8,128)(2,1)S(1)} collective-permute-done((bf16[2,2,16,1024]{3,2,1,0:T(8,128)(2,1)S(1)}, bf16[2,2,16,1024]{3,2,1,0:T(8,128)(2,1)S(1)}, u32[]{:S(2)}, u32[]{:S(2)}) %collective-permute-start.93) | collective-permute-done | bytes 131104 | tf_op jit(solution)/shard_map/ppermute | solution.py:487
  816.8 40.4 %collective-permute-done.94 = bf16[1,2,16,1024]{3,2,1,0:T(8,128)(2,1)S(1)} collective-permute-done((bf16[1,2,16,1024]{3,2,1,0:T(8,128)(2,1)S(1)}, bf16[1,2,16,1024]{3,2,1,0:T(8,128)(2,1)S(1)}, u32[]{:S(2)}, u32[]{:S(2)}) %collective-permute-start.94) | collective-permute-done | bytes 65568 | tf_op jit(solution)/shard_map/ppermute | solution.py:487
  866.2 5.5 collective-permute-done.100
  871.8 5.5 collective-permute-start.101
  877.4 5.0 fusion.88
  893.8 5.7 collective-permute-done.57
  914.2 7.5 collective-permute-done.64
  934.2 5.2 collective-permute-done.65
  941.8 5.0 collective-permute-start.102
  960.8 9.4 collective-permute-done.73
  (946 shorter events, 476.3 us)
Async XLA Ops:
  3.2 37.6 %collective-permute-start = (bf16[2,256,512]{2,1,0:T(8,128)(2,1)S(1)}, bf16[2,256,512]{2,1,0:T(8,128)(2,1)S(1)}, u32[]{:S(2)}, u32[]{:S(2)}) collective-permute-start(bf16[2,256,512]{2,1,0:T(8,128)(2,1)S(1)} %get-tuple-element.187), channel_id=1, source_target_pairs={{0,2},{1,3},{2,0},{3,1},{4,6},{5,7},{6,4},{7,5},{8,10},{9,11},{10,... | collective-permute-start | bytes 1572872 | tf_op jit(solution)/shard_map/ppermute | solution.py:487
  6.3 38.4 %collective-permute-start.2 = (bf16[2,256,512]{2,1,0:T(8,128)(2,1)S(1)}, bf16[2,256,512]{2,1,0:T(8,128)(2,1)S(1)}, u32[]{:S(2)}, u32[]{:S(2)}) collective-permute-start(bf16[2,256,512]{2,1,0:T(8,128)(2,1)S(1)} %get-tuple-element.187), channel_id=1, source_target_pairs={{0,1},{1,0},{2,3},{3,2},{4,5},{5,4},{6,7},{7,6},{8,9},{9,8},{10,11... | collective-permute-start | bytes 1572872 | tf_op jit(solution)/shard_map/ppermute | solution.py:487
  6.3 34.7 %collective-permute-start.3 = (f32[2,256]{1,0:T(2,128)S(1)}, f32[2,256]{1,0:T(2,128)S(1)}, u32[]{:S(2)}, u32[]{:S(2)}) collective-permute-start(f32[2,256]{1,0:T(2,128)S(1)} %get-tuple-element.188), channel_id=1, source_target_pairs={{0,1},{1,0},{2,3},{3,2},{4,5},{5,4},{6,7},{7,6},{8,9},{9,8},{10,11... | collective-permute-start | bytes 6152 | tf_op jit(solution)/shard_map/ppermute | solution.py:487
  159.7 27.3 %collective-permute-start.62 = (bf16[512,1024]{1,0:T(8,128)(2,1)}, bf16[512,1024]{1,0:T(8,128)(2,1)}, u32[]{:S(2)}, u32[]{:S(2)}) collective-permute-start(bf16[512,1024]{1,0:T(8,128)(2,1)} %bitcast.193), channel_id=1, source_target_pairs={{0,4},{4,0},{8,12},{12,8},{16,20},{20,16},{24,28},{28,24},{1,5},{5... | collective-permute-start | bytes 3145736 | tf_op jit(solution)/shard_map/ppermute | solution.py:487
  172.8 21.5 %collective-permute-start.16 = (bf16[2,256,512]{2,1,0:T(8,128)(2,1)}, bf16[2,256,512]{2,1,0:T(8,128)(2,1)S(1)}, u32[]{:S(2)}, u32[]{:S(2)}) collective-permute-start(bf16[2,256,512]{2,1,0:T(8,128)(2,1)} %get-tuple-element.80), channel_id=1, source_target_pairs={{0,1},{1,0},{2,3},{3,2},{4,5},{5,4},{6,7},{7,6},{8,9},{9,8},{10,11... | collective-permute-start | bytes 1572872 | tf_op jit(solution)/shard_map/ppermute | solution.py:487
  188.4 32.8 %collective-permute-start.30 = (bf16[2,256,512]{2,1,0:T(8,128)(2,1)}, bf16[2,256,512]{2,1,0:T(8,128)(2,1)}, u32[]{:S(2)}, u32[]{:S(2)}) collective-permute-start(bf16[2,256,512]{2,1,0:T(8,128)(2,1)} %get-tuple-element.223), channel_id=1, source_target_pairs={{0,1},{1,0},{2,3},{3,2},{4,5},{5,4},{6,7},{7,6},{8,9},{9,8},{10,11... | collective-permute-start | bytes 1572872 | tf_op jit(solution)/shard_map/ppermute | solution.py:487
  194.2 27.0 %collective-permute-start.29 = (bf16[2,256,512]{2,1,0:T(8,128)(2,1)}, bf16[2,256,512]{2,1,0:T(8,128)(2,1)}, u32[]{:S(2)}, u32[]{:S(2)}) collective-permute-start(bf16[2,256,512]{2,1,0:T(8,128)(2,1)} %collective-permute-done.28), channel_id=1, source_target_pairs={{0,1},{1,0},{2,3},{3,2},{4,5},{5,4},{6,7},{7,6},{8,9},{9,8},{10,11... | collective-permute-start | bytes 1572872 | tf_op jit(solution)/shard_map/ppermute | solution.py:487
  244.8 188.8 %collective-permute-start.77 = (bf16[512,1024]{1,0:T(8,128)(2,1)}, bf16[512,1024]{1,0:T(8,128)(2,1)}, u32[]{:S(2)}, u32[]{:S(2)}) collective-permute-start(bf16[512,1024]{1,0:T(8,128)(2,1)} %bitcast.201), channel_id=1, source_target_pairs={{0,4},{4,0},{8,12},{12,8},{16,20},{20,16},{24,28},{28,24},{1,5},{5... | collective-permute-start | bytes 3145736 | tf_op jit(solution)/shard_map/ppermute | solution.py:487
  315.0 149.0 %collective-permute-start.106 = (bf16[512,1024]{1,0:T(8,128)(2,1)}, bf16[512,1024]{1,0:T(8,128)(2,1)}, u32[]{:S(2)}, u32[]{:S(2)}) collective-permute-start(bf16[512,1024]{1,0:T(8,128)(2,1)} %bitcast.217), channel_id=1, source_target_pairs={{0,4},{4,0},{8,12},{12,8},{16,20},{20,16},{24,28},{28,24},{1,5},{5... | collective-permute-start | bytes 3145736 | tf_op jit(solution)/shard_map/ppermute | solution.py:487
  392.0 47.4 %collective-permute-start.25 = (bf16[2,256,512]{2,1,0:T(8,128)(2,1)}, bf16[2,256,512]{2,1,0:T(8,128)(2,1)}, u32[]{:S(2)}, u32[]{:S(2)}) collective-permute-start(bf16[2,256,512]{2,1,0:T(8,128)(2,1)} %get-tuple-element.101), channel_id=1, source_target_pairs={{0,1},{1,0},{2,3},{3,2},{4,5},{5,4},{6,7},{7,6},{8,9},{9,8},{10,11... | collective-permute-start | bytes 1572872 | tf_op jit(solution)/shard_map/ppermute | solution.py:487
  407.4 22.4 %collective-permute-start.95 = (bf16[4,2,16,1024]{3,2,1,0:T(8,128)(2,1)}, bf16[4,2,16,1024]{3,2,1,0:T(8,128)(2,1)S(1)}, u32[]{:S(2)}, u32[]{:S(2)}) collective-permute-start(bf16[4,2,16,1024]{3,2,1,0:T(8,128)(2,1)} %select_convert_fusion.12), channel_id=1, source_target_pairs={{0,16},{4,20},{8,24},{12,28},{16,0},{20,4},{24,8},{28,12},{1,17},{... | collective-permute-start | bytes 786440 | tf_op jit(solution)/shard_map/ppermute | solution.py:487
  430.5 34.6 %collective-permute-start.107 = (bf16[512,1024]{1,0:T(8,128)(2,1)S(1)}, bf16[512,1024]{1,0:T(8,128)(2,1)S(1)}, u32[]{:S(2)}, u32[]{:S(2)}) collective-permute-start(bf16[512,1024]{1,0:T(8,128)(2,1)S(1)} %bitcast.342), channel_id=1, source_target_pairs={{0,4},{4,0},{8,12},{12,8},{16,20},{20,16},{24,28},{28,24},{1,5},{5... | collective-permute-start | bytes 3145736 | tf_op jit(solution)/shard_map/ppermute | solution.py:487
  457.8 310.5 %collective-permute-start.99 = (bf16[512,1024]{1,0:T(8,128)(2,1)}, bf16[512,1024]{1,0:T(8,128)(2,1)}, u32[]{:S(2)}, u32[]{:S(2)}) collective-permute-start(bf16[512,1024]{1,0:T(8,128)(2,1)} %bitcast.120), channel_id=1, source_target_pairs={{0,4},{4,0},{8,12},{12,8},{16,20},{20,16},{24,28},{28,24},{1,5},{5... | collective-permute-start | bytes 3145736 | tf_op jit(solution)/shard_map/ppermute | solution.py:487
  460.2 46.4 %collective-permute-start.85 = (bf16[512,1024]{1,0:T(8,128)(2,1)}, bf16[512,1024]{1,0:T(8,128)(2,1)}, u32[]{:S(2)}, u32[]{:S(2)}) collective-permute-start(bf16[512,1024]{1,0:T(8,128)(2,1)} %bitcast.84), channel_id=1, source_target_pairs={{0,4},{4,0},{8,12},{12,8},{16,20},{20,16},{24,28},{28,24},{1,5},{5... | collective-permute-start | bytes 3145736 | tf_op jit(solution)/shard_map/ppermute | solution.py:487
  460.5 67.5 %collective-permute-start.78 = (bf16[512,1024]{1,0:T(8,128)(2,1)}, bf16[512,1024]{1,0:T(8,128)(2,1)}, u32[]{:S(2)}, u32[]{:S(2)}) collective-permute-start(bf16[512,1024]{1,0:T(8,128)(2,1)} %bitcast.75), channel_id=1, source_target_pairs={{0,4},{4,0},{8,12},{12,8},{16,20},{20,16},{24,28},{28,24},{1,5},{5... | collective-permute-start | bytes 3145736 | tf_op jit(solution)/shard_map/ppermute | solution.py:487
  464.0 22.0 %collective-permute-start.27 = (bf16[2,256,512]{2,1,0:T(8,128)(2,1)}, bf16[2,256,512]{2,1,0:T(8,128)(2,1)}, u32[]{:S(2)}, u32[]{:S(2)}) collective-permute-start(bf16[2,256,512]{2,1,0:T(8,128)(2,1)} %select_convert_fusion.6), channel_id=1, source_target_pairs={{0,2},{1,3},{2,0},{3,1},{4,6},{5,7},{6,4},{7,5},{8,10},{9,11},{10,... | collective-permute-start | bytes 1572872 | tf_op jit(solution)/shard_map/ppermute | solution.py:487
  465.1 23.2 %collective-permute-start.39 = (bf16[2,256,512]{2,1,0:T(8,128)(2,1)}, bf16[2,256,512]{2,1,0:T(8,128)(2,1)}, u32[]{:S(2)}, u32[]{:S(2)}) collective-permute-start(bf16[2,256,512]{2,1,0:T(8,128)(2,1)} %get-tuple-element.72), channel_id=1, source_target_pairs={{0,2},{1,3},{2,0},{3,1},{4,6},{5,7},{6,4},{7,5},{8,10},{9,11},{10,... | collective-permute-start | bytes 1572872 | tf_op jit(solution)/shard_map/ppermute | solution.py:487
  486.0 50.9 %collective-permute-start.111 = (bf16[256,1024]{0,1:T(8,128)(2,1)}, bf16[256,1024]{0,1:T(8,128)(2,1)S(1)}, u32[]{:S(2)}, u32[]{:S(2)}) collective-permute-start(bf16[256,1024]{0,1:T(8,128)(2,1)} %bitcast.394), channel_id=1, source_target_pairs={{24,16},{28,20},{25,17},{29,21},{26,18},{30,22},{27,19},{31,23}} | collective-permute-start | bytes 1572872 | tf_op jit(solution)/shard_map/ppermute | solution.py:592
  488.3 50.3 %collective-permute-start.108 = (bf16[256,1024]{0,1:T(8,128)(2,1)}, bf16[256,1024]{0,1:T(8,128)(2,1)S(1)}, u32[]{:S(2)}, u32[]{:S(2)}) collective-permute-start(bf16[256,1024]{0,1:T(8,128)(2,1)} %bitcast.393), channel_id=1, source_target_pairs={{0,8},{4,12},{1,9},{5,13},{2,10},{6,14},{3,11},{7,15}} | collective-permute-start | bytes 1572872 | tf_op jit(solution)/shard_map/ppermute | solution.py:591
  506.6 50.0 %collective-permute-start.42 = (bf16[2,256,512]{2,1,0:T(8,128)(2,1)S(1)}, bf16[2,256,512]{2,1,0:T(8,128)(2,1)S(1)}, u32[]{:S(2)}, u32[]{:S(2)}) collective-permute-start(bf16[2,256,512]{2,1,0:T(8,128)(2,1)S(1)} %get-tuple-element.70), channel_id=1, source_target_pairs={{0,2},{1,3},{2,0},{3,1},{4,6},{5,7},{6,4},{7,5},{8,10},{9,11},{10,... | collective-permute-start | bytes 1572872 | tf_op jit(solution)/shard_map/ppermute | solution.py:487
  556.6 45.6 %collective-permute-start.89 = (bf16[256,1024]{1,0:T(8,128)(2,1)}, bf16[256,1024]{1,0:T(8,128)(2,1)}, u32[]{:S(2)}, u32[]{:S(2)}) collective-permute-start(bf16[256,1024]{1,0:T(8,128)(2,1)} %get-tuple-element.142), channel_id=1, source_target_pairs={{24,16},{28,20},{25,17},{29,21},{26,18},{30,22},{27,19},{31,23}} | collective-permute-start | bytes 1572872 | tf_op jit(solution)/shard_map/ppermute | solution.py:592
  564.7 55.6 %collective-permute-start.82 = (bf16[256,1024]{1,0:T(8,128)(2,1)}, bf16[256,1024]{1,0:T(8,128)(2,1)}, u32[]{:S(2)}, u32[]{:S(2)}) collective-permute-start(bf16[256,1024]{1,0:T(8,128)(2,1)} %get-tuple-element.138), channel_id=1, source_target_pairs={{24,16},{28,20},{25,17},{29,21},{26,18},{30,22},{27,19},{31,23}} | collective-permute-start | bytes 1572872 | tf_op jit(solution)/shard_map/ppermute | solution.py:592
  567.1 36.7 %collective-permute-start.87 = (bf16[256,1024]{1,0:T(8,128)(2,1)}, bf16[256,1024]{1,0:T(8,128)(2,1)}, u32[]{:S(2)}, u32[]{:S(2)}) collective-permute-start(bf16[256,1024]{1,0:T(8,128)(2,1)} %fusion.117), channel_id=1, source_target_pairs={{0,8},{4,12},{8,16},{12,20},{1,9},{5,13},{9,17},{13,21},{2,10},{6,... | collective-permute-start | bytes 1572872 | tf_op jit(solution)/shard_map/ppermute | solution.py:591
  572.4 49.3 %collective-permute-start.80 = (bf16[256,1024]{1,0:T(8,128)(2,1)}, bf16[256,1024]{1,0:T(8,128)(2,1)}, u32[]{:S(2)}, u32[]{:S(2)}) collective-permute-start(bf16[256,1024]{1,0:T(8,128)(2,1)} %fusion.122), channel_id=1, source_target_pairs={{0,8},{4,12},{8,16},{12,20},{1,9},{5,13},{9,17},{13,21},{2,10},{6,... | collective-permute-start | bytes 1572872 | tf_op jit(solution)/shard_map/ppermute | solution.py:591
  602.2 36.3 %collective-permute-start.113 = (bf16[256,1024]{0,1:T(8,128)(2,1)S(1)}, bf16[256,1024]{0,1:T(8,128)(2,1)S(1)}, u32[]{:S(2)}, u32[]{:S(2)}) collective-permute-start(bf16[256,1024]{0,1:T(8,128)(2,1)S(1)} %copy-done.133), channel_id=1, source_target_pairs={{8,0},{12,4},{16,8},{20,12},{24,16},{28,20},{9,1},{13,5},{17,9},{2... | collective-permute-start | bytes 1572872 | tf_op jit(solution)/shard_map/ppermute | solution.py:592
  610.7 29.5 %collective-permute-start.110 = (bf16[256,1024]{0,1:T(8,128)(2,1)S(1)}, bf16[256,1024]{0,1:T(8,128)(2,1)S(1)}, u32[]{:S(2)}, u32[]{:S(2)}) collective-permute-start(bf16[256,1024]{0,1:T(8,128)(2,1)S(1)} %copy-done.134), channel_id=1, source_target_pairs={{0,8},{4,12},{8,16},{12,20},{16,24},{20,28},{1,9},{5,13},{9,17},{1... | collective-permute-start | bytes 1572872 | tf_op jit(solution)/shard_map/ppermute | solution.py:591
  620.3 77.8 %collective-permute-start.90 = (bf16[256,1024]{1,0:T(8,128)(2,1)}, bf16[256,1024]{1,0:T(8,128)(2,1)}, u32[]{:S(2)}, u32[]{:S(2)}) collective-permute-start(bf16[256,1024]{1,0:T(8,128)(2,1)} %get-tuple-element.140), channel_id=1, source_target_pairs={{16,8},{20,12},{24,16},{28,20},{17,9},{21,13},{25,17},{29,21},{18,... | collective-permute-start | bytes 1572872 | tf_op jit(solution)/shard_map/ppermute | solution.py:592
  628.6 178.7 %collective-permute-start.88 = (bf16[256,1024]{1,0:T(8,128)(2,1)}, bf16[256,1024]{1,0:T(8,128)(2,1)}, u32[]{:S(2)}, u32[]{:S(2)}) collective-permute-start(bf16[256,1024]{1,0:T(8,128)(2,1)} %get-tuple-element.139), channel_id=1, source_target_pairs={{0,8},{4,12},{8,16},{12,20},{16,24},{20,28},{1,9},{5,13},{9,17},{1... | collective-permute-start | bytes 1572872 | tf_op jit(solution)/shard_map/ppermute | solution.py:591
  638.5 63.0 %collective-permute-start.83 = (bf16[256,1024]{1,0:T(8,128)(2,1)}, bf16[256,1024]{1,0:T(8,128)(2,1)}, u32[]{:S(2)}, u32[]{:S(2)}) collective-permute-start(bf16[256,1024]{1,0:T(8,128)(2,1)} %get-tuple-element.136), channel_id=1, source_target_pairs={{16,8},{20,12},{24,16},{28,20},{17,9},{21,13},{25,17},{29,21},{18,... | collective-permute-start | bytes 1572872 | tf_op jit(solution)/shard_map/ppermute | solution.py:592
  695.8 114.4 %collective-permute-start.81 = (bf16[256,1024]{1,0:T(8,128)(2,1)}, bf16[256,1024]{1,0:T(8,128)(2,1)}, u32[]{:S(2)}, u32[]{:S(2)}) collective-permute-start(bf16[256,1024]{1,0:T(8,128)(2,1)} %get-tuple-element.135), channel_id=1, source_target_pairs={{0,8},{4,12},{8,16},{12,20},{16,24},{20,28},{1,9},{5,13},{9,17},{1... | collective-permute-start | bytes 1572872 | tf_op jit(solution)/shard_map/ppermute | solution.py:591
  718.6 21.4 %collective-permute-start.59 = (bf16[40,1024]{1,0:T(8,128)(2,1)S(1)}, bf16[40,1024]{1,0:T(8,128)(2,1)S(1)}, u32[]{:S(2)}, u32[]{:S(2)}) collective-permute-start(bf16[40,1024]{1,0:T(8,128)(2,1)S(1)} %convert_element_type.991), channel_id=1, source_target_pairs={{0,4},{4,0},{8,12},{12,8},{16,20},{20,16},{24,28},{28,24},{1,5},{5... | collective-permute-start | bytes 245768 | tf_op jit(solution)/shard_map/ppermute | solution.py:487
  742.4 27.5 %collective-permute-start.98 = (bf16[512,1024]{1,0:T(8,128)(2,1)S(1)}, bf16[512,1024]{1,0:T(8,128)(2,1)S(1)}, u32[]{:S(2)}, u32[]{:S(2)}) collective-permute-start(bf16[512,1024]{1,0:T(8,128)(2,1)S(1)} %bitcast.389), channel_id=1, source_target_pairs={{0,4},{4,0},{8,12},{12,8},{16,20},{20,16},{24,28},{28,24},{1,5},{5... | collective-permute-start | bytes 3145736 | tf_op jit(solution)/shard_map/ppermute | solution.py:487
  766.9 41.0 %collective-permute-start.91 = (bf16[256,1024]{1,0:T(8,128)(2,1)}, bf16[256,1024]{1,0:T(8,128)(2,1)}, u32[]{:S(2)}, u32[]{:S(2)}) collective-permute-start(bf16[256,1024]{1,0:T(8,128)(2,1)} %fusion.116), channel_id=1, source_target_pairs={{8,0},{12,4},{16,8},{20,12},{24,16},{28,20},{9,1},{13,5},{17,9},{2... | collective-permute-start | bytes 1572872 | tf_op jit(solution)/shard_map/ppermute | solution.py:592
  768.3 44.1 %collective-permute-start.84 = (bf16[256,1024]{1,0:T(8,128)(2,1)}, bf16[256,1024]{1,0:T(8,128)(2,1)}, u32[]{:S(2)}, u32[]{:S(2)}) collective-permute-start(bf16[256,1024]{1,0:T(8,128)(2,1)} %fusion.121), channel_id=1, source_target_pairs={{8,0},{12,4},{16,8},{20,12},{24,16},{28,20},{9,1},{13,5},{17,9},{2... | collective-permute-start | bytes 1572872 | tf_op jit(solution)/shard_map/ppermute | solution.py:592
  769.8 26.6 %collective-permute-start.93 = (bf16[2,2,16,1024]{3,2,1,0:T(8,128)(2,1)S(1)}, bf16[2,2,16,1024]{3,2,1,0:T(8,128)(2,1)S(1)}, u32[]{:S(2)}, u32[]{:S(2)}) collective-permute-start(bf16[2,2,16,1024]{3,2,1,0:T(8,128)(2,1)S(1)} %select_convert_fusion.15), channel_id=1, source_target_pairs={{0,8},{4,12},{8,0},{12,4},{16,24},{20,28},{24,16},{28,20},{1,9},{5... | collective-permute-start | bytes 393224 | tf_op jit(solution)/shard_map/ppermute | solution.py:487
  796.4 62.8 %collective-permute-start.51 = (bf16[2,256,512]{2,1,0:T(8,128)(2,1)}, bf16[2,256,512]{2,1,0:T(8,128)(2,1)}, u32[]{:S(2)}, u32[]{:S(2)}) collective-permute-start(bf16[2,256,512]{2,1,0:T(8,128)(2,1)} %get-tuple-element.97), channel_id=1, source_target_pairs={{0,1},{1,0},{2,3},{3,2},{4,5},{5,4},{6,7},{7,6},{8,9},{9,8},{10,11... | collective-permute-start | bytes 1572872 | tf_op jit(solution)/shard_map/ppermute | solution.py:487
  807.3 53.5 %collective-permute-start.52 = (bf16[2,256,512]{2,1,0:T(8,128)(2,1)}, bf16[2,256,512]{2,1,0:T(8,128)(2,1)S(1)}, u32[]{:S(2)}, u32[]{:S(2)}) collective-permute-start(bf16[2,256,512]{2,1,0:T(8,128)(2,1)} %get-tuple-element.96), channel_id=1, source_target_pairs={{0,1},{1,0},{2,3},{3,2},{4,5},{5,4},{6,7},{7,6},{8,9},{9,8},{10,11... | collective-permute-start | bytes 1572872 | tf_op jit(solution)/shard_map/ppermute | solution.py:487
  807.9 69.5 %collective-permute-start.70 = (bf16[512,1024]{1,0:T(8,128)(2,1)}, bf16[512,1024]{1,0:T(8,128)(2,1)S(1)}, u32[]{:S(2)}, u32[]{:S(2)}) collective-permute-start(bf16[512,1024]{1,0:T(8,128)(2,1)} %bitcast.65), channel_id=1, source_target_pairs={{0,4},{4,0},{8,12},{12,8},{16,20},{20,16},{24,28},{28,24},{1,5},{5... | collective-permute-start | bytes 3145736 | tf_op jit(solution)/shard_map/ppermute | solution.py:487
  810.3 79.1 %collective-permute-start.63 = (bf16[512,1024]{1,0:T(8,128)(2,1)}, bf16[512,1024]{1,0:T(8,128)(2,1)}, u32[]{:S(2)}, u32[]{:S(2)}) collective-permute-start(bf16[512,1024]{1,0:T(8,128)(2,1)} %bitcast.56), channel_id=1, source_target_pairs={{0,4},{4,0},{8,12},{12,8},{16,20},{20,16},{24,28},{28,24},{1,5},{5... | collective-permute-start | bytes 3145736 | tf_op jit(solution)/shard_map/ppermute | solution.py:487
  812.4 44.8 %collective-permute-start.94 = (bf16[1,2,16,1024]{3,2,1,0:T(8,128)(2,1)S(1)}, bf16[1,2,16,1024]{3,2,1,0:T(8,128)(2,1)S(1)}, u32[]{:S(2)}, u32[]{:S(2)}) collective-permute-start(bf16[1,2,16,1024]{3,2,1,0:T(8,128)(2,1)S(1)} %select_convert_fusion.17), channel_id=1, source_target_pairs={{0,4},{4,0},{8,12},{12,8},{16,20},{20,16},{24,28},{28,24},{1,5},{5... | collective-permute-start | bytes 196616 | tf_op jit(solution)/shard_map/ppermute | solution.py:487
  864.7 57.9 %collective-permute-start.104 = (bf16[256,1024]{0,1:T(8,128)(2,1)}, bf16[256,1024]{0,1:T(8,128)(2,1)}, u32[]{:S(2)}, u32[]{:S(2)}) collective-permute-start(bf16[256,1024]{0,1:T(8,128)(2,1)} %fusion.109), channel_id=1, source_target_pairs={{16,8},{20,12},{24,16},{28,20},{17,9},{21,13},{25,17},{29,21},{18,... | collective-permute-start | bytes 1572872 | tf_op jit(solution)/shard_map/ppermute | solution.py:592
  871.8 68.7 %collective-permute-start.101 = (bf16[256,1024]{0,1:T(8,128)(2,1)S(1)}, bf16[256,1024]{0,1:T(8,128)(2,1)}, u32[]{:S(2)}, u32[]{:S(2)}) collective-permute-start(bf16[256,1024]{0,1:T(8,128)(2,1)S(1)} %fusion.111), channel_id=1, source_target_pairs={{0,8},{4,12},{8,16},{12,20},{1,9},{5,13},{9,17},{13,21},{2,10},{6,... | collective-permute-start | bytes 1572872 | tf_op jit(solution)/shard_map/ppermute | solution.py:591
  886.0 26.0 %collective-permute-start.71 = (bf16[256,1024]{1,0:T(8,128)(2,1)S(1)}, bf16[256,1024]{1,0:T(8,128)(2,1)S(1)}, u32[]{:S(2)}, u32[]{:S(2)}) collective-permute-start(bf16[256,1024]{1,0:T(8,128)(2,1)S(1)} %get-tuple-element.131), channel_id=1, source_target_pairs={{0,8},{4,12},{1,9},{5,13},{2,10},{6,14},{3,11},{7,15}} | collective-permute-start | bytes 1572872 | tf_op jit(solution)/shard_map/ppermute | solution.py:591
  888.7 39.5 %collective-permute-start.74 = (bf16[256,1024]{1,0:T(8,128)(2,1)S(1)}, bf16[256,1024]{1,0:T(8,128)(2,1)S(1)}, u32[]{:S(2)}, u32[]{:S(2)}) collective-permute-start(bf16[256,1024]{1,0:T(8,128)(2,1)S(1)} %get-tuple-element.132), channel_id=1, source_target_pairs={{24,16},{28,20},{25,17},{29,21},{26,18},{30,22},{27,19},{31,23}} | collective-permute-start | bytes 1572872 | tf_op jit(solution)/shard_map/ppermute | solution.py:592
  928.2 29.0 %collective-permute-start.105 = (bf16[256,1024]{0,1:T(8,128)(2,1)S(1)}, bf16[256,1024]{0,1:T(8,128)(2,1)S(1)}, u32[]{:S(2)}, u32[]{:S(2)}) collective-permute-start(bf16[256,1024]{0,1:T(8,128)(2,1)S(1)} %fusion.110), channel_id=1, source_target_pairs={{8,0},{12,4},{16,8},{20,12},{24,16},{28,20},{9,1},{13,5},{17,9},{2... | collective-permute-start | bytes 1572872 | tf_op jit(solution)/shard_map/ppermute | solution.py:592
  947.4 22.8 %collective-permute-start.73 = (bf16[256,1024]{1,0:T(8,128)(2,1)S(1)}, bf16[256,1024]{1,0:T(8,128)(2,1)S(1)}, u32[]{:S(2)}, u32[]{:S(2)}) collective-permute-start(bf16[256,1024]{1,0:T(8,128)(2,1)S(1)} %get-tuple-element.129), channel_id=1, source_target_pairs={{0,8},{4,12},{8,16},{12,20},{16,24},{20,28},{1,9},{5,13},{9,17},{1... | collective-permute-start | bytes 1572872 | tf_op jit(solution)/shard_map/ppermute | solution.py:591
  952.0 23.9 %collective-permute-start.66 = (bf16[256,1024]{1,0:T(8,128)(2,1)S(1)}, bf16[256,1024]{1,0:T(8,128)(2,1)S(1)}, u32[]{:S(2)}, u32[]{:S(2)}) collective-permute-start(bf16[256,1024]{1,0:T(8,128)(2,1)S(1)} %get-tuple-element.125), channel_id=1, source_target_pairs={{0,8},{4,12},{8,16},{12,20},{16,24},{20,28},{1,9},{5,13},{9,17},{1... | collective-permute-start | bytes 1572872 | tf_op jit(solution)/shard_map/ppermute | solution.py:591
  957.2 21.6 %collective-permute-start.69 = (bf16[256,1024]{1,0:T(8,128)(2,1)S(1)}, bf16[256,1024]{1,0:T(8,128)(2,1)S(1)}, u32[]{:S(2)}, u32[]{:S(2)}) collective-permute-start(bf16[256,1024]{1,0:T(8,128)(2,1)S(1)} %fusion.131), channel_id=1, source_target_pairs={{8,0},{12,4},{16,8},{20,12},{24,16},{28,20},{9,1},{13,5},{17,9},{2... | collective-permute-start | bytes 1572872 | tf_op jit(solution)/shard_map/ppermute | solution.py:592
  (307 other events, 3229.2 us)

commit v2 on v1

--- a/solution.py
+++ b/solution.py
@@ -9,9 +9,9 @@
 
 CH = 16
 LANES = 128
-VMEM_BYTES = 40 * 1024 * 1024
+VMEM_BYTES = 20 * 1024 * 1024
+BLOCK = 128
 norm_epsilon = 1e-05
-BLOCK = 128
 F32 = jnp.float32
 LOW = jnp.bfloat16
 
@@ -166,15 +166,16 @@
 
     def pair(turn, carry):
         values = list(carry)
+        finish(jnp.maximum(2 * turn - 1, 0), 1)
         prepare(2 * turn + 1, 1)
         process(2 * turn, 0, values)
         finish(2 * turn, 0)
         prepare(jnp.minimum(2 * turn + 2, count - 1), 0)
         process(2 * turn + 1, 1, values)
-        finish(2 * turn + 1, 1)
         return tuple(values)
 
     values = lax.fori_loop(0, count // 2, pair, tuple(state_ref[:, lanes] for lanes in parts))
+    finish(count - 1, 1)
     for at, lanes in enumerate(parts):
         state_ref[:, lanes] = values[at]
 
@@ -327,12 +328,12 @@
     def pair(turn, carry):
         values, held = list(carry[0]), list(carry[1])
         index = count - 1 - 2 * turn
+        finish(jnp.minimum(index + 1, count - 1), 1)
         prepare(index - 1, 1)
         process(index, 0, values, held)
         finish(index, 0)
         prepare(jnp.maximum(index - 2, 0), 0)
         process(index - 1, 1, values, held)
-        finish(index - 1, 1)
         return (tuple(values), tuple(held))
 
     tail = pl.ds((count * CH - 1) * states, states)
@@ -341,13 +342,14 @@
         tuple(states_ref[tail, lanes].astype(F32) for lanes in parts),
     )
     values, _ = lax.fori_loop(0, count // 2, pair, start)
+    finish(0, 1)
     for at, lanes in enumerate(parts):
         carry_ref[:, lanes] = values[at]
 
 
 def plan(rate):
     batch, rows, channels = rate.shape
-    block = 128 if rows % 128 == 0 else rows
+    block = BLOCK if rows % BLOCK == 0 else rows
     return batch, rows, channels, block, (batch, rows // block)
 
 
@@ -356,9 +358,9 @@
     return pl.CostEstimate(flops=size * work, bytes_accessed=size * 2, transcendentals=0)
 
 
-def params():
+def params(limit=VMEM_BYTES):
     return pltpu.CompilerParams(
-        dimension_semantics=("arbitrary", "arbitrary"), vmem_limit_bytes=VMEM_BYTES
+        dimension_semantics=("arbitrary", "arbitrary"), vmem_limit_bytes=limit
     )
 
 
@@ -383,7 +385,7 @@
     )(rate, act, cols)
 
 
-def run_forward(rate, act, cols, gate, skip, incoming, states, table):
+def run_forward(rate, act, cols, gate, skip, incoming, states, table, limit):
     batch, rows, channels, block, grid = plan(rate)
     part = pl.BlockSpec((1, block, channels), lambda m, b: (m, b, 0))
     narrow = pl.BlockSpec((1, block, LANES), lambda m, b: (m, b, 0))
@@ -406,7 +408,7 @@
         scratch_shapes=[pltpu.VMEM((CH, channels), F32)] * 2
         + [pltpu.VMEM((CH * states, channels), LOW)] * 2
         + [pltpu.VMEM((states, channels), F32)],
-        compiler_params=params(),
+        compiler_params=params(limit),
         cost_estimate=cost(rate, states, 8),
     )(rate, act, cols, gate, skip, incoming, *consts)
 
@@ -428,7 +430,9 @@
     )(rate, grad_mixed, cols)
 
 
-def run_backward(rate, act, grad_mixed, cols, skip, kept_states, incoming, carry, states, table):
+def run_backward(
+    rate, act, grad_mixed, cols, skip, kept_states, incoming, carry, states, table, limit
+):
     batch, rows, channels, block, grid = plan(rate)
     final = rows // block - 1
     part = pl.BlockSpec((1, block, channels), lambda m, b: (m, final - b, 0))
@@ -464,7 +468,7 @@
         + [pltpu.VMEM((CH * states, channels), LOW)] * 4
         + [pltpu.VMEM((CH * states, 3 * LANES), LOW)] * 2
         + [pltpu.VMEM((states, channels), LOW), pltpu.VMEM((states, channels), F32)],
-        compiler_params=params(),
+        compiler_params=params(limit),
         cost_estimate=cost(rate, states, 16),
     )(rate, act, grad_mixed, cols, skip, kept_states, kept_states, incoming, carry, *consts)
 
@@ -502,21 +506,29 @@
     return value
 
 
-def tp_gather(value):
+def tp_gather(value, beside=None):
     pieces = {0: value}
     for bit in reversed(tp_bits()):
         for at in list(pieces):
             pieces[at + bit] = swapped(pieces[at], "tp", bit)
+        if beside is not None and bit == tp_bits()[-1]:
+            pieces[bit], beside = lax.optimization_barrier((pieces[bit], beside))
     ordered = [pieces[at] for at in range(len(pieces))]
     for bit in tp_bits():
         flip = odd("tp", bit)
         ordered = [
             jnp.where(flip, ordered[at ^ bit], ordered[at]) for at in range(len(ordered))
         ]
-    return jnp.concatenate(ordered, axis=-1)
-
-
-def tp_scatter(value):
+    gathered = jnp.concatenate(ordered, axis=-1)
+    return gathered if beside is None else (gathered, beside)
+
+
+def crossing(value):
+    rows = value.shape[0] // 2
+    return [swapped(value[:rows], "seq", 1), swapped(value[rows:], "seq", 1)]
+
+
+def tp_scatter(value, beside=None):
     count = lax.axis_size("tp")
     width = value.shape[-1] // count
     parts = [value[..., at * width : (at + 1) * width] for at in range(count)]
@@ -525,13 +537,14 @@
         pairs = [(parts[2 * at], parts[2 * at + 1]) for at in range(len(parts) // 2)]
         sent = [jnp.where(flip, even, other).astype(LOW) for even, other in pairs]
         mine = [jnp.where(flip, other, even) for even, other in pairs]
-        parts = [
-            here + swapped(there, "tp", bit).astype(F32) for here, there in zip(mine, sent)
-        ]
-    return parts[0]
-
-
-def scan_exclusive(decay, value, direction):
+        got = [swapped(there, "tp", bit) for there in sent]
+        if beside is not None and bit == tp_bits()[-1]:
+            got, beside = lax.optimization_barrier((got, beside))
+        parts = [here + there.astype(F32) for here, there in zip(mine, got)]
+    return parts[0] if beside is None else (parts[0], beside)
+
+
+def scan_exclusive(decay, value, direction, beside=None):
     count = lax.axis_size("seq")
     states = decay.shape[1]
     outer = None
@@ -539,7 +552,10 @@
     while step < count:
         packed = jnp.concatenate([decay, value], axis=1).astype(LOW)
         final = 2 * step >= count
-        got = shifted(packed[:, states:] if final else packed, "seq", direction * step).astype(F32)
+        got = shifted(packed[:, states:] if final else packed, "seq", direction * step)
+        if beside is not None and step == 1:
+            got, beside = lax.optimization_barrier((got, beside))
+        got = got.astype(F32)
         if final:
             got_value = got
         else:
@@ -553,28 +569,129 @@
             value = decay * got_value + value
             decay = decay * got_decay
         step *= 2
-    return outer[1]
-
-
-def halves(value):
+    return outer[1] if beside is None else (outer[1], beside)
+
+
+def after(value, *anchors):
+    return lax.optimization_barrier((value,) + anchors)[0]
+
+
+def other_half(value, anchor):
+    count = lax.axis_size("seq") // lax.axis_size("tp")
+    width = value.shape[-1] // count
+    flip = odd("seq", 1)
+    blocks = [value[..., at * width : (at + 1) * width] for at in range(count)]
+    picked = [jnp.where(flip, blocks[at], blocks[at + 1]) for at in range(0, count, 2)]
+    local = jnp.concatenate(picked, axis=-1).reshape(-1, value.shape[-1] // 2)
+    return tp_gather(swapped(after(local, anchor), "seq", 1))
+
+
+def store_products(out_ref, at, count, total):
+    parts, block, width = out_ref.shape[0], out_ref.shape[1], out_ref.shape[2] // count
+    for part in range(parts):
+        rows = total[part * block : (part + 1) * block]
+        out_ref[part, :, at * width : (at + 1) * width] = rows.astype(LOW)
+
+
+def product(left, right):
+    return lax.dot_general(left, right, (((0,), (0,)), ((), ())), preferred_element_type=F32)
+
+
+def pair_kernel(count, side_ref, *refs):
+    for at in range(count):
+        left, left_other, right, right_other = (ref[...] for ref in refs[4 * at : 4 * at + 4])
+        total = product(left, right) + product(left_other, right_other)
+        store_products(refs[-1], at, count, total)
+
+
+def plain_kernel(count, *refs):
+    for at in range(count):
+        total = product(refs[2 * at][...], refs[2 * at + 1][...])
+        store_products(refs[-1], at, count, total)
+
+
+def product_params(rows, width, total):
+    return dict(
+        compiler_params=pltpu.CompilerParams(
+            dimension_semantics=("arbitrary",), vmem_limit_bytes=56 * 1024 * 1024
+        ),
+        cost_estimate=pl.CostEstimate(
+            flops=2 * rows * width * total, bytes_accessed=4 * rows * total, transcendentals=0
+        ),
+    )
+
+
+def own_half(value, other=0):
     count = lax.axis_size("seq")
-    batch, rows, width = value.shape
-    parted = value.reshape(batch, rows, count // 2, 2, width // count)
-    even, other = (
-        parted[:, :, :, at, :].reshape(batch * rows, width // 2) for at in range(2)
-    )
+    width = value.shape[-1] // count
     flip = odd("seq", 1)
-    mine = jnp.where(flip, other, even)
-    theirs = swapped(jnp.where(flip, even, other), "seq", 1)
-    return jnp.concatenate([mine, theirs], axis=0)
-
-
-def paired(value):
-    flat = value.reshape(-1, value.shape[-1])
-    return jnp.concatenate([flat, swapped(flat, "seq", 1)], axis=0)
-
-
-def line_reduce(value):
+    blocks = [value[..., at * width : (at + 1) * width] for at in range(count)]
+    picked = [
+        jnp.where(flip, blocks[at + 1 - other], blocks[at + other]) for at in range(0, count, 2)
+    ]
+    return jnp.concatenate(picked, axis=-1)
+
+
+def pair_products(pieces):
+    rows, width = pieces[0][0].shape
+    channels = pieces[0][2].shape[1]
+    parts = lax.axis_size("seq")
+    block = width // parts
+    group = max(1, LANES // block)
+    side = (lax.axis_index("seq") % 2).astype(jnp.int32).reshape(1)
+    specs, operands = [], []
+    contiguous = pl.BlockSpec((rows, block * group), lambda at, side: (0, at))
+    strided = pl.BlockSpec((rows, block), lambda at, side: (0, 2 * at + side[0]))
+    full = pl.BlockSpec((rows, channels), lambda at, side: (0, 0))
+    for left, left_other, right, right_other in pieces:
+        specs += [strided if group == 1 else contiguous, contiguous, full, full]
+        operands += [left if group == 1 else own_half(left), left_other, right, right_other]
+    total = len(pieces) * channels
+    return pl.pallas_call(
+        functools.partial(pair_kernel, len(pieces)),
+        grid_spec=pltpu.PrefetchScalarGridSpec(
+            num_scalar_prefetch=1,
+            grid=(parts // 2 // group,),
+            in_specs=specs,
+            out_specs=pl.BlockSpec((group, block, total), lambda at, side: (at, 0, 0)),
+        ),
+        out_shape=jax.ShapeDtypeStruct((parts // 2, block, total), LOW),
+        **product_params(rows, width, total),
+    )(side, *operands)
+
+
+def plain_products(pieces):
+    rows, width = pieces[0][0].shape
+    channels = pieces[0][1].shape[1]
+    parts = lax.axis_size("seq")
+    block = width // parts
+    group = max(1, LANES // block)
+    total = len(pieces) * channels
+    specs = [
+        pl.BlockSpec((rows, block * group), lambda at: (0, at)),
+        pl.BlockSpec((rows, channels), lambda at: (0, 0)),
+    ] * len(pieces)
+    return pl.pallas_call(
+        functools.partial(plain_kernel, len(pieces)),
+        grid=(parts // group,),
+        in_specs=specs,
+        out_specs=pl.BlockSpec((group, block, total), lambda at: (at, 0, 0)),
+        out_shape=jax.ShapeDtypeStruct((parts, block, total), LOW),
+        **product_params(rows, width, total),
+    )(*[operand for piece in pieces for operand in piece])
+
+
+def line_scatter(value):
+    count = lax.axis_size("seq")
+    groups = [list(range(side, count, 2)) for side in range(2)]
+    return lax.psum_scatter(
+        value, "seq", scatter_dimension=0, axis_index_groups=groups, tiled=True
+    )[0]
+
+
+def line_task(make):
+    anchor = yield
+    value = make(anchor)
     long = lax.axis_size("seq") // 2
     place = lax.axis_index("seq") // 2
     pairs = lambda sources, move: [
@@ -586,35 +703,55 @@
         ahead = pick(place + long - step)
         behind = pick(place - long + step)
         if right is not None:
+            right, left, anchor = lax.optimization_barrier((right, left, anchor))
             ahead = (ahead.astype(F32) + right.astype(F32)).astype(LOW)
             behind = (behind.astype(F32) + left.astype(F32)).astype(LOW)
         right = lax.ppermute(ahead, "seq", pairs(range(min(step, long - 1)), 1))
         left = lax.ppermute(behind, "seq", pairs(range(max(long - step, 1), long), -1))
+        anchor = yield anchor
     own = pick(place).astype(F32)
     if right is not None:
+        right, left, anchor = lax.optimization_barrier((right, left, anchor))
         own = own + right.astype(F32) + left.astype(F32)
-    return own
-
-
-def seq_scatter(value):
-    count = lax.axis_size("seq")
-    bit = count // 2
-    while bit:
+    return own, anchor
+
+
+def advance(tasks, results, anchor):
+    if not tasks:
+        return anchor
+    name, task = tasks[0]
+    try:
+        return task.send(anchor)
+    except StopIteration as ended:
+        results[name], anchor = ended.value
+        tasks.pop(0)
+        return advance(tasks, results, anchor)
+
+
+def add_task(tasks, name, make):
+    task = line_task(make)
+    next(task)
+    tasks.append((name, task))
+
+
+def small_task(scattered, summed):
+    anchor = yield
+    scattered, summed, anchor = lax.optimization_barrier((scattered, summed, anchor))
+    bit = 1
+    rows, channels = scattered.shape[1:]
+    while bit < lax.axis_size("seq"):
         flip = odd("seq", bit)
-        low, high = value[: value.shape[0] // 2], value[value.shape[0] // 2 :]
-        sent = jnp.where(flip, low, high).astype(LOW)
-        value = jnp.where(flip, high, low).astype(F32) + swapped(sent, "seq", bit).astype(F32)
-        bit //= 2
-    return value
-
-
-def seq_sum(value):
-    count = lax.axis_size("seq")
-    bit = 1
-    while bit < count:
-        value = value + swapped(value.astype(LOW), "seq", bit).astype(F32)
+        parted = scattered.reshape(-1, 2, rows, channels)
+        low, high = parted[:, 0], parted[:, 1]
+        sent = jnp.where(flip, low, high).astype(LOW).reshape(-1, channels)
+        got = swapped(jnp.concatenate([sent, summed.astype(LOW)], axis=0), "seq", bit)
+        anchor = yield anchor
+        got, anchor = lax.optimization_barrier((got, anchor))
+        scattered = jnp.where(flip, high, low).astype(F32)
+        scattered = scattered + got[: sent.shape[0]].astype(F32).reshape(scattered.shape)
+        summed = summed + got[sent.shape[0] :].astype(F32)
         bit *= 2
-    return value
+    return (scattered[0], summed), anchor
 
 
 def gated_silu(argument):
@@ -650,21 +787,28 @@
     return (extended, running)
 
 
-def forward_layer(hidden, weights, valid_mask, keep_mask, tap_masks, table):
-    gain, conv_w, gate_w, conv_weight, conv_bias, select_w, step_w, step_bias, skip, out_w = weights
-    width = conv_w.shape[0]
+def rows_of(value):
+    return value.reshape(-1, value.shape[-1])
+
+
+def forward_layer(hidden, weights, valid_mask, keep_mask, tap_masks, table, side, inverse_gain, limit):
+    gain, input_w, conv_weight, conv_bias, select_w, step_w, step_bias, skip, out_w = weights
+    width = input_w.shape[0]
     scaled = (hidden * gain.astype(F32)).astype(LOW)
-    square_sums = tp_sum(jnp.sum(hidden * hidden, axis=2), F32)
+    complete, input_w = tp_gather(scaled, input_w)
+    unscaled = complete.astype(F32) * inverse_gain
+    square_sums = jnp.sum(unscaled * unscaled, axis=2)
     inverse_norm = lax.rsqrt(square_sums / width + norm_epsilon)
-    complete = tp_gather(scaled)
-    conv_in = (matmul(complete, conv_w, "bph,hg->bpg") * inverse_norm[:, :, None]).astype(LOW)
+    normed_other = None if side is None else other_half(scaled, complete)
+    projected = matmul(complete, input_w, "bph,htg->bptg")
+    projected = (projected * inverse_norm[:, :, None, None]).astype(LOW)
+    conv_in, gate_in = projected[:, :, 0, :], projected[:, :, 1, :]
     edge = conv_weight.shape[0] - 1
     rows = hidden.shape[1]
     previous = shifted(conv_in[:, rows - edge :], "seq", 1)
     extended, conv_out = conv_forward(conv_in, previous, conv_weight, conv_bias, tap_masks)
     conv_act = gated_silu(conv_out).astype(LOW)
     selection = tp_sum(matmul(conv_act, select_w, "mri,ic->mrc"), LOW)
-    gate_in = (matmul(complete, gate_w, "bph,hg->bpg") * inverse_norm[:, :, None]).astype(LOW)
     rank = step_w.shape[0]
     states = (selection.shape[2] - rank) // 2
     low_rank = selection[:, :, :rank].astype(LOW)
@@ -675,19 +819,25 @@
     key_norm = jnp.sum(key_state * key_state, axis=2)
     rate = step_size / (1.0 + step_size * key_norm[:, :, None])
     cols = columns(key_state, query_state, keep_mask)
+    side_rows = None if side is None else tp_gather(after(side, rate))
     summary = run_summary(rate, conv_act, cols, states).astype(F32)
     decay_total, local_state = summary[:, :states], summary[:, states:]
     incoming = scan_exclusive(decay_total, local_state, 1)
+    if side is not None:
+        incoming, normed_other = lax.optimization_barrier((incoming, normed_other))
     skip_row = skip.astype(F32)[None]
     kept_states, mixed, gated = run_forward(
-        rate, conv_act, cols, gate_in, skip_row, incoming, states, table
-    )
-    branch = tp_scatter(matmul(gated, out_w, "mri,id->mrd"))
+        rate, conv_act, cols, gate_in, skip_row, incoming, states, table, limit
+    )
+    if side is not None:
+        gated, side_rows = lax.optimization_barrier((gated, side_rows))
+    branch = tp_scatter(matmul(gated, out_w, "mri,id->mrd").astype(LOW))
     new_hidden = hidden + valid_mask[:, :, None] * branch
     kept = dict(
         hidden=hidden,
         inverse_norm=inverse_norm,
         complete=complete,
+        normed_other=normed_other,
         conv_in=conv_in,
         gate_in=gate_in,
         extended=extended,
@@ -705,29 +855,66 @@
         mixed=mixed,
         gated=gated,
     )
-    return (new_hidden, kept)
-
-
-def backward_layer(grad_new, weights, kept, valid_mask, keep_mask, tap_masks, table):
-    gain, conv_w, gate_w, conv_weight, conv_bias, select_w, step_w, step_bias, skip, out_w = weights
+    return (new_hidden, kept, input_w, side_rows)
+
+
+def backward_layer(
+    at,
+    grad_new,
+    weights,
+    kept,
+    valid_mask,
+    keep_mask,
+    tap_masks,
+    table,
+    tasks,
+    results,
+    waiting,
+    ready,
+    beside,
+):
+    gain, input_w, conv_weight, conv_bias, select_w, step_w, step_bias, skip, out_w = weights
     hidden, inverse_norm, rate, cols = (
         kept[name] for name in ("hidden", "inverse_norm", "rate", "cols")
     )
     conv_act, key_state = kept["conv_act"], kept["key_state"]
-    width = conv_w.shape[0]
+    width = input_w.shape[0]
     states = key_state.shape[2]
     rank = step_w.shape[0]
-    long = lax.axis_size("seq") // 2
     skip_row = skip.astype(F32)[None]
-    branch_rows = tp_gather((grad_new * valid_mask[:, :, None]).astype(LOW))
+    first = waiting is not None
+    if ready is None:
+        branch_local = (grad_new * valid_mask[:, :, None]).astype(LOW)
+        branch_rows, last = tp_gather(branch_local, waiting[3][1])
+        waiting = waiting[:3] + (jnp.concatenate([waiting[3][0], last], axis=0),)
+    else:
+        branch_rows = ready
     grad_gated = matmul(branch_rows, out_w, "mrd,id->mri")
     gate_in = kept["gate_in"].astype(F32)
     grad_mixed = grad_gated * gated_silu(gate_in)
-    grad_gate = grad_gated * kept["mixed"].astype(F32) * silu_slope(gate_in)
+    inverse = inverse_norm[:, :, None]
+    grad_gate = grad_gated * kept["mixed"].astype(F32) * silu_slope(gate_in) * inverse
+    grad_gate = grad_gate.astype(LOW)
     act_float = conv_act.astype(F32)
     skip_grad = jnp.sum(grad_mixed * act_float, axis=(0, 1))
-    local_carry = run_adjoint(rate, grad_mixed, cols, states).astype(F32)
-    carried = scan_exclusive(kept["decay_total"], local_carry, -1)
+    normed = rows_of(kept["complete"])
+    local_carry = run_adjoint(rate, grad_mixed, cols, states)
+    carried = scan_exclusive(kept["decay_total"], local_carry.astype(F32), -1)
+    if first:
+        carried, results[("early", at + 1)] = lax.optimization_barrier(
+            (carried, results[("early", at + 1)])
+        )
+        last = pair_products([waiting])
+        carried, last = lax.optimization_barrier((carried, last))
+        results[("conv", at + 1)] = line_scatter(last).astype(F32)
+    partial = plain_products(
+        [
+            (normed, rows_of(grad_gate)),
+            (rows_of(branch_rows), rows_of(kept["gated"])),
+        ]
+    )
+    carried, partial = lax.optimization_barrier((carried, partial))
+    results[("early", at)] = lax.psum_scatter(partial, "seq", scatter_dimension=0, tiled=True)[0]
     grad_rate, grad_act, sums = run_backward(
         rate,
         conv_act,
@@ -739,15 +926,13 @@
         carried,
         states,
         table,
-    )
-    branch_half = halves(branch_rows)
-    outweight_grad = matmul(branch_half, paired(kept["gated"]), "rd,ri->di").astype(LOW)
-    outweight_grad = line_reduce(outweight_grad.reshape(long, -1, outweight_grad.shape[1]))
-    normed_half = halves(kept["complete"])
-    inverse = inverse_norm[:, :, None]
-    grad_gate = (grad_gate * inverse).astype(LOW)
-    gate_grad = matmul(normed_half, paired(grad_gate), "rd,ri->di").astype(LOW)
-    gate_grad = line_reduce(gate_grad.reshape(long, -1, gate_grad.shape[1]))
+        2 * VMEM_BYTES,
+    )
+    if not first:
+        normed_other = swapped(own_half(normed, 1), "seq", 1)
+        grad_rate, beside, normed_other = lax.optimization_barrier(
+            (grad_rate, beside, normed_other)
+        )
     denominator = 1.0 + jax.nn.softplus(kept["biased"]) * kept["key_norm"][:, :, None]
     grad_step = grad_rate / (denominator * denominator)
     grad_norm_key = -jnp.sum(grad_rate * rate * rate, axis=2)
@@ -786,10 +971,19 @@
         returned, ((0, 0), (rows - edge, 0), (0, 0))
     )
     grad_conv_in = (grad_conv_in * inverse).astype(LOW)
-    grad_normed = matmul(grad_conv_in, conv_w, "bpg,hg->bph") + matmul(
-        grad_gate, gate_w, "bpg,hg->bph"
-    )
-    grad_normed = tp_scatter(grad_normed)
+    conv_other = crossing(rows_of(grad_conv_in))
+    if first:
+        normed_other = kept["normed_other"]
+    grad_projected = jnp.stack([grad_conv_in, grad_gate], axis=2)
+    grad_normed = matmul(grad_projected, input_w, "bptg,htg->bph").astype(LOW)
+    if first:
+        grad_normed = tp_scatter(grad_normed)
+        conv_other = jnp.concatenate(conv_other, axis=0)
+    else:
+        grad_normed, conv_first = tp_scatter(grad_normed, conv_other[0])
+        conv_other = (conv_first, conv_other[1])
+    grad_normed = grad_normed.astype(F32)
+    conv_piece = (normed, normed_other, rows_of(grad_conv_in), conv_other)
     inner = tp_sum(
         jnp.sum(
             grad_conv_in.astype(F32) * kept["conv_in"].astype(F32)
@@ -798,8 +992,6 @@
         ),
         F32,
     )
-    conv_grad = matmul(normed_half, paired(grad_conv_in), "rd,ri->di").astype(LOW)
-    conv_grad = line_reduce(conv_grad.reshape(long, -1, conv_grad.shape[1]))
     gain_grad = jnp.sum(grad_normed * hidden, axis=(0, 1))
     grad_hidden = (
         grad_new
@@ -809,31 +1001,16 @@
     count = lax.axis_size("seq")
     scattered = jnp.stack([select_full[:rank], step_grad], axis=0)
     scattered = scattered.reshape(2, count, rank // count, -1).swapaxes(0, 1)
-    scattered = seq_scatter(scattered)[0]
     channels = conv_act.shape[2]
-    summed = seq_sum(
-        jnp.concatenate(
-            [
-                jnp.stack(tap_grads + [convbias_grad, stepbias_grad, skip_grad], axis=0),
-                select_full[rank:],
-                jnp.pad(gain_grad, (0, channels - gain_grad.shape[0]))[None],
-            ],
-            axis=0,
-        )
-    )
-    grads = dict(
-        inweight=jnp.stack([conv_grad, gate_grad], axis=1),
-        outweight=outweight_grad.T,
-        select=scattered[0].T,
-        step=scattered[1],
-        convweight=summed[: edge + 1],
-        convbias=summed[edge + 1],
-        stepbias=summed[edge + 2],
-        skip=summed[edge + 3],
-        keyquery=summed[edge + 4 : -1].T,
-        gain=summed[-1, : gain_grad.shape[0]],
-    )
-    return (grad_hidden, grads)
+    summed = jnp.concatenate(
+        [
+            jnp.stack(tap_grads + [convbias_grad, stepbias_grad, skip_grad], axis=0),
+            select_full[rank:],
+            jnp.pad(gain_grad, (0, channels - gain_grad.shape[0]))[None],
+        ],
+        axis=0,
+    )
+    return (grad_hidden, conv_piece, scattered, summed)
 
 
 def on_device(
@@ -860,49 +1037,90 @@
     ]
     layers = input_weight.shape[0]
     table = tables((select_weight.shape[2] - step_weight.shape[1]) // 2)
-    weights = [
-        (
-            norm_gain[at],
-            input_weight[at, :, 0],
-            input_weight[at, :, 1],
-            conv_weight[at],
-            conv_bias[at],
-            select_weight[at],
-            step_weight[at],
-            step_bias[at],
-            skip_gain[at],
-            out_weight[at],
+    small = (conv_weight, conv_bias, select_weight, step_weight, step_bias, skip_gain, out_weight)
+    shared = [tuple(member[at] for member in small) for at in range(layers)]
+    hidden = tokens.astype(F32)
+    grad = cotangent.astype(F32)
+    side = (grad * valid_mask[:, :, None]).astype(LOW)
+    inverse_gains = 1.0 / tp_gather(norm_gain.astype(F32))
+    saved, inputs, ready = [], [None] * layers, None
+    for at in range(layers):
+        own = after(input_weight[at], hidden)
+        hidden, kept, inputs[at], extra = forward_layer(
+            hidden,
+            (norm_gain[at], own) + shared[at],
+            valid_mask,
+            keep_mask,
+            tap_masks,
+            table,
+            side if at == 0 else None,
+            inverse_gains[at],
+            2 * VMEM_BYTES,
         )
+        ready = extra if at == 0 else ready
+        saved.append(kept)
+    layer_out = hidden.astype(LOW)
+    tasks, results, waiting = [], {}, None
+    scattered, summed = [None] * layers, [None] * layers
+    for at in reversed(range(layers)):
+        grad, waiting, scattered[at], summed[at] = backward_layer(
+            at,
+            grad,
+            (norm_gain[at], inputs[at]) + shared[at],
+            saved[at],
+            valid_mask,
+            keep_mask,
+            tap_masks,
+            table,
+            tasks,
+            results,
+            waiting,
+            ready if waiting is None else None,
+            hidden if waiting is None else None,
+        )
+    piece = waiting
+    add_task(tasks, ("conv", 0), lambda anchor: pair_products([piece]))
+    rank = step_weight.shape[1]
+    count = lax.axis_size("seq")
+    packed = jnp.stack(scattered, axis=1).reshape(count, -1, out_weight.shape[1])
+    small = small_task(packed, jnp.concatenate(summed, axis=0))
+    next(small)
+    extra = [("small", small)]
+    while tasks or extra:
+        grad = advance(tasks, results, grad)
+        grad = advance(extra, results, grad)
+    scattered, summed = results["small"]
+    scattered = scattered.reshape(layers, 2, rank // count, -1)
+    summed = summed.reshape(layers, -1, summed.shape[1])
+    channels = out_weight.shape[1]
+    parts = [
+        [results[("early", at)][:, piece * channels : (piece + 1) * channels] for piece in range(2)]
         for at in range(layers)
     ]
-    hidden = tokens.astype(F32)
-    saved = []
-    for at in range(layers):
-        hidden, kept = forward_layer(
-            hidden, weights[at], valid_mask, keep_mask, tap_masks, table
-        )
-        saved.append(kept)
-    layer_out = hidden.astype(LOW)
-    grad = cotangent.astype(F32)
-    grads = [None] * layers
-    for at in reversed(range(layers)):
-        grad, grads[at] = backward_layer(
-            grad, weights[at], saved[at], valid_mask, keep_mask, tap_masks, table
-        )
-    stacked = lambda name: jnp.stack([member[name] for member in grads], axis=0)
+    conv_parts = [results[("conv", at)] for at in range(layers)]
+    gate_parts = [parts[at][0].astype(F32) for at in range(layers)]
+    out_parts = [parts[at][1].astype(F32) for at in range(layers)]
+    edge = conv_weight.shape[1]
+    blank = [jnp.zeros_like(conv_parts[0])] + conv_parts[1:]
+    inweight_grad = jnp.stack(
+        [jnp.stack([conv, gate], axis=1) for conv, gate in zip(blank, gate_parts)], axis=0
+    )
+    inweight_grad = lax.dynamic_update_slice(
+        after(inweight_grad, grad), conv_parts[0][None, :, None, :], (0, 0, 0, 0)
+    )
     return (
         layer_out,
         grad.astype(LOW),
-        stacked("gain"),
-        stacked("inweight"),
-        stacked("convweight"),
-        stacked("convbias"),
-        stacked("select"),
-        stacked("keyquery"),
-        stacked("step"),
-        stacked("stepbias"),
-        stacked("skip"),
-        stacked("outweight"),
+        summed[:, -1, : norm_gain.shape[1]],
+        inweight_grad,
+        summed[:, :edge],
+        summed[:, edge],
+        jnp.swapaxes(scattered[:, 0], 1, 2),
+        jnp.swapaxes(summed[:, edge + 3 : -1], 1, 2),
+        scattered[:, 1],
+        summed[:, edge + 1],
+        summed[:, edge + 2],
+        jnp.swapaxes(jnp.stack(out_parts, axis=0), 1, 2),
     )
 
 

time: 998 us -> 747 us (0.75)
  local copies, waits for them, and re-layouts: 157 us -> 78.1 us
  starting transfers between devices: 186 us -> 121 us
  other arithmetic: 138 us -> 79.5 us
  waiting for transfers between devices: 254 us -> 196 us
  matrix products: 99.6 us -> 67.8 us
  Pallas kernels: 147 us -> 175 us
  between operations: 5.49 us -> 17.3 us
    ppermute x36 -> x6, starting transfers between devices: 95 us -> 29 us  [the longest x3 24.5 us: line_task(): right = lax.ppermute(ahead, 'seq', pairs(range(min(step, long - 1)), 1))]
    slice x12 -> x9, local copies, waits for them, and re-layouts: 54.5 us -> 3 us  [the longest x2 1 us: small_task(): got[:sent.shape[0]].astype(F32).reshape(scattered.shape)]
    ppermute x62 -> x51, waiting for transfers between devices: 175 us -> 134 us  [swapped(): lax.ppermute(value, axis, [(source, source ^ bit) for source in range(cou...]
    ppermute x36 -> x6, waiting for transfers between devices: 54.6 us -> 17.9 us  [the longest x3 17.9 us: line_task(): right = lax.ppermute(ahead, 'seq', pairs(range(min(step, long - 1)), 1))]
    pallas_call x0 -> x4, Pallas kernels: none -> 33.7 us  [the longest x2 21.5 us: plain_products(): pl.pallas_call(functools.partial(plain_kernel, len(pieces)), grid=(parts...]
    dot_general x30 -> x20, matrix products: 99.6 us -> 67.8 us  [matmul(): return jnp.einsum(dims, left, right, preferred_element_type=F32)]
    ppermute x16, waiting for transfers between devices: 24.5 us -> 43.9 us  [shifted(): lax.ppermute(value, axis, [(source, source + steps) for source in range(l...]
    reshape x4 -> x0, local copies, waits for them, and re-layouts: 18.2 us -> none  [halves(): parted = value.reshape(batch, rows, count // 2, 2, width // count)]
  transfers between devices with their start and end apart: 114 -> 76, of which waited for: 47 -> 44; matrix products, arithmetic and copies ran while one was open for 33% -> 19% of each run, Pallas kernels for 12% -> 21%
where the time goes in v2:
time: 747 us; the launch traced here: 734 us
  waiting for transfers between devices  196 us (26%)
  Pallas kernels  175 us (23%)
  starting transfers between devices  121 us (16%)
  other arithmetic  79.5 us (11%)
  local copies, waits for them, and re-layouts  78.1 us (10%)
  matrix products  67.8 us (9%)
  between operations  17.3 us (2%)
    ppermute x51, waiting for transfers between devices, swapped(): lax.ppermute(value, axis, [(source, source ^ bit) for source in range(cou...  134 us
    pallas_call x2, Pallas kernels, run_backward(): pl.pallas_call(functools.partial(backward_kernel, states), grid=grid, in_...  70.2 us
    dot_general x20, matrix products, matmul(): return jnp.einsum(dims, left, right, preferred_element_type=F32)  67.8 us
    ppermute x16, starting transfers between devices, shifted(): lax.ppermute(value, axis, [(source, source + steps) for source in range(l...  47.4 us
    ppermute x16, waiting for transfers between devices, shifted(): lax.ppermute(value, axis, [(source, source + steps) for source in range(l...  43.9 us
    ppermute x51, starting transfers between devices, swapped(): lax.ppermute(value, axis, [(source, source ^ bit) for source in range(cou...  43.7 us
    unnamed x430, local copies, waits for them, and re-layouts  34.8 us
    pallas_call x2, Pallas kernels, run_forward(): pl.pallas_call(functools.partial(forward_kernel, states), grid=grid, in_s...  31.9 us
  transfers between devices with their start and end apart: 76, of which 44 were waited for; matrix products, arithmetic and copies ran while one was open for 19% of the time, Pallas kernels for 21%

profile of v2, /device:TPU:0, one launch (start us, length us, event | category | flops | bytes accessed | tf_op | source)
XLA Modules:
  0.0 734.2 jit_solution(7295796456822774134)
XLA Ops:
  13.7 14.2 %slice_bitcast_fusion = (bf16[2048,2,1024]{2,1,0:T(2,128)(2,1)}, bf16[2048,2,1024]{2,1,0:T(2,128)(2,1)}) fusion(bf16[2,2048,2,1024]{3,2,1,0:T(2,128)(2,1)} %param.20), kind=kLoop, calls=%fused_computation | loop fusion | bytes 33554432 | tf_op jit(solution)/shard_map/squeeze | solution.py:1048
  36.1 4.9 multiply_convert_fusion.1
  68.6 10.2 %shard_map.265 = bf16[2,32,1024]{2,1,0:T(8,128)(2,1)S(1)} custom-call(f32[2,256,1024]{2,1,0:T(8,128)S(1)} %fusion.71.r_ref, bf16[2,256,1024]{2,1,0:T(8,128)(2,1)S(1)} %get-tuple-element.215.act_ref, f32[2,256,128]{2,1,0:T(8,128)S(1)} %concatenate.96.col_ref), custom_call_target="tpu_custom_call" | custom-call | flops 50331648 | bytes 16777216 | tf_op jit(solution)/shard_map/pallas_call | solution.py:375
  78.9 4.3 collective-permute-start.9
  85.8 6.2 collective-permute-start.10
  94.6 5.6 collective-permute-start.11
  106.6 15.9 %shard_map.266 = (bf16[2,4096,1024]{2,1,0:T(8,128)(2,1)}, bf16[2,256,1024]{2,1,0:T(8,128)(2,1)S(1)}, bf16[2,256,1024]{2,1,0:T(8,128)(2,1)S(1)}) custom-call(f32[2,256,1024]{2,1,0:T(8,128)S(1)} %fusion.71.r_ref, bf16[2,256,1024]{2,1,0:T(8,128)(2,1)S(1)} %get-tuple-element.215.act_ref, f32[2,256,128]{2,1,0:T(8,128)S(1)} %concatenate.96.col_ref, ...), custom_call_target="tpu_custom_call" | custom-call | flops 67108864 | bytes 16777216 | tf_op jit(solution)/shard_map/pallas_call | solution.py:394
  133.5 12.7 %collective-permute-done.21 = bf16[2,256,512]{2,1,0:T(8,128)(2,1)S(1)} collective-permute-done((bf16[2,256,512]{2,1,0:T(8,128)(2,1)S(1)}, bf16[2,256,512]{2,1,0:T(8,128)(2,1)S(1)}, u32[]{:S(2)}, u32[]{:S(2)}) %collective-permute-start.21) | collective-permute-done | bytes 524320 | tf_op jit(solution)/shard_map/ppermute | solution.py:491
  149.4 11.9 %collective-permute-done.22 = bf16[2,256,512]{2,1,0:T(8,128)(2,1)S(1)} collective-permute-done((bf16[2,256,512]{2,1,0:T(8,128)(2,1)S(1)}, bf16[2,256,512]{2,1,0:T(8,128)(2,1)S(1)}, u32[]{:S(2)}, u32[]{:S(2)}) %collective-permute-start.22) | collective-permute-done | bytes 524320 | tf_op jit(solution)/shard_map/ppermute | solution.py:491
  164.8 4.9 multiply_convert_fusion
  175.3 7.4 %multiply_reduce_fusion.2 = (f32[1024]{0:T(1024)}, f32[2,256,1024]{2,1,0:T(8,128)}, bf16[2,256,1024]{2,1,0:T(8,128)(2,1)S(1)}, f32[2,256,1024]{2,1,0:T(8,128)}, f32[2,256,1024]{2,1,0:T(8,128)}) fusion(bf16[2,256,2,1024]{3,1,0,2:T(8,128)(2,1)S(1)} %multiply_convert_fusion, f32[2,256]{1,0:T(2,128)S(1)} %copy-done.146, ...), kind=kOutput, calls=%fused_computation.92 | convolution fusion | flops 2161114112 | bytes 23101440 | tf_op jit(solution)/shard_map/mrd,id->mri/dot_general | solution.py:776
  191.5 7.2 collective-permute-done.27
  210.6 10.2 %shard_map.267 = bf16[2,32,1024]{2,1,0:T(8,128)(2,1)S(1)} custom-call(f32[2,256,1024]{2,1,0:T(8,128)S(1)} %copy-done, bf16[2,256,1024]{2,1,0:T(8,128)(2,1)S(1)} %copy-done.4, f32[2,256,128]{2,1,0:T(8,128)S(1)} %copy-done.12), custom_call_target="tpu_custom_call" | custom-call | flops 50331648 | bytes 16777216 | tf_op jit(solution)/shard_map/pallas_call | solution.py:375
  220.8 9.1 %shard_map.269 = bf16[2,16,1024]{2,1,0:T(8,128)(2,1)S(1)} custom-call(f32[2,256,1024]{2,1,0:T(8,128)S(1)} %copy-done, f32[2,256,1024]{2,1,0:T(8,128)S(1)} %copy-done.8, f32[2,256,128]{2,1,0:T(8,128)S(1)} %copy-done.12), custom_call_target="tpu_custom_call" | custom-call | flops 41943040 | bytes 16777216 | tf_op jit(solution)/shard_map/pallas_call | solution.py:421
  231.3 5.1 collective-permute-start.28
  241.5 4.9 collective-permute-start.29
  249.0 4.4 collective-permute-done.35
  259.9 16.0 %shard_map.268 = (bf16[2,4096,1024]{2,1,0:T(8,128)(2,1)}, bf16[2,256,1024]{2,1,0:T(8,128)(2,1)S(1)}, bf16[2,256,1024]{2,1,0:T(8,128)(2,1)S(1)}) custom-call(f32[2,256,1024]{2,1,0:T(8,128)S(1)} %copy-done.1, bf16[2,256,1024]{2,1,0:T(8,128)(2,1)S(1)} %copy-done.5, f32[2,256,128]{2,1,0:T(8,128)S(1)} %copy-done.13, bf16[2,256,1024]{2,1,0:T(8,128)(2,1)S(1)} %copy-done.16, ...), custom_call_target="tpu_custom_call" | custom-call | flops 67108864 | bytes 16777216 | tf_op jit(solution)/shard_map/pallas_call | solution.py:394
  278.0 10.7 %shard_map.270 = bf16[8,256,2048]{2,1,0:T(8,128)(2,1)} custom-call(bf16[512,2048]{1,0:T(8,128)(2,1)} %bitcast.286, bf16[512,1024]{1,0:T(8,128)(2,1)} %bitcast.297, bf16[512,2048]{1,0:T(8,128)(2,1)} %bitcast.306, bf16[512,1024]{1,0:T(8,128)(2,1)} %bitcast.283), custom_call_target="tpu_custom_call" | custom-call | flops 4294967296 | bytes 4194304 | tf_op jit(solution)/shard_map/pallas_call | solution.py:674
  290.8 4.9 fusion.27
  300.9 35.1 %shard_map.271 = (f32[2,256,1024]{2,1,0:T(8,128)S(1)}, f32[2,256,1024]{2,1,0:T(8,128)S(1)}, f32[2,256,128]{2,1,0:T(8,128)S(1)}) custom-call(f32[2,256,1024]{2,1,0:T(8,128)S(1)} %copy-done.2, bf16[2,256,1024]{2,1,0:T(8,128)(2,1)S(1)} %copy-done.6, f32[2,256,1024]{2,1,0:T(8,128)S(1)} %copy-done.9, f32[2,256,128]{2,1,0:T(8,128)S(1)} %copy-done.14, ...), custom_call_target="tpu_custom_call" | custom-call | flops 134217728 | bytes 16777216 | tf_op jit(solution)/shard_map/pallas_call | solution.py:443
  338.9 4.2 fusion.147
  354.3 4.7 collective-permute-done.39
  369.7 5.2 bitcast_convert_fusion.1
  384.3 8.5 %collective-permute-done.46 = f32[2,256]{1,0:T(2,128)S(1)} collective-permute-done((f32[2,256]{1,0:T(2,128)S(1)}, f32[2,256]{1,0:T(2,128)S(1)}, u32[]{:S(2)}, u32[]{:S(2)}) %collective-permute-start.46) | collective-permute-done | bytes 2080 | tf_op jit(solution)/shard_map/ppermute | solution.py:491
  392.9 6.9 collective-permute-done.44
  402.6 10.7 %collective-permute-done.48 = bf16[256,1024]{1,0:T(8,128)(2,1)S(1)} collective-permute-done((bf16[256,1024]{1,0:T(8,128)(2,1)S(1)}, bf16[256,1024]{1,0:T(8,128)(2,1)S(1)}, u32[]{:S(2)}, u32[]{:S(2)}) %collective-permute-start.48) | collective-permute-done | bytes 524320 | tf_op jit(solution)/shard_map/ppermute | solution.py:491
  415.9 8.5 %multiply_reduce_fusion.7 = (f32[1024]{0:T(1024)}, f32[2,256,1024]{2,1,0:T(8,128)S(1)}, bf16[2,256,1024]{2,1,0:T(8,128)(2,1)}) fusion(bf16[2,256,1024]{2,1,0:T(8,128)(2,1)S(1)} %get-tuple-element.215.act_ref, bf16[2,256,2,1024]{3,1,0,2:T(8,128)(2,1)S(1)} %copy-done.68, f32[2,256]{1,0:T(2,128)S(1)} %copy-done.196, bf16[2,256,1024]{2,1,0:T(8,128)(2,1)S(1)} %copy-done.44, ...), kind=kOutput, calls=%fused_computation.97 | convolution fusion | flops 2165308416 | bytes 12589056 | tf_op jit(solution)/shard_map/mrd,id->mri/dot_general | solution.py:776
  424.5 9.3 %shard_map.272 = bf16[2,16,1024]{2,1,0:T(8,128)(2,1)S(1)} custom-call(f32[2,256,1024]{2,1,0:T(8,128)S(1)} %fusion.71.r_ref, f32[2,256,1024]{2,1,0:T(8,128)S(1)} %get-tuple-element.204.gm_ref, f32[2,256,128]{2,1,0:T(8,128)S(1)} %concatenate.96.col_ref), custom_call_target="tpu_custom_call" | custom-call | flops 41943040 | bytes 16777216 | tf_op jit(solution)/shard_map/pallas_call | solution.py:421
  435.1 6.7 collective-permute-done.51
  444.3 14.9 %collective-permute-done.52 = bf16[2,32,1024]{2,1,0:T(8,128)(2,1)S(1)} collective-permute-done((bf16[2,32,1024]{2,1,0:T(8,128)(2,1)S(1)}, bf16[2,32,1024]{2,1,0:T(8,128)(2,1)S(1)}, u32[]{:S(2)}, u32[]{:S(2)}) %collective-permute-start.52) | collective-permute-done | bytes 131104 | tf_op jit(solution)/shard_map/ppermute | solution.py:486
  461.3 6.1 shard_map.273
  474.2 10.8 %shard_map.274 = bf16[8,256,2048]{2,1,0:T(8,128)(2,1)} custom-call(bf16[512,2048]{1,0:T(8,128)(2,1)} %bitcast.311, bf16[512,1024]{1,0:T(8,128)(2,1)} %bitcast.323, bf16[512,2048]{1,0:T(8,128)(2,1)} %bitcast.307, bf16[512,1024]{1,0:T(8,128)(2,1)} %bitcast.282), custom_call_target="tpu_custom_call" | custom-call | flops 4294967296 | bytes 4194304 | tf_op jit(solution)/shard_map/pallas_call | solution.py:674
  494.1 35.2 %shard_map.275 = (f32[2,256,1024]{2,1,0:T(8,128)S(1)}, f32[2,256,1024]{2,1,0:T(8,128)S(1)}, f32[2,256,128]{2,1,0:T(8,128)S(1)}) custom-call(f32[2,256,1024]{2,1,0:T(8,128)S(1)} %fusion.71.r_ref, bf16[2,256,1024]{2,1,0:T(8,128)(2,1)S(1)} %get-tuple-element.215.act_ref, f32[2,256,1024]{2,1,0:T(8,128)S(1)} %copy-done.11, ...), custom_call_target="tpu_custom_call" | custom-call | flops 134217728 | bytes 16777216 | tf_op jit(solution)/shard_map/pallas_call | solution.py:443
  545.3 9.0 %multiply_reduce_fusion.8 = (f32[1024]{0:T(1024)S(1)}, f32[1024]{0:T(1024)S(1)}, f32[1024]{0:T(1024)S(1)}, f32[1024]{0:T(1024)S(1)}, f32[1024]{0:T(1024)S(1)}, /...) fusion(f32[2,259,1024]{2,1,0:T(8,128)S(1)} %copy-done.47, ...), kind=kOutput, calls=%fused_computation.98 | convolution fusion | flops 188209152 | bytes 32014336 | tf_op jit(solution)/shard_map/mrc,ic->mri/dot_general | solution.py:776
  561.5 9.8 %bitcast_convert_fusion = bf16[2,256,2048]{2,1,0:T(8,128)(2,1)S(1)} fusion(bf16[2048,2,1024,1]{2,1,0,3:T(2,128)(2,1)} %bitcast.289, bf16[2,256,1,1024]{3,1,0,2:T(8,128)(2,1)S(1)} %bitcast.324, bf16[2,256,1,1024]{3,1,0,2:T(8,128)(2,1)S(1)} %bitcast.302), kind=kOutput, calls=%fused_computation.10 | convolution fusion | flops 4297064448 | bytes 12582912 | tf_op jit(solution)/shard_map/bptg,htg->bph/dot_general | solution.py:776
  578.7 8.8 %collective-permute-done.64 = bf16[256,1024]{1,0:T(8,128)(2,1)S(1)} collective-permute-done((bf16[256,1024]{1,0:T(8,128)(2,1)S(1)}, bf16[256,1024]{1,0:T(8,128)(2,1)S(1)}, u32[]{:S(2)}, u32[]{:S(2)}) %collective-permute-start.64) | collective-permute-done | bytes 524320 | tf_op jit(solution)/shard_map/ppermute | solution.py:491
  587.5 18.6 %collective-permute-done.63 = bf16[256,1024]{1,0:T(8,128)(2,1)S(1)} collective-permute-done((bf16[256,1024]{1,0:T(8,128)(2,1)S(1)}, bf16[256,1024]{1,0:T(8,128)(2,1)S(1)}, u32[]{:S(2)}, u32[]{:S(2)}) %collective-permute-start.63) | collective-permute-done | bytes 524320 | tf_op jit(solution)/shard_map/ppermute | solution.py:491
  607.2 6.1 shard_map.276
  615.8 7.5 %collective-permute-start.65 = (bf16[256,1024]{1,0:T(8,128)(2,1)}, bf16[256,1024]{1,0:T(8,128)(2,1)}, u32[]{:S(2)}, u32[]{:S(2)}) collective-permute-start(bf16[256,1024]{1,0:T(8,128)(2,1)} %get-tuple-element.231), channel_id=1, source_target_pairs={{0,8},{4,12},{1,9},{5,13},{2,10},{6,14},{3,11},{7,15}} | collective-permute-start | bytes 1572872 | tf_op jit(solution)/shard_map/ppermute | solution.py:709
  636.6 5.2 collective-permute-start.68
  643.4 12.9 %collective-permute-done.62 = bf16[336,1024]{1,0:T(8,128)(2,1)S(1)} collective-permute-done((bf16[336,1024]{1,0:T(8,128)(2,1)}, bf16[336,1024]{1,0:T(8,128)(2,1)S(1)}, u32[]{:S(2)}, u32[]{:S(2)}) %collective-permute-start.62) | collective-permute-done | bytes 688160 | tf_op jit(solution)/shard_map/ppermute | solution.py:491
  659.3 5.4 collective-permute-done.68
  667.4 11.8 %collective-permute-start.71 = (bf16[256,1024]{1,0:T(8,128)(2,1)}, bf16[256,1024]{1,0:T(8,128)(2,1)}, u32[]{:S(2)}, u32[]{:S(2)}) collective-permute-start(bf16[256,1024]{1,0:T(8,128)(2,1)} %get-tuple-element.227), channel_id=1, source_target_pairs={{0,8},{4,12},{8,16},{12,20},{16,24},{20,28},{1,9},{5,13},{9,17},{1... | collective-permute-start | bytes 1572872 | tf_op jit(solution)/shard_map/ppermute | solution.py:709
  686.0 4.6 collective-permute-start.70
  692.9 10.8 %collective-permute-done.71 = bf16[256,1024]{1,0:T(8,128)(2,1)} collective-permute-done((bf16[256,1024]{1,0:T(8,128)(2,1)}, bf16[256,1024]{1,0:T(8,128)(2,1)}, u32[]{:S(2)}, u32[]{:S(2)}) %collective-permute-start.71) | collective-permute-done | bytes 524320 | tf_op jit(solution)/shard_map/ppermute | solution.py:709
  703.7 5.5 collective-permute-done.70
  720.3 5.2 copy.138
  (747 shorter events, 258.2 us)
Async XLA Ops:
  7.2 463.4 %reduce-scatter.4.cloned.1.call-start = ((), (), s32[]{:S(2)}) async-start(), calls=%async_computation.3 | async-start | bytes 9437184 | tf_op jit(solution)/shard_map/reduce_scatter | solution.py:917
  7.9 21.3 %collective-permute-start.5 = (f32[2,512]{1,0:T(2,128)S(1)}, f32[2,512]{1,0:T(2,128)S(1)}, u32[]{:S(2)}, u32[]{:S(2)}) collective-permute-start(f32[2,512]{1,0:T(2,128)S(1)} %convert_element_type.571), channel_id=1, source_target_pairs={{0,1},{1,0},{2,3},{3,2},{4,5},{5,4},{6,7},{7,6},{8,9},{9,8},{10,11... | collective-permute-start | bytes 12296 | tf_op jit(solution)/shard_map/ppermute | solution.py:491
  8.4 20.4 %collective-permute-start.3 = (f32[2,512]{1,0:T(2,128)S(1)}, f32[2,512]{1,0:T(2,128)S(1)}, u32[]{:S(2)}, u32[]{:S(2)}) collective-permute-start(f32[2,512]{1,0:T(2,128)S(1)} %convert_element_type.571), channel_id=1, source_target_pairs={{0,2},{1,3},{2,0},{3,1},{4,6},{5,7},{6,4},{7,5},{8,10},{9,11},{10,... | collective-permute-start | bytes 12296 | tf_op jit(solution)/shard_map/ppermute | solution.py:491
  13.3 16.7 %collective-permute-start = (bf16[2,256,512]{2,1,0:T(8,128)(2,1)S(1)}, bf16[2,256,512]{2,1,0:T(8,128)(2,1)S(1)}, u32[]{:S(2)}, u32[]{:S(2)}) collective-permute-start(bf16[2,256,512]{2,1,0:T(8,128)(2,1)S(1)} %multiply_convert_fusion.6), channel_id=1, source_target_pairs={{0,2},{1,3},{2,0},{3,1},{4,6},{5,7},{6,4},{7,5},{8,10},{9,11},{10,... | collective-permute-start | bytes 1572872 | tf_op jit(solution)/shard_map/ppermute | solution.py:491
  13.4 17.6 %collective-permute-start.2 = (bf16[2,256,512]{2,1,0:T(8,128)(2,1)S(1)}, bf16[2,256,512]{2,1,0:T(8,128)(2,1)S(1)}, u32[]{:S(2)}, u32[]{:S(2)}) collective-permute-start(bf16[2,256,512]{2,1,0:T(8,128)(2,1)S(1)} %multiply_convert_fusion.6), channel_id=1, source_target_pairs={{0,1},{1,0},{2,3},{3,2},{4,5},{5,4},{6,7},{7,6},{8,9},{9,8},{10,11... | collective-permute-start | bytes 1572872 | tf_op jit(solution)/shard_map/ppermute | solution.py:491
  53.6 8.4 %collective-permute-start.8 = (bf16[2,256,160]{2,1,0:T(8,128)(2,1)S(1)}, bf16[2,256,160]{2,1,0:T(8,128)(2,1)S(1)}, u32[]{:S(2)}, u32[]{:S(2)}) collective-permute-start(bf16[2,256,160]{2,1,0:T(8,128)(2,1)S(1)} %fusion.91), channel_id=1, source_target_pairs={{0,2},{1,3},{2,0},{3,1},{4,6},{5,7},{6,4},{7,5},{8,10},{9,11},{10,... | collective-permute-start | bytes 491528 | tf_op jit(solution)/shard_map/ppermute | solution.py:491
  55.8 27.5 %collective-permute-start.12 = (bf16[512,256]{1,0:T(8,128)(2,1)}, bf16[512,256]{1,0:T(8,128)(2,1)}, u32[]{:S(2)}, u32[]{:S(2)}) collective-permute-start(bf16[512,256]{1,0:T(8,128)(2,1)} %bitcast.17), channel_id=1, source_target_pairs={{0,4},{4,0},{8,12},{12,8},{16,20},{20,16},{24,28},{28,24},{1,5},{5... | collective-permute-start | bytes 786440 | tf_op jit(solution)/shard_map/ppermute | solution.py:491
  83.2 10.6 %collective-permute-start.13 = (bf16[512,256]{1,0:T(8,128)(2,1)}, bf16[512,256]{1,0:T(8,128)(2,1)S(1)}, u32[]{:S(2)}, u32[]{:S(2)}) collective-permute-start(bf16[512,256]{1,0:T(8,128)(2,1)} %collective-permute-done.12), channel_id=1, source_target_pairs={{0,2},{1,3},{2,0},{3,1},{4,6},{5,7},{6,4},{7,5},{8,10},{9,11},{10,... | collective-permute-start | bytes 786440 | tf_op jit(solution)/shard_map/ppermute | solution.py:491
  85.8 8.7 %collective-permute-start.10 = (bf16[2,32,1024]{2,1,0:T(8,128)(2,1)S(1)}, bf16[2,32,1024]{2,1,0:T(8,128)(2,1)S(1)}, u32[]{:S(2)}, u32[]{:S(2)}) collective-permute-start(bf16[2,32,1024]{2,1,0:T(8,128)(2,1)S(1)} %pad_maximum_fusion.14), channel_id=1, source_target_pairs={{0,8},{4,12},{8,16},{12,20},{16,24},{20,28},{1,9},{5,13},{9,17},{1... | collective-permute-start | bytes 393224 | tf_op jit(solution)/shard_map/ppermute | solution.py:486
  92.2 11.9 %collective-permute-start.16 = (bf16[2,256,512]{2,1,0:T(8,128)(2,1)S(1)}, bf16[2,256,512]{2,1,0:T(8,128)(2,1)S(1)}, u32[]{:S(2)}, u32[]{:S(2)}) collective-permute-start(bf16[2,256,512]{2,1,0:T(8,128)(2,1)S(1)} %fusion.72), channel_id=1, source_target_pairs={{0,2},{1,3},{2,0},{3,1},{4,6},{5,7},{6,4},{7,5},{8,10},{9,11},{10,... | collective-permute-start | bytes 1572872 | tf_op jit(solution)/shard_map/ppermute | solution.py:491
  93.8 10.4 %collective-permute-start.15 = (bf16[512,256]{1,0:T(8,128)(2,1)}, bf16[512,256]{1,0:T(8,128)(2,1)S(1)}, u32[]{:S(2)}, u32[]{:S(2)}) collective-permute-start(bf16[512,256]{1,0:T(8,128)(2,1)} %collective-permute-done.12), channel_id=1, source_target_pairs={{0,1},{1,0},{2,3},{3,2},{4,5},{5,4},{6,7},{7,6},{8,9},{9,8},{10,11... | collective-permute-start | bytes 786440 | tf_op jit(solution)/shard_map/ppermute | solution.py:491
  93.8 10.4 %collective-permute-start.14 = (bf16[512,256]{1,0:T(8,128)(2,1)S(1)}, bf16[512,256]{1,0:T(8,128)(2,1)S(1)}, u32[]{:S(2)}, u32[]{:S(2)}) collective-permute-start(bf16[512,256]{1,0:T(8,128)(2,1)S(1)} %collective-permute-done.13), channel_id=1, source_target_pairs={{0,1},{1,0},{2,3},{3,2},{4,5},{5,4},{6,7},{7,6},{8,9},{9,8},{10,11... | collective-permute-start | bytes 786440 | tf_op jit(solution)/shard_map/ppermute | solution.py:491
  94.6 9.5 %collective-permute-start.11 = (bf16[2,16,1024]{2,1,0:T(8,128)(2,1)S(1)}, bf16[2,16,1024]{2,1,0:T(8,128)(2,1)S(1)}, u32[]{:S(2)}, u32[]{:S(2)}) collective-permute-start(bf16[2,16,1024]{2,1,0:T(8,128)(2,1)S(1)} %add_convert_fusion.5), channel_id=1, source_target_pairs={{0,16},{4,20},{8,24},{12,28},{1,17},{5,21},{9,25},{13,29},{2,18},{... | collective-permute-start | bytes 196616 | tf_op jit(solution)/shard_map/ppermute | solution.py:486
  100.8 21.7 %collective-permute-start.18 = (bf16[2,256,512]{2,1,0:T(8,128)(2,1)S(1)}, bf16[2,256,512]{2,1,0:T(8,128)(2,1)S(1)}, u32[]{:S(2)}, u32[]{:S(2)}) collective-permute-start(bf16[2,256,512]{2,1,0:T(8,128)(2,1)S(1)} %fusion.72), channel_id=1, source_target_pairs={{0,1},{1,0},{2,3},{3,2},{4,5},{5,4},{6,7},{7,6},{8,9},{9,8},{10,11... | collective-permute-start | bytes 1572872 | tf_op jit(solution)/shard_map/ppermute | solution.py:491
  104.1 18.4 %collective-permute-start.17 = (bf16[2,256,512]{2,1,0:T(8,128)(2,1)S(1)}, bf16[2,256,512]{2,1,0:T(8,128)(2,1)S(1)}, u32[]{:S(2)}, u32[]{:S(2)}) collective-permute-start(bf16[2,256,512]{2,1,0:T(8,128)(2,1)S(1)} %collective-permute-done.16), channel_id=1, source_target_pairs={{0,1},{1,0},{2,3},{3,2},{4,5},{5,4},{6,7},{7,6},{8,9},{9,8},{10,11... | collective-permute-start | bytes 1572872 | tf_op jit(solution)/shard_map/ppermute | solution.py:491
  131.9 14.3 %collective-permute-start.21 = (bf16[2,256,512]{2,1,0:T(8,128)(2,1)S(1)}, bf16[2,256,512]{2,1,0:T(8,128)(2,1)S(1)}, u32[]{:S(2)}, u32[]{:S(2)}) collective-permute-start(bf16[2,256,512]{2,1,0:T(8,128)(2,1)S(1)} %select_convert_fusion.4), channel_id=1, source_target_pairs={{0,2},{1,3},{2,0},{3,1},{4,6},{5,7},{6,4},{7,5},{8,10},{9,11},{10,... | collective-permute-start | bytes 1572872 | tf_op jit(solution)/shard_map/ppermute | solution.py:491
  147.9 13.4 %collective-permute-start.22 = (bf16[2,256,512]{2,1,0:T(8,128)(2,1)S(1)}, bf16[2,256,512]{2,1,0:T(8,128)(2,1)S(1)}, u32[]{:S(2)}, u32[]{:S(2)}) collective-permute-start(bf16[2,256,512]{2,1,0:T(8,128)(2,1)S(1)} %get-tuple-element.213), channel_id=1, source_target_pairs={{0,2},{1,3},{2,0},{3,1},{4,6},{5,7},{6,4},{7,5},{8,10},{9,11},{10,... | collective-permute-start | bytes 1572872 | tf_op jit(solution)/shard_map/ppermute | solution.py:491
  149.4 11.9 %collective-permute-start.24 = (bf16[2,256,512]{2,1,0:T(8,128)(2,1)S(1)}, bf16[2,256,512]{2,1,0:T(8,128)(2,1)S(1)}, u32[]{:S(2)}, u32[]{:S(2)}) collective-permute-start(bf16[2,256,512]{2,1,0:T(8,128)(2,1)S(1)} %get-tuple-element.213), channel_id=1, source_target_pairs={{0,1},{1,0},{2,3},{3,2},{4,5},{5,4},{6,7},{7,6},{8,9},{9,8},{10,11... | collective-permute-start | bytes 1572872 | tf_op jit(solution)/shard_map/ppermute | solution.py:491
  189.9 8.8 %collective-permute-start.27 = (bf16[2,256,160]{2,1,0:T(8,128)(2,1)S(1)}, bf16[2,256,160]{2,1,0:T(8,128)(2,1)S(1)}, u32[]{:S(2)}, u32[]{:S(2)}) collective-permute-start(bf16[2,256,160]{2,1,0:T(8,128)(2,1)S(1)} %fusion.92), channel_id=1, source_target_pairs={{0,2},{1,3},{2,0},{3,1},{4,6},{5,7},{6,4},{7,5},{8,10},{9,11},{10,... | collective-permute-start | bytes 491528 | tf_op jit(solution)/shard_map/ppermute | solution.py:491
  230.0 7.9 %collective-permute-start.34 = (bf16[2,32,1024]{2,1,0:T(8,128)(2,1)S(1)}, bf16[2,32,1024]{2,1,0:T(8,128)(2,1)S(1)}, u32[]{:S(2)}, u32[]{:S(2)}) collective-permute-start(bf16[2,32,1024]{2,1,0:T(8,128)(2,1)S(1)} %pad_maximum_fusion.16), channel_id=1, source_target_pairs={{4,0},{8,4},{12,8},{16,12},{20,16},{24,20},{28,24},{5,1},{9,5},{13... | collective-permute-start | bytes 393224 | tf_op jit(solution)/shard_map/ppermute | solution.py:486
  231.3 10.1 %collective-permute-start.28 = (bf16[2,32,1024]{2,1,0:T(8,128)(2,1)S(1)}, bf16[2,32,1024]{2,1,0:T(8,128)(2,1)S(1)}, u32[]{:S(2)}, u32[]{:S(2)}) collective-permute-start(bf16[2,32,1024]{2,1,0:T(8,128)(2,1)S(1)} %shard_map.267), channel_id=1, source_target_pairs={{0,4},{4,8},{8,12},{12,16},{16,20},{20,24},{24,28},{1,5},{5,9},{9,... | collective-permute-start | bytes 393224 | tf_op jit(solution)/shard_map/ppermute | solution.py:486
  241.5 7.5 %collective-permute-start.29 = (bf16[2,32,1024]{2,1,0:T(8,128)(2,1)S(1)}, bf16[2,32,1024]{2,1,0:T(8,128)(2,1)S(1)}, u32[]{:S(2)}, u32[]{:S(2)}) collective-permute-start(bf16[2,32,1024]{2,1,0:T(8,128)(2,1)S(1)} %pad_maximum_fusion.15), channel_id=1, source_target_pairs={{0,8},{4,12},{8,16},{12,20},{16,24},{20,28},{1,9},{5,13},{9,17},{1... | collective-permute-start | bytes 393224 | tf_op jit(solution)/shard_map/ppermute | solution.py:486
  257.9 30.9 %collective-permute-start.36 = (bf16[2,16,1024]{2,1,0:T(8,128)(2,1)}, bf16[2,16,1024]{2,1,0:T(8,128)(2,1)}, u32[]{:S(2)}, u32[]{:S(2)}) collective-permute-start(bf16[2,16,1024]{2,1,0:T(8,128)(2,1)} %get-tuple-element.306), channel_id=1, source_target_pairs={{16,0},{20,4},{24,8},{28,12},{17,1},{21,5},{25,9},{29,13},{18,2},{... | collective-permute-start | bytes 196616 | tf_op jit(solution)/shard_map/ppermute | solution.py:486
  290.6 425.2 %reduce-scatter.8.cloned.1.call-start = ((), (), s32[]{:S(2)}) async-start(), calls=%async_computation.5 | async-start | bytes 2621440 | tf_op jit(solution)/shard_map/reduce_scatter | solution.py:687
  297.6 39.8 %collective-permute-start.37 = (bf16[512,1024]{1,0:T(8,128)(2,1)S(1)}, bf16[512,1024]{1,0:T(8,128)(2,1)S(1)}, u32[]{:S(2)}, u32[]{:S(2)}) collective-permute-start(bf16[512,1024]{1,0:T(8,128)(2,1)S(1)} %pad_maximum_fusion.6), channel_id=1, source_target_pairs={{0,4},{4,0},{8,12},{12,8},{16,20},{20,16},{24,28},{28,24},{1,5},{5... | collective-permute-start | bytes 3145736 | tf_op jit(solution)/shard_map/ppermute | solution.py:491
  299.0 37.0 %collective-permute-start.33 = (bf16[2,256,512]{2,1,0:T(8,128)(2,1)S(1)}, bf16[2,256,512]{2,1,0:T(8,128)(2,1)S(1)}, u32[]{:S(2)}, u32[]{:S(2)}) collective-permute-start(bf16[2,256,512]{2,1,0:T(8,128)(2,1)S(1)} %select_convert_fusion.3), channel_id=1, source_target_pairs={{0,2},{1,3},{2,0},{3,1},{4,6},{5,7},{6,4},{7,5},{8,10},{9,11},{10,... | collective-permute-start | bytes 1572872 | tf_op jit(solution)/shard_map/ppermute | solution.py:491
  375.8 24.0 %collective-permute-start.44 = (bf16[256,1024]{1,0:T(8,128)(2,1)S(1)}, bf16[256,1024]{1,0:T(8,128)(2,1)S(1)}, u32[]{:S(2)}, u32[]{:S(2)}) collective-permute-start(bf16[256,1024]{1,0:T(8,128)(2,1)S(1)} %get-tuple-element.276), channel_id=1, source_target_pairs={{0,4},{4,0},{8,12},{12,8},{16,20},{20,16},{24,28},{28,24},{1,5},{5... | collective-permute-start | bytes 1572872 | tf_op jit(solution)/shard_map/ppermute | solution.py:491
  379.1 20.7 %collective-permute-start.43 = (bf16[2,256,512]{2,1,0:T(8,128)(2,1)S(1)}, bf16[2,256,512]{2,1,0:T(8,128)(2,1)S(1)}, u32[]{:S(2)}, u32[]{:S(2)}) collective-permute-start(bf16[2,256,512]{2,1,0:T(8,128)(2,1)S(1)} %select_convert_fusion.2), channel_id=1, source_target_pairs={{0,2},{1,3},{2,0},{3,1},{4,6},{5,7},{6,4},{7,5},{8,10},{9,11},{10,... | collective-permute-start | bytes 1572872 | tf_op jit(solution)/shard_map/ppermute | solution.py:491
  381.1 11.7 %collective-permute-start.46 = (f32[2,256]{1,0:T(2,128)S(1)}, f32[2,256]{1,0:T(2,128)S(1)}, u32[]{:S(2)}, u32[]{:S(2)}) collective-permute-start(f32[2,256]{1,0:T(2,128)S(1)} %add.575), channel_id=1, source_target_pairs={{0,2},{1,3},{2,0},{3,1},{4,6},{5,7},{6,4},{7,5},{8,10},{9,11},{10,... | collective-permute-start | bytes 6152 | tf_op jit(solution)/shard_map/ppermute | solution.py:491
  382.3 31.0 %collective-permute-start.48 = (bf16[256,1024]{1,0:T(8,128)(2,1)S(1)}, bf16[256,1024]{1,0:T(8,128)(2,1)S(1)}, u32[]{:S(2)}, u32[]{:S(2)}) collective-permute-start(bf16[256,1024]{1,0:T(8,128)(2,1)S(1)} %get-tuple-element.275), channel_id=1, source_target_pairs={{0,4},{4,0},{8,12},{12,8},{16,20},{20,16},{24,28},{28,24},{1,5},{5... | collective-permute-start | bytes 1572872 | tf_op jit(solution)/shard_map/ppermute | solution.py:491
  401.2 12.5 %collective-permute-start.47 = (bf16[2,256,512]{2,1,0:T(8,128)(2,1)S(1)}, bf16[2,256,512]{2,1,0:T(8,128)(2,1)S(1)}, u32[]{:S(2)}, u32[]{:S(2)}) collective-permute-start(bf16[2,256,512]{2,1,0:T(8,128)(2,1)S(1)} %multiply_convert_fusion.4), channel_id=1, source_target_pairs={{0,2},{1,3},{2,0},{3,1},{4,6},{5,7},{6,4},{7,5},{8,10},{9,11},{10,... | collective-permute-start | bytes 1572872 | tf_op jit(solution)/shard_map/ppermute | solution.py:491
  402.6 11.2 %collective-permute-start.50 = (bf16[2,256,512]{2,1,0:T(8,128)(2,1)S(1)}, bf16[2,256,512]{2,1,0:T(8,128)(2,1)S(1)}, u32[]{:S(2)}, u32[]{:S(2)}) collective-permute-start(bf16[2,256,512]{2,1,0:T(8,128)(2,1)S(1)} %multiply_convert_fusion.4), channel_id=1, source_target_pairs={{0,1},{1,0},{2,3},{3,2},{4,5},{5,4},{6,7},{7,6},{8,9},{9,8},{10,11... | collective-permute-start | bytes 1572872 | tf_op jit(solution)/shard_map/ppermute | solution.py:491
  433.8 8.0 %collective-permute-start.51 = (bf16[2,32,1024]{2,1,0:T(8,128)(2,1)S(1)}, bf16[2,32,1024]{2,1,0:T(8,128)(2,1)S(1)}, u32[]{:S(2)}, u32[]{:S(2)}) collective-permute-start(bf16[2,32,1024]{2,1,0:T(8,128)(2,1)S(1)} %pad_maximum_fusion.18), channel_id=1, source_target_pairs={{4,0},{8,4},{12,8},{16,12},{20,16},{24,20},{28,24},{5,1},{9,5},{13... | collective-permute-start | bytes 393224 | tf_op jit(solution)/shard_map/ppermute | solution.py:486
  442.0 17.3 %collective-permute-start.52 = (bf16[2,32,1024]{2,1,0:T(8,128)(2,1)S(1)}, bf16[2,32,1024]{2,1,0:T(8,128)(2,1)S(1)}, u32[]{:S(2)}, u32[]{:S(2)}) collective-permute-start(bf16[2,32,1024]{2,1,0:T(8,128)(2,1)S(1)} %pad_maximum_fusion.19), channel_id=1, source_target_pairs={{8,0},{12,4},{16,8},{20,12},{24,16},{28,20},{9,1},{13,5},{17,9},{2... | collective-permute-start | bytes 393224 | tf_op jit(solution)/shard_map/ppermute | solution.py:486
  460.0 8.8 %collective-permute-start.53 = (bf16[2,16,1024]{2,1,0:T(8,128)(2,1)}, bf16[2,16,1024]{2,1,0:T(8,128)(2,1)}, u32[]{:S(2)}, u32[]{:S(2)}) collective-permute-start(bf16[2,16,1024]{2,1,0:T(8,128)(2,1)} %add_convert_fusion.2), channel_id=1, source_target_pairs={{16,0},{20,4},{24,8},{28,12},{17,1},{21,5},{25,9},{29,13},{18,2},{... | collective-permute-start | bytes 196616 | tf_op jit(solution)/shard_map/ppermute | solution.py:486
  470.6 246.5 %reduce-scatter.6.cloned.1.call-start = ((), (), s32[]{:S(2)}) async-start(), calls=%async_computation.4 | async-start | bytes 9437184 | tf_op jit(solution)/shard_map/reduce_scatter | solution.py:917
  572.7 14.8 %collective-permute-start.64 = (bf16[256,1024]{1,0:T(8,128)(2,1)S(1)}, bf16[256,1024]{1,0:T(8,128)(2,1)S(1)}, u32[]{:S(2)}, u32[]{:S(2)}) collective-permute-start(bf16[256,1024]{1,0:T(8,128)(2,1)S(1)} %get-tuple-element.274), channel_id=1, source_target_pairs={{0,4},{4,0},{8,12},{12,8},{16,20},{20,16},{24,28},{28,24},{1,5},{5... | collective-permute-start | bytes 1572872 | tf_op jit(solution)/shard_map/ppermute | solution.py:491
  574.6 31.5 %collective-permute-start.63 = (bf16[256,1024]{1,0:T(8,128)(2,1)S(1)}, bf16[256,1024]{1,0:T(8,128)(2,1)S(1)}, u32[]{:S(2)}, u32[]{:S(2)}) collective-permute-start(bf16[256,1024]{1,0:T(8,128)(2,1)S(1)} %get-tuple-element.273), channel_id=1, source_target_pairs={{0,4},{4,0},{8,12},{12,8},{16,20},{20,16},{24,28},{28,24},{1,5},{5... | collective-permute-start | bytes 1572872 | tf_op jit(solution)/shard_map/ppermute | solution.py:491
  577.9 47.0 %collective-permute-start.59 = (bf16[2,256,512]{2,1,0:T(8,128)(2,1)}, bf16[2,256,512]{2,1,0:T(8,128)(2,1)}, u32[]{:S(2)}, u32[]{:S(2)}) collective-permute-start(bf16[2,256,512]{2,1,0:T(8,128)(2,1)} %select_convert_fusion.1), channel_id=1, source_target_pairs={{0,2},{1,3},{2,0},{3,1},{4,6},{5,7},{6,4},{7,5},{8,10},{9,11},{10,... | collective-permute-start | bytes 1572872 | tf_op jit(solution)/shard_map/ppermute | solution.py:491
  615.8 17.9 %collective-permute-start.65 = (bf16[256,1024]{1,0:T(8,128)(2,1)}, bf16[256,1024]{1,0:T(8,128)(2,1)}, u32[]{:S(2)}, u32[]{:S(2)}) collective-permute-start(bf16[256,1024]{1,0:T(8,128)(2,1)} %get-tuple-element.231), channel_id=1, source_target_pairs={{0,8},{4,12},{1,9},{5,13},{2,10},{6,14},{3,11},{7,15}} | collective-permute-start | bytes 1572872 | tf_op jit(solution)/shard_map/ppermute | solution.py:709
  623.3 10.4 %collective-permute-start.66 = (bf16[256,1024]{1,0:T(8,128)(2,1)}, bf16[256,1024]{1,0:T(8,128)(2,1)}, u32[]{:S(2)}, u32[]{:S(2)}) collective-permute-start(bf16[256,1024]{1,0:T(8,128)(2,1)} %get-tuple-element.230), channel_id=1, source_target_pairs={{24,16},{28,20},{25,17},{29,21},{26,18},{30,22},{27,19},{31,23}} | collective-permute-start | bytes 1572872 | tf_op jit(solution)/shard_map/ppermute | solution.py:710
  629.5 26.9 %collective-permute-start.62 = (bf16[336,1024]{1,0:T(8,128)(2,1)}, bf16[336,1024]{1,0:T(8,128)(2,1)S(1)}, u32[]{:S(2)}, u32[]{:S(2)}) collective-permute-start(bf16[336,1024]{1,0:T(8,128)(2,1)} %pad_maximum_fusion.9), channel_id=1, source_target_pairs={{0,4},{4,0},{8,12},{12,8},{16,20},{20,16},{24,28},{28,24},{1,5},{5... | collective-permute-start | bytes 2064392 | tf_op jit(solution)/shard_map/ppermute | solution.py:491
  636.6 28.2 %collective-permute-start.68 = (bf16[256,1024]{1,0:T(8,128)(2,1)}, bf16[256,1024]{1,0:T(8,128)(2,1)}, u32[]{:S(2)}, u32[]{:S(2)}) collective-permute-start(bf16[256,1024]{1,0:T(8,128)(2,1)} %get-tuple-element.229), channel_id=1, source_target_pairs={{0,8},{4,12},{8,16},{12,20},{1,9},{5,13},{9,17},{13,21},{2,10},{6,... | collective-permute-start | bytes 1572872 | tf_op jit(solution)/shard_map/ppermute | solution.py:709
  641.8 23.0 %collective-permute-start.69 = (bf16[256,1024]{1,0:T(8,128)(2,1)}, bf16[256,1024]{1,0:T(8,128)(2,1)}, u32[]{:S(2)}, u32[]{:S(2)}) collective-permute-start(bf16[256,1024]{1,0:T(8,128)(2,1)} %get-tuple-element.228), channel_id=1, source_target_pairs={{16,8},{20,12},{24,16},{28,20},{17,9},{21,13},{25,17},{29,21},{18,... | collective-permute-start | bytes 1572872 | tf_op jit(solution)/shard_map/ppermute | solution.py:710
  659.3 23.7 %collective-permute-start.67 = (bf16[208,1024]{1,0:T(8,128)(2,1)}, bf16[208,1024]{1,0:T(8,128)(2,1)}, u32[]{:S(2)}, u32[]{:S(2)}) collective-permute-start(bf16[208,1024]{1,0:T(8,128)(2,1)} %pad_maximum_fusion.10), channel_id=1, source_target_pairs={{0,8},{4,12},{8,0},{12,4},{16,24},{20,28},{24,16},{28,20},{1,9},{5... | collective-permute-start | bytes 1277960 | tf_op jit(solution)/shard_map/ppermute | solution.py:491
  667.4 36.4 %collective-permute-start.71 = (bf16[256,1024]{1,0:T(8,128)(2,1)}, bf16[256,1024]{1,0:T(8,128)(2,1)}, u32[]{:S(2)}, u32[]{:S(2)}) collective-permute-start(bf16[256,1024]{1,0:T(8,128)(2,1)} %get-tuple-element.227), channel_id=1, source_target_pairs={{0,8},{4,12},{8,16},{12,20},{16,24},{20,28},{1,9},{5,13},{9,17},{1... | collective-permute-start | bytes 1572872 | tf_op jit(solution)/shard_map/ppermute | solution.py:709
  679.2 24.5 %collective-permute-start.72 = (bf16[256,1024]{1,0:T(8,128)(2,1)}, bf16[256,1024]{1,0:T(8,128)(2,1)}, u32[]{:S(2)}, u32[]{:S(2)}) collective-permute-start(bf16[256,1024]{1,0:T(8,128)(2,1)} %get-tuple-element.226), channel_id=1, source_target_pairs={{8,0},{12,4},{16,8},{20,12},{24,16},{28,20},{9,1},{13,5},{17,9},{2... | collective-permute-start | bytes 1572872 | tf_op jit(solution)/shard_map/ppermute | solution.py:710
  686.0 23.2 %collective-permute-start.70 = (bf16[144,1024]{1,0:T(8,128)(2,1)S(1)}, bf16[144,1024]{1,0:T(8,128)(2,1)}, u32[]{:S(2)}, u32[]{:S(2)}) collective-permute-start(bf16[144,1024]{1,0:T(8,128)(2,1)S(1)} %pad_maximum_fusion.13), channel_id=1, source_target_pairs={{0,16},{4,20},{8,24},{12,28},{16,0},{20,4},{24,8},{28,12},{1,17},{... | collective-permute-start | bytes 884744 | tf_op jit(solution)/shard_map/ppermute | solution.py:491
  (243 other events, 2135.1 us)
Sparse Core Ops, SparseCore 0:
  290.7 170.0 reduce-scatter.3
  470.7 44.3 reduce-scatter.7
  518.8 184.5 reduce-scatter.5

commit v3 on v2

--- a/solution.py
+++ b/solution.py
@@ -16,27 +16,33 @@
 LOW = jnp.bfloat16
 
 
-def tables(states):
-    wide = CH * states
-    rows = np.arange(wide)
-    lanes = np.arange(LANES)
-    repeat = (rows[:, None] // states == np.arange(CH)[None, :]).astype(np.float32)
-    picks = [lanes[:, None] == group * states + rows[None, :] % states for group in (0, 1, 3)]
-    diagonal = (np.arange(CH)[:, None] == rows[None, :] // states).astype(np.float32)
-    fold = (np.arange(3 * LANES)[:, None] // LANES == lanes[None, :] // states).astype(np.float32)
-    fold_own = (rows[:, None] % states == lanes[None, :] % states).astype(np.float32)
-    low = lambda value: jnp.asarray(value, LOW)
-    return dict(
-        pick=low(np.stack(picks).astype(np.float32)),
-        diagonal=jnp.asarray(diagonal, F32),
-        fold=low(fold),
-        fold_own=jnp.asarray(fold_own, F32),
-        gather=low(repeat.T),
-    )
+def positions_of(shape, dimension):
+    return lax.broadcasted_iota(jnp.int32, shape, dimension)
+
+
+def fill_tables(states, pick_ref, diagonal_ref, fold_ref=None, own_ref=None):
+    low, bits = states - 1, states.bit_length() - 1
+    rows, lanes = positions_of(pick_ref.shape, 0), positions_of(pick_ref.shape, 1)
+    pick_ref[...] = jnp.where(rows == (lanes & low), 1.0, 0.0).astype(LOW)
+    diagonal_ref[...] = jnp.where(rows == (lanes >> bits), 1.0, 0.0).astype(F32)
+    if fold_ref is not None:
+        rows, lanes = positions_of(fold_ref.shape, 0), positions_of(fold_ref.shape, 1)
+        same = (rows >> (LANES.bit_length() - 1)) == (lanes >> bits)
+        fold_ref[...] = jnp.where(same, 1.0, 0.0).astype(LOW)
+        rows, lanes = positions_of(own_ref.shape, 0), positions_of(own_ref.shape, 1)
+        own_ref[...] = jnp.where((rows & low) == (lanes & low), 1.0, 0.0).astype(F32)
 
 
 def dot(left, right):
     return jnp.dot(left, right, preferred_element_type=F32)
+
+
+def spread_table(sel_ref, keep_ref, rows, states):
+    start = sel_ref.shape[1] - 2 * states
+    turned = sel_ref[rows, start:].T
+    key, query = turned[:states], turned[states:]
+    keep = keep_ref[rows, :].T[:states]
+    return jnp.concatenate([key, keep * key * key, keep, query], axis=0)
 
 
 def spread_rows(table, row, states):
@@ -44,6 +50,10 @@
     return [wide[at : at + states] for at in range(0, 4 * states, states)]
 
 
+def expanded(value, pick_ref, diagonal_ref):
+    return (dot(value.astype(LOW), pick_ref[...]) * diagonal_ref[...]).astype(LOW)
+
+
 def groups(width):
     return [slice(at, at + LANES) for at in range(0, width, LANES)]
 
@@ -53,12 +63,12 @@
 
 
 def summary_kernel(
-    states, r_ref, act_ref, col_ref, out_ref, *scratch
+    states, r_ref, act_ref, sel_ref, keep_ref, out_ref, *scratch
 ):
     feed_refs = scratch[0:2]
     decay_ref, state_ref = scratch[2:]
     step = pl.program_id(1)
-    r_ref, act_ref, col_ref = r_ref.at[0], act_ref.at[0], col_ref.at[0]
+    r_ref, act_ref, sel_ref, keep_ref = r_ref.at[0], act_ref.at[0], sel_ref.at[0], keep_ref.at[0]
     count = r_ref.shape[0] // CH
     parts = groups(r_ref.shape[1])
 
@@ -74,7 +84,7 @@
     def process(index, which, decays, values):
         base = pl.multiple_of(index * CH, CH)
         rates = r_ref.at[pl.ds(base, CH)]
-        table, feeds = col_ref[pl.ds(base, CH), :].T[: 4 * states], feed_refs[which]
+        table, feeds = spread_table(sel_ref, keep_ref, pl.ds(base, CH), states), feed_refs[which]
         for row in range(CH):
             mine = slice(row * states, (row + 1) * states)
             key, square, keep, _ = spread_rows(table, row, states)
@@ -112,20 +122,22 @@
     states,
     r_ref,
     act_ref,
-    col_ref,
+    sel_ref,
+    keep_ref,
     gate_ref,
     skip_ref,
     in_ref,
-    pick_ref,
-    diagonal_ref,
     states_ref,
     mixed_ref,
     gated_ref,
     *scratch,
 ):
-    feed_refs, value_refs, (state_ref,) = scratch[0:2], scratch[2:4], scratch[4:]
+    feed_refs, value_refs = scratch[0:2], scratch[2:4]
+    state_ref, pick_ref, diagonal_ref = scratch[4:]
+    fill_tables(states, pick_ref, diagonal_ref)
     step = pl.program_id(1)
-    r_ref, act_ref, col_ref, gate_ref = r_ref.at[0], act_ref.at[0], col_ref.at[0], gate_ref.at[0]
+    r_ref, act_ref, sel_ref, gate_ref = r_ref.at[0], act_ref.at[0], sel_ref.at[0], gate_ref.at[0]
+    keep_ref = keep_ref.at[0]
     states_ref, mixed_ref, gated_ref = states_ref.at[0], mixed_ref.at[0], gated_ref.at[0]
     count = r_ref.shape[0] // CH
     parts = groups(r_ref.shape[1])
@@ -142,7 +154,7 @@
         base = pl.multiple_of(index * CH, CH)
         rates = r_ref.at[pl.ds(base, CH)]
         first = pl.multiple_of(index * (CH * states), CH * states)
-        table, feeds = col_ref[pl.ds(base, CH), :].T[: 4 * states], feed_refs[which]
+        table, feeds = spread_table(sel_ref, keep_ref, pl.ds(base, CH), states), feed_refs[which]
         for row in range(CH):
             mine = slice(row * states, (row + 1) * states)
             key, square, keep, _ = spread_rows(table, row, states)
@@ -155,7 +167,7 @@
 
     def finish(index, which):
         rows = pl.ds(pl.multiple_of(index * CH, CH), CH)
-        query = (dot(col_ref[rows, :].astype(LOW), pick_ref[2]) * diagonal_ref[...]).astype(LOW)
+        query = expanded(sel_ref[rows, sel_ref.shape[1] - states :], pick_ref, diagonal_ref)
         recurrent = dot(query, value_refs[which][...])
         mixed = recurrent + skip_ref[...] * act_ref[rows, :].astype(F32)
         gate = gate_ref[rows, :].astype(F32)
@@ -181,11 +193,11 @@
 
 
 def adjoint_kernel(
-    states, r_ref, gm_ref, col_ref, out_ref, *scratch
+    states, r_ref, gm_ref, sel_ref, keep_ref, out_ref, *scratch
 ):
     (carry_ref,) = scratch
     step = pl.program_id(1)
-    r_ref, gm_ref, col_ref = r_ref.at[0], gm_ref.at[0], col_ref.at[0]
+    r_ref, gm_ref, sel_ref, keep_ref = r_ref.at[0], gm_ref.at[0], sel_ref.at[0], keep_ref.at[0]
     count = r_ref.shape[0] // CH
     parts = groups(r_ref.shape[1])
 
@@ -198,7 +210,7 @@
         base = pl.multiple_of(index * CH, CH)
         rates = r_ref.at[pl.ds(base, CH)]
         grads = gm_ref.at[pl.ds(base, CH)]
-        table = col_ref[pl.ds(base, CH), :].T[: 4 * states]
+        table = spread_table(sel_ref, keep_ref, pl.ds(base, CH), states)
         for row in reversed(range(CH)):
             mine = slice(row * states, (row + 1) * states)
             _, square, keep, query = spread_rows(table, row, states)
@@ -228,17 +240,13 @@
     r_ref,
     act_ref,
     gm_ref,
-    col_ref,
+    sel_ref,
+    keep_ref,
     skip_ref,
     states_ref,
     before_ref,
     in_ref,
     carry_in_ref,
-    pick_ref,
-    diagonal_ref,
-    fold_ref,
-    fold_own_ref,
-    gather_ref,
     rate_ref,
     gact_ref,
     sums_ref,
@@ -247,10 +255,12 @@
     feed_refs, adjoint_refs, product_refs, part_refs = (
         scratch[2 * at : 2 * at + 2] for at in range(4)
     )
-    first_ref, carry_ref = scratch[8:]
+    first_ref, carry_ref, pick_ref, diagonal_ref, fold_ref, fold_own_ref = scratch[8:]
+    fill_tables(states, pick_ref, diagonal_ref, fold_ref, fold_own_ref)
     step = pl.program_id(1)
     last = pl.num_programs(1) - 1
-    r_ref, act_ref, gm_ref, col_ref = r_ref.at[0], act_ref.at[0], gm_ref.at[0], col_ref.at[0]
+    r_ref, act_ref, gm_ref, sel_ref = r_ref.at[0], act_ref.at[0], gm_ref.at[0], sel_ref.at[0]
+    keep_ref = keep_ref.at[0]
     states_ref, rate_ref, gact_ref, sums_ref = (
         states_ref.at[0],
         rate_ref.at[0],
@@ -281,7 +291,7 @@
         rates = r_ref.at[pl.ds(base, CH)]
         grads = gm_ref.at[pl.ds(base, CH)]
         first = pl.multiple_of(index * (CH * states), CH * states)
-        table, feeds = col_ref[pl.ds(base, CH), :].T[: 4 * states], feed_refs[which]
+        table, feeds = spread_table(sel_ref, keep_ref, pl.ds(base, CH), states), feed_refs[which]
         for row in reversed(range(CH)):
             mine = slice(row * states, (row + 1) * states)
             _, square, keep, query = spread_rows(table, row, states)
@@ -311,9 +321,11 @@
 
     def finish(index, which):
         rows = pl.ds(pl.multiple_of(index * CH, CH), CH)
-        cols = col_ref[rows, :].astype(LOW)
-        keys = (dot(cols, pick_ref[0]) * diagonal_ref[...]).astype(LOW)
-        squares = (dot(cols, pick_ref[1]) * diagonal_ref[...]).astype(LOW)
+        start = sel_ref.shape[1] - 2 * states
+        key = sel_ref[rows, start : start + states]
+        kept_key = keep_ref[rows, :states] * key
+        keys = expanded(key, pick_ref, diagonal_ref)
+        squares = expanded(kept_key * key, pick_ref, diagonal_ref)
         through_key = dot(keys, adjoint_refs[which][...])
         through_decay = dot(squares, product_refs[which][...])
         rate_ref[rows, :] = act_ref[rows, :].astype(F32) * through_key - through_decay
@@ -321,7 +333,12 @@
         folded = dot(part_refs[which][...], fold_ref[...]) * fold_own_ref[...]
         high = folded.astype(LOW)
         rest = (folded - high.astype(F32)).astype(LOW)
-        sums_ref[rows, :] = dot(gather_ref[...], high) + dot(gather_ref[...], rest)
+        gather = diagonal_ref[...].astype(LOW)
+        total = dot(gather, high) + dot(gather, rest)
+        grad_key = total[:, :states] - 2.0 * kept_key * total[:, states : 2 * states]
+        sums_ref[rows, :start] = jnp.zeros((CH, start), F32)
+        sums_ref[rows, start : start + states] = grad_key
+        sums_ref[rows, start + states :] = total[:, 2 * states : 3 * states]
 
     prepare(count - 1, 0)
 
@@ -368,33 +385,43 @@
     return pl.BlockSpec(value.shape, lambda m, b: (0,) * value.ndim)
 
 
-def run_summary(rate, act, cols, states):
+def table_shapes(states):
+    return [
+        pltpu.VMEM((states, CH * states), LOW),
+        pltpu.VMEM((CH, CH * states), F32),
+        pltpu.VMEM((3 * LANES, LANES), LOW),
+        pltpu.VMEM((CH * states, LANES), F32),
+    ]
+
+
+def run_summary(rate, act, sel, keep, states):
     batch, rows, channels, block, grid = plan(rate)
     part = pl.BlockSpec((1, block, channels), lambda m, b: (m, b, 0))
-    narrow = pl.BlockSpec((1, block, LANES), lambda m, b: (m, b, 0))
+    narrow = pl.BlockSpec((1, block, sel.shape[2]), lambda m, b: (m, b, 0))
+    marks = pl.BlockSpec((1, block, LANES), lambda m, b: (m, b, 0))
     return pl.pallas_call(
         functools.partial(summary_kernel, states),
         grid=grid,
-        in_specs=[part, part, narrow],
+        in_specs=[part, part, narrow, marks],
         out_specs=pl.BlockSpec((1, 2 * states, channels), lambda m, b: (m, 0, 0)),
         out_shape=jax.ShapeDtypeStruct((batch, 2 * states, channels), LOW),
         scratch_shapes=[pltpu.VMEM((CH, channels), F32)] * 2
         + [pltpu.VMEM((states, channels), F32)] * 2,
         compiler_params=params(),
         cost_estimate=cost(rate, states, 6),
-    )(rate, act, cols)
-
-
-def run_forward(rate, act, cols, gate, skip, incoming, states, table, limit):
+    )(rate, act, sel, keep)
+
+
+def run_forward(rate, act, sel, keep, gate, skip, incoming, states, limit):
     batch, rows, channels, block, grid = plan(rate)
     part = pl.BlockSpec((1, block, channels), lambda m, b: (m, b, 0))
-    narrow = pl.BlockSpec((1, block, LANES), lambda m, b: (m, b, 0))
+    narrow = pl.BlockSpec((1, block, sel.shape[2]), lambda m, b: (m, b, 0))
+    marks = pl.BlockSpec((1, block, LANES), lambda m, b: (m, b, 0))
     edge = pl.BlockSpec((1, states, channels), lambda m, b: (m, 0, 0))
-    consts = [table[name] for name in ("pick", "diagonal")]
     return pl.pallas_call(
         functools.partial(forward_kernel, states),
         grid=grid,
-        in_specs=[part, part, narrow, part, whole(skip), edge] + [whole(value) for value in consts],
+        in_specs=[part, part, narrow, marks, part, whole(skip), edge],
         out_specs=[
             pl.BlockSpec((1, block * states, channels), lambda m, b: (m, b, 0)),
             part,
@@ -407,39 +434,40 @@
         ],
         scratch_shapes=[pltpu.VMEM((CH, channels), F32)] * 2
         + [pltpu.VMEM((CH * states, channels), LOW)] * 2
-        + [pltpu.VMEM((states, channels), F32)],
+        + [pltpu.VMEM((states, channels), F32)]
+        + table_shapes(states)[:2],
         compiler_params=params(limit),
         cost_estimate=cost(rate, states, 8),
-    )(rate, act, cols, gate, skip, incoming, *consts)
-
-
-def run_adjoint(rate, grad_mixed, cols, states):
+    )(rate, act, sel, keep, gate, skip, incoming)
+
+
+def run_adjoint(rate, grad_mixed, sel, keep, states):
     batch, rows, channels, block, grid = plan(rate)
     final = rows // block - 1
     part = pl.BlockSpec((1, block, channels), lambda m, b: (m, final - b, 0))
-    narrow = pl.BlockSpec((1, block, LANES), lambda m, b: (m, final - b, 0))
+    narrow = pl.BlockSpec((1, block, sel.shape[2]), lambda m, b: (m, final - b, 0))
+    marks = pl.BlockSpec((1, block, LANES), lambda m, b: (m, final - b, 0))
     return pl.pallas_call(
         functools.partial(adjoint_kernel, states),
         grid=grid,
-        in_specs=[part, part, narrow],
+        in_specs=[part, part, narrow, marks],
         out_specs=pl.BlockSpec((1, states, channels), lambda m, b: (m, 0, 0)),
         out_shape=jax.ShapeDtypeStruct((batch, states, channels), LOW),
         scratch_shapes=[pltpu.VMEM((states, channels), F32)],
         compiler_params=params(),
         cost_estimate=cost(rate, states, 5),
-    )(rate, grad_mixed, cols)
+    )(rate, grad_mixed, sel, keep)
 
 
 def run_backward(
-    rate, act, grad_mixed, cols, skip, kept_states, incoming, carry, states, table, limit
+    rate, act, grad_mixed, sel, keep, skip, kept_states, incoming, carry, states, limit
 ):
     batch, rows, channels, block, grid = plan(rate)
     final = rows // block - 1
     part = pl.BlockSpec((1, block, channels), lambda m, b: (m, final - b, 0))
-    narrow = pl.BlockSpec((1, block, LANES), lambda m, b: (m, final - b, 0))
+    narrow = pl.BlockSpec((1, block, sel.shape[2]), lambda m, b: (m, final - b, 0))
+    marks = pl.BlockSpec((1, block, LANES), lambda m, b: (m, final - b, 0))
     edge = pl.BlockSpec((1, states, channels), lambda m, b: (m, 0, 0))
-    names = ("pick", "diagonal", "fold", "fold_own", "gather")
-    consts = [table[name] for name in names]
     return pl.pallas_call(
         functools.partial(backward_kernel, states),
         grid=grid,
@@ -448,6 +476,7 @@
             part,
             part,
             narrow,
+            marks,
             whole(skip),
             pl.BlockSpec((1, block * states, channels), lambda m, b: (m, final - b, 0)),
             pl.BlockSpec(
@@ -457,27 +486,21 @@
             edge,
             edge,
         ]
-        + [whole(value) for value in consts],
+       ,
         out_specs=[part, part, narrow],
         out_shape=[
             jax.ShapeDtypeStruct((batch, rows, channels), F32),
             jax.ShapeDtypeStruct((batch, rows, channels), F32),
-            jax.ShapeDtypeStruct((batch, rows, LANES), F32),
+            jax.ShapeDtypeStruct((batch, rows, sel.shape[2]), F32),
         ],
         scratch_shapes=[pltpu.VMEM((CH, channels), F32)] * 2
         + [pltpu.VMEM((CH * states, channels), LOW)] * 4
         + [pltpu.VMEM((CH * states, 3 * LANES), LOW)] * 2
-        + [pltpu.VMEM((states, channels), LOW), pltpu.VMEM((states, channels), F32)],
+        + [pltpu.VMEM((states, channels), LOW), pltpu.VMEM((states, channels), F32)]
+        + table_shapes(states),
         compiler_params=params(limit),
         cost_estimate=cost(rate, states, 16),
-    )(rate, act, grad_mixed, cols, skip, kept_states, kept_states, incoming, carry, *consts)
-
-
-def columns(key, query, keep):
-    kept = jnp.broadcast_to(keep[:, :, None], key.shape)
-    parts = [key, kept * key * key, kept, query]
-    blank = jnp.zeros(key.shape[:2] + (LANES - 4 * key.shape[2],), F32)
-    return jnp.concatenate(parts + [blank], axis=2)
+    )(rate, act, grad_mixed, sel, keep, skip, kept_states, kept_states, incoming, carry)
 
 
 def shifted(value, axis, steps):
@@ -544,7 +567,7 @@
     return parts[0] if beside is None else (parts[0], beside)
 
 
-def scan_exclusive(decay, value, direction, beside=None):
+def scan_exclusive(decay, value, direction, beside=()):
     count = lax.axis_size("seq")
     states = decay.shape[1]
     outer = None
@@ -553,8 +576,8 @@
         packed = jnp.concatenate([decay, value], axis=1).astype(LOW)
         final = 2 * step >= count
         got = shifted(packed[:, states:] if final else packed, "seq", direction * step)
-        if beside is not None and step == 1:
-            got, beside = lax.optimization_barrier((got, beside))
+        if step in beside:
+            got, beside[step] = lax.optimization_barrier((got, beside[step]))
         got = got.astype(F32)
         if final:
             got_value = got
@@ -569,7 +592,7 @@
             value = decay * got_value + value
             decay = decay * got_decay
         step *= 2
-    return outer[1] if beside is None else (outer[1], beside)
+    return outer[1]
 
 
 def after(value, *anchors):
@@ -791,7 +814,7 @@
     return value.reshape(-1, value.shape[-1])
 
 
-def forward_layer(hidden, weights, valid_mask, keep_mask, tap_masks, table, side, inverse_gain, limit):
+def forward_layer(hidden, weights, valid_mask, keep_lanes, tap_masks, side, inverse_gain, limit):
     gain, input_w, conv_weight, conv_bias, select_w, step_w, step_bias, skip, out_w = weights
     width = input_w.shape[0]
     scaled = (hidden * gain.astype(F32)).astype(LOW)
@@ -813,26 +836,25 @@
     states = (selection.shape[2] - rank) // 2
     low_rank = selection[:, :, :rank].astype(LOW)
     key_state = selection[:, :, rank : rank + states]
-    query_state = selection[:, :, rank + states :]
     biased = matmul(low_rank, step_w, "mrk,ki->mri") + step_bias
     step_size = jax.nn.softplus(biased)
     key_norm = jnp.sum(key_state * key_state, axis=2)
     rate = step_size / (1.0 + step_size * key_norm[:, :, None])
-    cols = columns(key_state, query_state, keep_mask)
     side_rows = None if side is None else tp_gather(after(side, rate))
-    summary = run_summary(rate, conv_act, cols, states).astype(F32)
+    summary = run_summary(rate, conv_act, selection, keep_lanes, states).astype(F32)
     decay_total, local_state = summary[:, :states], summary[:, states:]
     incoming = scan_exclusive(decay_total, local_state, 1)
     if side is not None:
         incoming, normed_other = lax.optimization_barrier((incoming, normed_other))
     skip_row = skip.astype(F32)[None]
     kept_states, mixed, gated = run_forward(
-        rate, conv_act, cols, gate_in, skip_row, incoming, states, table, limit
+        rate, conv_act, selection, keep_lanes, gate_in, skip_row, incoming, states, limit
     )
     if side is not None:
         gated, side_rows = lax.optimization_barrier((gated, side_rows))
-    branch = tp_scatter(matmul(gated, out_w, "mri,id->mrd").astype(LOW))
-    new_hidden = hidden + valid_mask[:, :, None] * branch
+    finish = lambda rows: hidden + valid_mask[:, :, None] * tp_scatter(
+        matmul(rows, out_w, "mri,id->mrd").astype(LOW)
+    )
     kept = dict(
         hidden=hidden,
         inverse_norm=inverse_norm,
@@ -844,8 +866,7 @@
         conv_out=conv_out,
         conv_act=conv_act,
         low_rank=low_rank,
-        key_state=key_state,
-        cols=cols,
+        selection=selection,
         biased=biased,
         key_norm=key_norm,
         rate=rate,
@@ -855,7 +876,7 @@
         mixed=mixed,
         gated=gated,
     )
-    return (new_hidden, kept, input_w, side_rows)
+    return (finish, kept, input_w, side_rows)
 
 
 def backward_layer(
@@ -864,23 +885,22 @@
     weights,
     kept,
     valid_mask,
-    keep_mask,
+    keep_lanes,
     tap_masks,
-    table,
     tasks,
     results,
     waiting,
     ready,
-    beside,
+    gated_other,
 ):
     gain, input_w, conv_weight, conv_bias, select_w, step_w, step_bias, skip, out_w = weights
-    hidden, inverse_norm, rate, cols = (
-        kept[name] for name in ("hidden", "inverse_norm", "rate", "cols")
-    )
-    conv_act, key_state = kept["conv_act"], kept["key_state"]
+    hidden, inverse_norm, rate, selection = (
+        kept[name] for name in ("hidden", "inverse_norm", "rate", "selection")
+    )
+    conv_act = kept["conv_act"]
     width = input_w.shape[0]
-    states = key_state.shape[2]
     rank = step_w.shape[0]
+    states = (selection.shape[2] - rank) // 2
     skip_row = skip.astype(F32)[None]
     first = waiting is not None
     if ready is None:
@@ -898,41 +918,53 @@
     act_float = conv_act.astype(F32)
     skip_grad = jnp.sum(grad_mixed * act_float, axis=(0, 1))
     normed = rows_of(kept["complete"])
-    local_carry = run_adjoint(rate, grad_mixed, cols, states)
-    carried = scan_exclusive(kept["decay_total"], local_carry.astype(F32), -1)
+    local_carry = run_adjoint(rate, grad_mixed, selection, keep_lanes, states)
     if first:
+        branch_other = swapped(own_half(rows_of(branch_rows), 1), "seq", 1)
+        inside = {1: pair_products([waiting]), 4: branch_other}
+        carried = scan_exclusive(kept["decay_total"], local_carry.astype(F32), -1, inside)
         carried, results[("early", at + 1)] = lax.optimization_barrier(
             (carried, results[("early", at + 1)])
         )
-        last = pair_products([waiting])
-        carried, last = lax.optimization_barrier((carried, last))
-        results[("conv", at + 1)] = line_scatter(last).astype(F32)
-    partial = plain_products(
-        [
-            (normed, rows_of(grad_gate)),
-            (rows_of(branch_rows), rows_of(kept["gated"])),
-        ]
-    )
-    carried, partial = lax.optimization_barrier((carried, partial))
-    results[("early", at)] = lax.psum_scatter(partial, "seq", scatter_dimension=0, tiled=True)[0]
+        results[("conv", at + 1)] = line_scatter(inside[1]).astype(F32)
+    else:
+        local_carry, gated_other = lax.optimization_barrier((local_carry, gated_other))
+        carried = scan_exclusive(kept["decay_total"], local_carry.astype(F32), -1)
+        partial = plain_products(
+            [
+                (normed, rows_of(grad_gate)),
+                (rows_of(branch_rows), rows_of(kept["gated"])),
+            ]
+        )
+        carried, partial = lax.optimization_barrier((carried, partial))
+        results[("early", at)] = lax.psum_scatter(
+            partial, "seq", scatter_dimension=0, tiled=True
+        )[0]
     grad_rate, grad_act, sums = run_backward(
         rate,
         conv_act,
         grad_mixed,
-        cols,
+        selection,
+        keep_lanes,
         skip_row,
         kept["kept_states"],
         kept["incoming"],
         carried,
         states,
-        table,
         2 * VMEM_BYTES,
     )
-    if not first:
+    if first:
+        gate_other = swapped(after(rows_of(grad_gate), carried), "seq", 1)
+        grad_rate, gate_other = lax.optimization_barrier((grad_rate, gate_other))
+        partial = pair_products(
+            [
+                (normed, kept["normed_other"], rows_of(grad_gate), gate_other),
+                (rows_of(branch_rows), inside.get(4, branch_other), rows_of(kept["gated"]), gated_other),
+            ]
+        )
+    else:
         normed_other = swapped(own_half(normed, 1), "seq", 1)
-        grad_rate, beside, normed_other = lax.optimization_barrier(
-            (grad_rate, beside, normed_other)
-        )
+        grad_rate, normed_other = lax.optimization_barrier((grad_rate, normed_other))
     denominator = 1.0 + jax.nn.softplus(kept["biased"]) * kept["key_norm"][:, :, None]
     grad_step = grad_rate / (denominator * denominator)
     grad_norm_key = -jnp.sum(grad_rate * rate * rate, axis=2)
@@ -940,17 +972,16 @@
     stepbias_grad = jnp.sum(grad_pre, axis=(0, 1))
     grad_pre_low = grad_pre.astype(LOW)
     step_grad = matmul(kept["low_rank"], grad_pre_low, "mrk,mri->ki")
-    grad_rank = matmul(grad_pre_low, step_w, "mri,ki->mrk")
-    through_feed, through_decay, grad_query = (
-        sums[:, :, at * states : (at + 1) * states] for at in range(3)
-    )
-    grad_key = (
-        through_feed
-        - 2.0 * keep_mask[:, :, None] * key_state * through_decay
-        + 2.0 * key_state * grad_norm_key[:, :, None]
-    )
-    grad_selection = tp_sum(jnp.concatenate([grad_rank, grad_key, grad_query], axis=2), LOW)
+    padded = jnp.pad(step_w, ((0, 2 * states), (0, 0)))
+    lanes = jnp.arange(selection.shape[2], dtype=jnp.int32)
+    is_key = ((lanes >= rank) & (lanes < rank + states)).astype(F32)
+    grad_selection = matmul(grad_pre_low, padded, "mri,ki->mrk") + sums
+    grad_selection = grad_selection + 2.0 * is_key * selection * grad_norm_key[:, :, None]
+    grad_selection = tp_sum(grad_selection, LOW)
     grad_selection = grad_selection.astype(LOW)
+    if first:
+        grad_selection, partial = lax.optimization_barrier((grad_selection, partial))
+        results[("early", at)] = line_scatter(partial)
     select_full = matmul(grad_selection, conv_act, "mrc,mri->ci")
     grad_act = grad_act + matmul(grad_selection, select_w, "mrc,ic->mri")
     grad_conv = grad_act * silu_slope(kept["conv_out"])
@@ -977,8 +1008,9 @@
     grad_projected = jnp.stack([grad_conv_in, grad_gate], axis=2)
     grad_normed = matmul(grad_projected, input_w, "bptg,htg->bph").astype(LOW)
     if first:
-        grad_normed = tp_scatter(grad_normed)
-        conv_other = jnp.concatenate(conv_other, axis=0)
+        grad_normed, conv_first = lax.optimization_barrier((grad_normed, conv_other[0]))
+        grad_normed, conv_last = tp_scatter(grad_normed, conv_other[1])
+        conv_other = jnp.concatenate([conv_first, conv_last], axis=0)
     else:
         grad_normed, conv_first = tp_scatter(grad_normed, conv_other[0])
         conv_other = (conv_first, conv_other[1])
@@ -1010,7 +1042,7 @@
         ],
         axis=0,
     )
-    return (grad_hidden, conv_piece, scattered, summed)
+    return (grad_hidden, conv_piece, gated_other, scattered, summed)
 
 
 def on_device(
@@ -1036,7 +1068,7 @@
         (positions[None, :] - back >= starts).astype(F32) for back in range(conv_weight.shape[1])
     ]
     layers = input_weight.shape[0]
-    table = tables((select_weight.shape[2] - step_weight.shape[1]) // 2)
+    keep_lanes = jnp.broadcast_to(keep_mask[:, :, None], keep_mask.shape + (LANES,))
     small = (conv_weight, conv_bias, select_weight, step_weight, step_bias, skip_gain, out_weight)
     shared = [tuple(member[at] for member in small) for at in range(layers)]
     hidden = tokens.astype(F32)
@@ -1046,38 +1078,39 @@
     saved, inputs, ready = [], [None] * layers, None
     for at in range(layers):
         own = after(input_weight[at], hidden)
-        hidden, kept, inputs[at], extra = forward_layer(
+        finish, kept, inputs[at], extra = forward_layer(
             hidden,
             (norm_gain[at], own) + shared[at],
             valid_mask,
-            keep_mask,
+            keep_lanes,
             tap_masks,
-            table,
             side if at == 0 else None,
             inverse_gains[at],
             2 * VMEM_BYTES,
         )
         ready = extra if at == 0 else ready
         saved.append(kept)
-    layer_out = hidden.astype(LOW)
+        if at + 1 < layers:
+            hidden = finish(kept["gated"])
     tasks, results, waiting = [], {}, None
+    passing = swapped(rows_of(saved[0]["gated"]), "seq", 1)
     scattered, summed = [None] * layers, [None] * layers
     for at in reversed(range(layers)):
-        grad, waiting, scattered[at], summed[at] = backward_layer(
+        grad, waiting, passing, scattered[at], summed[at] = backward_layer(
             at,
             grad,
             (norm_gain[at], inputs[at]) + shared[at],
             saved[at],
             valid_mask,
-            keep_mask,
+            keep_lanes,
             tap_masks,
-            table,
             tasks,
             results,
             waiting,
             ready if waiting is None else None,
-            hidden if waiting is None else None,
+            passing,
         )
+    layer_out = finish(after(saved[-1]["gated"], grad)).astype(LOW)
     piece = waiting
     add_task(tasks, ("conv", 0), lambda anchor: pair_products([piece]))
     rank = step_weight.shape[1]
@@ -1106,7 +1139,7 @@
         [jnp.stack([conv, gate], axis=1) for conv, gate in zip(blank, gate_parts)], axis=0
     )
     inweight_grad = lax.dynamic_update_slice(
-        after(inweight_grad, grad), conv_parts[0][None, :, None, :], (0, 0, 0, 0)
+        inweight_grad, conv_parts[0][None, :, None, :], (0, 0, 0, 0)
     )
     return (
         layer_out,

time: 747 us -> 712 us (0.953)
  matrix products: 67.8 us -> 52.8 us
  local copies, waits for them, and re-layouts: 78.1 us -> 63.5 us
  starting transfers between devices: 121 us -> 113 us
    ppermute x51 -> x54, waiting for transfers between devices: 134 us -> 107 us  [swapped(): lax.ppermute(value, axis, [(source, source ^ bit) for source in range(cou...]
    dot_general x20, matrix products: 67.8 us -> 52.8 us  [matmul(): return jnp.einsum(dims, left, right, preferred_element_type=F32)]
    ppermute x16, waiting for transfers between devices: 43.9 us -> 57.6 us  [shifted(): lax.ppermute(value, axis, [(source, source + steps) for source in range(l...]
    ppermute x3, waiting for transfers between devices: 17.9 us -> 31.7 us  [line_task(): right = lax.ppermute(ahead, 'seq', pairs(range(min(step, long - 1)), 1))]
    ppermute x3, starting transfers between devices: 24.5 us -> 11.1 us  [line_task(): right = lax.ppermute(ahead, 'seq', pairs(range(min(step, long - 1)), 1))]
    reduce_sum x0 -> x3, other arithmetic: none -> 12.1 us  [the longest x1 11.8 us: backward_layer(): jnp.sum(masked * extended[:, edge - back:edge - back + rows], axis=(0, 1))]
    pallas_call x2 -> x1, Pallas kernels: 21.5 us -> 10.7 us  [plain_products(): pl.pallas_call(functools.partial(plain_kernel, len(pieces)), grid=(parts...]
    pallas_call x2 -> x3, Pallas kernels: 12.2 us -> 21.3 us  [pair_products(): pl.pallas_call(functools.partial(pair_kernel, len(pieces)), grid_spec=plt...]
  transfers between devices with their start and end apart: 76 -> 79, of which waited for: 44 -> 40; matrix products, arithmetic and copies ran while one was open for 19% -> 18% of each run, Pallas kernels for 21% -> 25%
where the time goes in v3:
time: 712 us; the launch traced here: 702 us
  waiting for transfers between devices  197 us (28%)
  Pallas kernels  177 us (25%)
  starting transfers between devices  113 us (16%)
  other arithmetic  79.9 us (11%)
  local copies, waits for them, and re-layouts  63.5 us (9%)
  matrix products  52.8 us (7%)
  between operations  19.3 us (3%)
    ppermute x54, waiting for transfers between devices, swapped(): lax.ppermute(value, axis, [(source, source ^ bit) for source in range(cou...  107 us
    pallas_call x2, Pallas kernels, run_backward(): pl.pallas_call(functools.partial(backward_kernel, states), grid=grid, in_...  72.6 us
    ppermute x16, waiting for transfers between devices, shifted(): lax.ppermute(value, axis, [(source, source + steps) for source in range(l...  57.6 us
    dot_general x20, matrix products, matmul(): return jnp.einsum(dims, left, right, preferred_element_type=F32)  52.8 us
    ppermute x54, starting transfers between devices, swapped(): lax.ppermute(value, axis, [(source, source ^ bit) for source in range(cou...  50.7 us
    ppermute x16, starting transfers between devices, shifted(): lax.ppermute(value, axis, [(source, source + steps) for source in range(l...  47.8 us
    pallas_call x2, Pallas kernels, run_forward(): pl.pallas_call(functools.partial(forward_kernel, states), grid=grid, in_s...  33.6 us
    ppermute x3, waiting for transfers between devices, line_task(): right = lax.ppermute(ahead, 'seq', pairs(range(min(step, long - 1)), 1))  31.7 us
  transfers between devices with their start and end apart: 79, of which 40 were waited for; matrix products, arithmetic and copies ran while one was open for 18% of the time, Pallas kernels for 25%

profile of v3, /device:TPU:0, one launch (start us, length us, event | category | flops | bytes accessed | tf_op | source)
XLA Modules:
  0.0 701.9 jit_solution(16931513676670327816)
XLA Ops:
  14.6 14.2 %slice_bitcast_fusion = (bf16[2048,2,1024]{2,1,0:T(2,128)(2,1)}, bf16[2048,2,1024]{2,1,0:T(2,128)(2,1)}) fusion(bf16[2,2048,2,1024]{3,2,1,0:T(2,128)(2,1)} %param.15), kind=kLoop, calls=%fused_computation | loop fusion | bytes 33554432 | tf_op jit(solution)/shard_map/squeeze | solution.py:1080
  37.0 4.9 multiply_convert_fusion.1
  43.6 3.8 collective-permute-start.6
  58.4 4.5 collective-permute-done.8
  65.4 10.2 %shard_map.220 = bf16[2,32,1024]{2,1,0:T(8,128)(2,1)S(1)} custom-call(f32[2,256,1024]{2,1,0:T(8,128)S(1)} %fusion.71.r_ref, bf16[2,256,1024]{2,1,0:T(8,128)(2,1)S(1)} %get-tuple-element.238.act_ref, f32[2,256,160]{2,1,0:T(8,128)S(1)} %convert_add_fusion.21.sel_ref, f32[2,256,128]{2,1,0:T(8,128)S(1)} %broadcast_in_dim.26.keep_ref), custom_call_target="tpu_custom_call" | custom-call | flops 50331648 | bytes 16777216 | tf_op jit(solution)/shard_map/pallas_call | solution.py:402
  75.7 4.3 collective-permute-start.9
  82.6 6.2 collective-permute-start.10
  91.4 5.8 collective-permute-start.11
  102.2 16.7 %shard_map.221 = (bf16[2,4096,1024]{2,1,0:T(8,128)(2,1)}, bf16[2,256,1024]{2,1,0:T(8,128)(2,1)S(1)}, bf16[2,256,1024]{2,1,0:T(8,128)(2,1)S(1)}) custom-call(f32[2,256,1024]{2,1,0:T(8,128)S(1)} %fusion.71.r_ref, bf16[2,256,1024]{2,1,0:T(8,128)(2,1)S(1)} %get-tuple-element.238.act_ref, f32[2,256,160]{2,1,0:T(8,128)S(1)} %convert_add_fusion.21.sel_ref, ...), custom_call_target="tpu_custom_call" | custom-call | flops 67108864 | bytes 16777216 | tf_op jit(solution)/shard_map/pallas_call | solution.py:421
  130.0 12.7 %collective-permute-done.21 = bf16[2,256,512]{2,1,0:T(8,128)(2,1)S(1)} collective-permute-done((bf16[2,256,512]{2,1,0:T(8,128)(2,1)S(1)}, bf16[2,256,512]{2,1,0:T(8,128)(2,1)S(1)}, u32[]{:S(2)}, u32[]{:S(2)}) %collective-permute-start.21) | collective-permute-done | bytes 524320 | tf_op jit(solution)/shard_map/ppermute | solution.py:514
  145.9 11.9 %collective-permute-done.22 = bf16[2,256,512]{2,1,0:T(8,128)(2,1)S(1)} collective-permute-done((bf16[2,256,512]{2,1,0:T(8,128)(2,1)S(1)}, bf16[2,256,512]{2,1,0:T(8,128)(2,1)S(1)}, u32[]{:S(2)}, u32[]{:S(2)}) %collective-permute-start.22) | collective-permute-done | bytes 524320 | tf_op jit(solution)/shard_map/ppermute | solution.py:514
  161.1 4.9 multiply_convert_fusion
  171.4 7.5 %multiply_reduce_fusion.2 = (f32[1024]{0:T(1024)}, f32[2,256,1024]{2,1,0:T(8,128)}, bf16[2,256,1024]{2,1,0:T(8,128)(2,1)S(1)}, f32[2,256,1024]{2,1,0:T(8,128)}, f32[2,256,1024]{2,1,0:T(8,128)}) fusion(bf16[2,256,2,1024]{3,1,0,2:T(8,128)(2,1)S(1)} %multiply_convert_fusion, f32[2,256]{1,0:T(2,128)S(1)} %copy-done.103, ...), kind=kOutput, calls=%fused_computation.92 | convolution fusion | flops 2161114112 | bytes 23101440 | tf_op jit(solution)/shard_map/mrd,id->mri/dot_general | solution.py:799
  190.6 4.3 collective-permute-done.27
  199.3 9.0 %shard_map.224 = bf16[2,16,1024]{2,1,0:T(8,128)(2,1)S(1)} custom-call(f32[2,256,1024]{2,1,0:T(8,128)S(1)} %fusion.70.r_ref, f32[2,256,1024]{2,1,0:T(8,128)S(1)} %copy-done.14, f32[2,256,160]{2,1,0:T(8,128)S(1)} %convert_add_fusion.19.sel_ref, f32[2,256,128]{2,1,0:T(8,128)S(1)} %broadcast_in_dim.26.keep_ref), custom_call_target="tpu_custom_call" | custom-call | flops 41943040 | bytes 16777216 | tf_op jit(solution)/shard_map/pallas_call | solution.py:450
  208.3 10.2 %shard_map.222 = bf16[2,32,1024]{2,1,0:T(8,128)(2,1)S(1)} custom-call(f32[2,256,1024]{2,1,0:T(8,128)S(1)} %fusion.70.r_ref, bf16[2,256,1024]{2,1,0:T(8,128)(2,1)S(1)} %copy-done.9, f32[2,256,160]{2,1,0:T(8,128)S(1)} %convert_add_fusion.19.sel_ref, f32[2,256,128]{2,1,0:T(8,128)S(1)} %broadcast_in_dim.26.keep_ref), custom_call_target="tpu_custom_call" | custom-call | flops 50331648 | bytes 16777216 | tf_op jit(solution)/shard_map/pallas_call | solution.py:402
  219.9 5.4 collective-permute-start.28
  230.4 4.8 collective-permute-start.29
  237.7 4.4 collective-permute-done.33
  248.4 16.9 %shard_map.223 = (bf16[2,4096,1024]{2,1,0:T(8,128)(2,1)}, bf16[2,256,1024]{2,1,0:T(8,128)(2,1)S(1)}, bf16[2,256,1024]{2,1,0:T(8,128)(2,1)S(1)}) custom-call(f32[2,256,1024]{2,1,0:T(8,128)S(1)} %fusion.70.r_ref, bf16[2,256,1024]{2,1,0:T(8,128)(2,1)S(1)} %copy-done.9, f32[2,256,160]{2,1,0:T(8,128)S(1)} %convert_add_fusion.19.sel_ref, ...), custom_call_target="tpu_custom_call" | custom-call | flops 67108864 | bytes 16777216 | tf_op jit(solution)/shard_map/pallas_call | solution.py:421
  267.3 10.7 %shard_map.225 = bf16[8,256,2048]{2,1,0:T(8,128)(2,1)} custom-call(bf16[512,2048]{1,0:T(8,128)(2,1)} %bitcast.293, bf16[512,1024]{1,0:T(8,128)(2,1)} %bitcast.306, bf16[512,2048]{1,0:T(8,128)(2,1)} %bitcast.314, bf16[512,1024]{1,0:T(8,128)(2,1)} %bitcast.290), custom_call_target="tpu_custom_call" | custom-call | flops 4294967296 | bytes 4194304 | tf_op jit(solution)/shard_map/pallas_call | solution.py:697
  284.4 36.3 %shard_map.226 = (f32[2,256,1024]{2,1,0:T(8,128)S(1)}, f32[2,256,1024]{2,1,0:T(8,128)S(1)}, f32[2,256,160]{2,1,0:T(8,128)S(1)}) custom-call(f32[2,256,1024]{2,1,0:T(8,128)S(1)} %copy-done.1, bf16[2,256,1024]{2,1,0:T(8,128)(2,1)S(1)} %copy-done.10, f32[2,256,1024]{2,1,0:T(8,128)S(1)} %copy-done.15, f32[2,256,160]{2,1,0:T(8,128)S(1)} %copy-done.7, ...), custom_call_target="tpu_custom_call" | custom-call | flops 134217728 | bytes 16777216 | tf_op jit(solution)/shard_map/pallas_call | solution.py:471
  327.9 6.8 collective-permute-done.37
  345.3 5.2 bitcast_convert_fusion.1
  360.6 8.5 %collective-permute-done.44 = f32[2,256]{1,0:T(2,128)S(1)} collective-permute-done((f32[2,256]{1,0:T(2,128)S(1)}, f32[2,256]{1,0:T(2,128)S(1)}, u32[]{:S(2)}, u32[]{:S(2)}) %collective-permute-start.44) | collective-permute-done | bytes 2080 | tf_op jit(solution)/shard_map/ppermute | solution.py:514
  369.2 7.6 %collective-permute-done.42 = bf16[256,1024]{1,0:T(8,128)(2,1)S(1)} collective-permute-done((bf16[256,1024]{1,0:T(8,128)(2,1)S(1)}, bf16[256,1024]{1,0:T(8,128)(2,1)S(1)}, u32[]{:S(2)}, u32[]{:S(2)}) %collective-permute-start.42) | collective-permute-done | bytes 524320 | tf_op jit(solution)/shard_map/ppermute | solution.py:514
  380.0 13.6 %collective-permute-done.46 = bf16[256,1024]{1,0:T(8,128)(2,1)S(1)} collective-permute-done((bf16[256,1024]{1,0:T(8,128)(2,1)S(1)}, bf16[256,1024]{1,0:T(8,128)(2,1)S(1)}, u32[]{:S(2)}, u32[]{:S(2)}) %collective-permute-start.46) | collective-permute-done | bytes 524320 | tf_op jit(solution)/shard_map/ppermute | solution.py:514
  400.2 5.0 multiply_reduce_fusion.7
  405.2 9.3 %shard_map.227 = bf16[2,16,1024]{2,1,0:T(8,128)(2,1)S(1)} custom-call(f32[2,256,1024]{2,1,0:T(8,128)S(1)} %fusion.71.r_ref, f32[2,256,1024]{2,1,0:T(8,128)S(1)} %get-tuple-element.224.gm_ref, f32[2,256,160]{2,1,0:T(8,128)S(1)} %copy-done.3, f32[2,256,128]{2,1,0:T(8,128)S(1)} %broadcast_in_dim.26.keep_ref), custom_call_target="tpu_custom_call" | custom-call | flops 41943040 | bytes 16777216 | tf_op jit(solution)/shard_map/pallas_call | solution.py:450
  416.5 6.1 shard_map.228
  422.5 15.4 %collective-permute-done.49 = bf16[2,32,1024]{2,1,0:T(8,128)(2,1)} collective-permute-done((bf16[2,32,1024]{2,1,0:T(8,128)(2,1)}, bf16[2,32,1024]{2,1,0:T(8,128)(2,1)}, u32[]{:S(2)}, u32[]{:S(2)}) %collective-permute-start.49) | collective-permute-done | bytes 131104 | tf_op jit(solution)/shard_map/ppermute | solution.py:509
  441.1 14.9 %collective-permute-done.50 = bf16[2,32,1024]{2,1,0:T(8,128)(2,1)S(1)} collective-permute-done((bf16[2,32,1024]{2,1,0:T(8,128)(2,1)S(1)}, bf16[2,32,1024]{2,1,0:T(8,128)(2,1)S(1)}, u32[]{:S(2)}, u32[]{:S(2)}) %collective-permute-start.50) | collective-permute-done | bytes 131104 | tf_op jit(solution)/shard_map/ppermute | solution.py:509
  458.5 7.0 collective-permute-done.51
  476.0 36.3 %shard_map.229 = (f32[2,256,1024]{2,1,0:T(8,128)S(1)}, f32[2,256,1024]{2,1,0:T(8,128)S(1)}, f32[2,256,160]{2,1,0:T(8,128)S(1)}) custom-call(f32[2,256,1024]{2,1,0:T(8,128)S(1)} %fusion.71.r_ref, bf16[2,256,1024]{2,1,0:T(8,128)(2,1)S(1)} %get-tuple-element.238.act_ref, f32[2,256,1024]{2,1,0:T(8,128)S(1)} %copy-done.13, f32[2,256,160]{2,1,0:T(8,128)S(1)} %copy-done.4, ...), custom_call_target="tpu_custom_call" | custom-call | flops 134217728 | bytes 16777216 | tf_op jit(solution)/shard_map/pallas_call | solution.py:471
  520.4 9.1 %shard_map.230 = bf16[4,256,2048]{2,1,0:T(8,128)(2,1)} custom-call(s32[1]{0:T(128)} %bitcast.51.side_ref, bf16[512,2048]{1,0:T(8,128)(2,1)} %bitcast.318, bf16[512,1024]{1,0:T(8,128)(2,1)} %pad_maximum_fusion.5.refs_1_, bf16[512,1024]{1,0:T(8,128)(2,1)} %bitcast.332, bf16[512,1024]{1,0:T(8,128)(2,1)} %collective-permute-done.53.refs_3_, ...), custom_call_target="tpu_custom_call" | custom-call | flops 4294967296 | bytes 4194304 | tf_op jit(solution)/shard_map/pallas_call | solution.py:673
  532.4 11.8 %multiply_reduce_fusion.8 = (f32[1024]{0:T(1024)}, f32[1024]{0:T(1024)}, f32[1024]{0:T(1024)}, f32[1024]{0:T(1024)}, f32[1024]{0:T(1024)}, /*index=5*/f32[1024]{...) fusion(f32[2,259,1024]{2,1,0:T(8,128)} %copy-done.32, ...), kind=kLoop, calls=%fused_computation.98 | loop fusion | flops 18339840 | bytes 27312128 | tf_op jit(solution)/shard_map/reduce_sum | solution.py:996
  557.0 9.2 %bitcast_convert_fusion = bf16[2,256,2048]{2,1,0:T(8,128)(2,1)S(1)} fusion(bf16[2048,2,1024,1]{2,1,0,3:T(2,128)(2,1)} %bitcast.298, bf16[2,256,1,1024]{3,1,0,2:T(8,128)(2,1)S(1)} %bitcast.333, bf16[2,256,1,1024]{3,1,0,2:T(8,128)(2,1)S(1)} %bitcast.309), kind=kOutput, calls=%fused_computation.10 | convolution fusion | flops 4297064448 | bytes 12582912 | tf_op jit(solution)/shard_map/bptg,htg->bph/dot_general | solution.py:799
  578.3 11.1 %collective-permute-done.63 = f32[2,256]{1,0:T(2,128)S(1)} collective-permute-done((f32[2,256]{1,0:T(2,128)S(1)}, f32[2,256]{1,0:T(2,128)S(1)}, u32[]{:S(2)}, u32[]{:S(2)}) %collective-permute-start.63) | collective-permute-done | bytes 2080 | tf_op jit(solution)/shard_map/ppermute | solution.py:514
  598.3 6.1 shard_map.231
  609.0 4.5 fusion.27
  614.4 16.9 %collective-permute-done.68 = bf16[256,1024]{1,0:T(8,128)(2,1)S(1)} collective-permute-done((bf16[256,1024]{1,0:T(8,128)(2,1)S(1)}, bf16[256,1024]{1,0:T(8,128)(2,1)S(1)}, u32[]{:S(2)}, u32[]{:S(2)}) %collective-permute-start.68) | collective-permute-done | bytes 524320 | tf_op jit(solution)/shard_map/ppermute | solution.py:732
  631.7 4.4 collective-permute-start.71
  639.3 9.1 %collective-permute-done.71 = bf16[256,1024]{1,0:T(8,128)(2,1)S(1)} collective-permute-done((bf16[256,1024]{1,0:T(8,128)(2,1)S(1)}, bf16[256,1024]{1,0:T(8,128)(2,1)S(1)}, u32[]{:S(2)}, u32[]{:S(2)}) %collective-permute-start.71) | collective-permute-done | bytes 524320 | tf_op jit(solution)/shard_map/ppermute | solution.py:732
  648.8 4.4 collective-permute-start.74
  657.8 3.9 collective-permute-start.73
  663.1 5.7 collective-permute-done.74
  669.1 9.2 %collective-permute-done.73 = bf16[144,1024]{1,0:T(8,128)(2,1)S(1)} collective-permute-done((bf16[144,1024]{1,0:T(8,128)(2,1)S(1)}, bf16[144,1024]{1,0:T(8,128)(2,1)S(1)}, u32[]{:S(2)}, u32[]{:S(2)}) %collective-permute-start.73) | collective-permute-done | bytes 294944 | tf_op jit(solution)/shard_map/ppermute | solution.py:514
  686.8 5.2 copy.141
  (705 shorter events, 226.6 us)
Async XLA Ops:
  8.0 458.1 %reduce-scatter.4.cloned.1.call-start = ((), (), s32[]{:S(2)}) async-start(), calls=%async_computation.3 | async-start | bytes 9437184 | tf_op jit(solution)/shard_map/reduce_scatter | solution.py:940
  8.7 21.3 %collective-permute-start.5 = (f32[2,512]{1,0:T(2,128)S(1)}, f32[2,512]{1,0:T(2,128)S(1)}, u32[]{:S(2)}, u32[]{:S(2)}) collective-permute-start(f32[2,512]{1,0:T(2,128)S(1)} %convert_element_type.575), channel_id=1, source_target_pairs={{0,1},{1,0},{2,3},{3,2},{4,5},{5,4},{6,7},{7,6},{8,9},{9,8},{10,11... | collective-permute-start | bytes 12296 | tf_op jit(solution)/shard_map/ppermute | solution.py:514
  9.2 20.4 %collective-permute-start.3 = (f32[2,512]{1,0:T(2,128)S(1)}, f32[2,512]{1,0:T(2,128)S(1)}, u32[]{:S(2)}, u32[]{:S(2)}) collective-permute-start(f32[2,512]{1,0:T(2,128)S(1)} %convert_element_type.575), channel_id=1, source_target_pairs={{0,2},{1,3},{2,0},{3,1},{4,6},{5,7},{6,4},{7,5},{8,10},{9,11},{10,... | collective-permute-start | bytes 12296 | tf_op jit(solution)/shard_map/ppermute | solution.py:514
  14.2 16.7 %collective-permute-start = (bf16[2,256,512]{2,1,0:T(8,128)(2,1)S(1)}, bf16[2,256,512]{2,1,0:T(8,128)(2,1)S(1)}, u32[]{:S(2)}, u32[]{:S(2)}) collective-permute-start(bf16[2,256,512]{2,1,0:T(8,128)(2,1)S(1)} %multiply_convert_fusion.6), channel_id=1, source_target_pairs={{0,2},{1,3},{2,0},{3,1},{4,6},{5,7},{6,4},{7,5},{8,10},{9,11},{10,... | collective-permute-start | bytes 1572872 | tf_op jit(solution)/shard_map/ppermute | solution.py:514
  14.3 17.6 %collective-permute-start.2 = (bf16[2,256,512]{2,1,0:T(8,128)(2,1)S(1)}, bf16[2,256,512]{2,1,0:T(8,128)(2,1)S(1)}, u32[]{:S(2)}, u32[]{:S(2)}) collective-permute-start(bf16[2,256,512]{2,1,0:T(8,128)(2,1)S(1)} %multiply_convert_fusion.6), channel_id=1, source_target_pairs={{0,1},{1,0},{2,3},{3,2},{4,5},{5,4},{6,7},{7,6},{8,9},{9,8},{10,11... | collective-permute-start | bytes 1572872 | tf_op jit(solution)/shard_map/ppermute | solution.py:514
  56.1 24.0 %collective-permute-start.12 = (bf16[512,256]{1,0:T(8,128)(2,1)}, bf16[512,256]{1,0:T(8,128)(2,1)S(1)}, u32[]{:S(2)}, u32[]{:S(2)}) collective-permute-start(bf16[512,256]{1,0:T(8,128)(2,1)} %bitcast.17), channel_id=1, source_target_pairs={{0,4},{4,0},{8,12},{12,8},{16,20},{20,16},{24,28},{28,24},{1,5},{5... | collective-permute-start | bytes 786440 | tf_op jit(solution)/shard_map/ppermute | solution.py:514
  80.1 10.6 %collective-permute-start.13 = (bf16[512,256]{1,0:T(8,128)(2,1)S(1)}, bf16[512,256]{1,0:T(8,128)(2,1)S(1)}, u32[]{:S(2)}, u32[]{:S(2)}) collective-permute-start(bf16[512,256]{1,0:T(8,128)(2,1)S(1)} %collective-permute-done.12), channel_id=1, source_target_pairs={{0,2},{1,3},{2,0},{3,1},{4,6},{5,7},{6,4},{7,5},{8,10},{9,11},{10,... | collective-permute-start | bytes 786440 | tf_op jit(solution)/shard_map/ppermute | solution.py:514
  89.1 11.8 %collective-permute-start.16 = (bf16[2,256,512]{2,1,0:T(8,128)(2,1)S(1)}, bf16[2,256,512]{2,1,0:T(8,128)(2,1)S(1)}, u32[]{:S(2)}, u32[]{:S(2)}) collective-permute-start(bf16[2,256,512]{2,1,0:T(8,128)(2,1)S(1)} %fusion.72), channel_id=1, source_target_pairs={{0,2},{1,3},{2,0},{3,1},{4,6},{5,7},{6,4},{7,5},{8,10},{9,11},{10,... | collective-permute-start | bytes 1572872 | tf_op jit(solution)/shard_map/ppermute | solution.py:514
  90.7 10.3 %collective-permute-start.15 = (bf16[512,256]{1,0:T(8,128)(2,1)S(1)}, bf16[512,256]{1,0:T(8,128)(2,1)S(1)}, u32[]{:S(2)}, u32[]{:S(2)}) collective-permute-start(bf16[512,256]{1,0:T(8,128)(2,1)S(1)} %collective-permute-done.12), channel_id=1, source_target_pairs={{0,1},{1,0},{2,3},{3,2},{4,5},{5,4},{6,7},{7,6},{8,9},{9,8},{10,11... | collective-permute-start | bytes 786440 | tf_op jit(solution)/shard_map/ppermute | solution.py:514
  90.7 10.3 %collective-permute-start.14 = (bf16[512,256]{1,0:T(8,128)(2,1)S(1)}, bf16[512,256]{1,0:T(8,128)(2,1)S(1)}, u32[]{:S(2)}, u32[]{:S(2)}) collective-permute-start(bf16[512,256]{1,0:T(8,128)(2,1)S(1)} %collective-permute-done.13), channel_id=1, source_target_pairs={{0,1},{1,0},{2,3},{3,2},{4,5},{5,4},{6,7},{7,6},{8,9},{9,8},{10,11... | collective-permute-start | bytes 786440 | tf_op jit(solution)/shard_map/ppermute | solution.py:514
  97.3 21.6 %collective-permute-start.18 = (bf16[2,256,512]{2,1,0:T(8,128)(2,1)S(1)}, bf16[2,256,512]{2,1,0:T(8,128)(2,1)S(1)}, u32[]{:S(2)}, u32[]{:S(2)}) collective-permute-start(bf16[2,256,512]{2,1,0:T(8,128)(2,1)S(1)} %fusion.72), channel_id=1, source_target_pairs={{0,1},{1,0},{2,3},{3,2},{4,5},{5,4},{6,7},{7,6},{8,9},{9,8},{10,11... | collective-permute-start | bytes 1572872 | tf_op jit(solution)/shard_map/ppermute | solution.py:514
  100.8 18.1 %collective-permute-start.17 = (bf16[2,256,512]{2,1,0:T(8,128)(2,1)S(1)}, bf16[2,256,512]{2,1,0:T(8,128)(2,1)S(1)}, u32[]{:S(2)}, u32[]{:S(2)}) collective-permute-start(bf16[2,256,512]{2,1,0:T(8,128)(2,1)S(1)} %collective-permute-done.16), channel_id=1, source_target_pairs={{0,1},{1,0},{2,3},{3,2},{4,5},{5,4},{6,7},{7,6},{8,9},{9,8},{10,11... | collective-permute-start | bytes 1572872 | tf_op jit(solution)/shard_map/ppermute | solution.py:514
  128.4 14.3 %collective-permute-start.21 = (bf16[2,256,512]{2,1,0:T(8,128)(2,1)S(1)}, bf16[2,256,512]{2,1,0:T(8,128)(2,1)S(1)}, u32[]{:S(2)}, u32[]{:S(2)}) collective-permute-start(bf16[2,256,512]{2,1,0:T(8,128)(2,1)S(1)} %select_convert_fusion.4), channel_id=1, source_target_pairs={{0,2},{1,3},{2,0},{3,1},{4,6},{5,7},{6,4},{7,5},{8,10},{9,11},{10,... | collective-permute-start | bytes 1572872 | tf_op jit(solution)/shard_map/ppermute | solution.py:514
  144.3 13.4 %collective-permute-start.22 = (bf16[2,256,512]{2,1,0:T(8,128)(2,1)S(1)}, bf16[2,256,512]{2,1,0:T(8,128)(2,1)S(1)}, u32[]{:S(2)}, u32[]{:S(2)}) collective-permute-start(bf16[2,256,512]{2,1,0:T(8,128)(2,1)S(1)} %get-tuple-element.236), channel_id=1, source_target_pairs={{0,2},{1,3},{2,0},{3,1},{4,6},{5,7},{6,4},{7,5},{8,10},{9,11},{10,... | collective-permute-start | bytes 1572872 | tf_op jit(solution)/shard_map/ppermute | solution.py:514
  145.8 11.9 %collective-permute-start.24 = (bf16[2,256,512]{2,1,0:T(8,128)(2,1)S(1)}, bf16[2,256,512]{2,1,0:T(8,128)(2,1)S(1)}, u32[]{:S(2)}, u32[]{:S(2)}) collective-permute-start(bf16[2,256,512]{2,1,0:T(8,128)(2,1)S(1)} %get-tuple-element.236), channel_id=1, source_target_pairs={{0,1},{1,0},{2,3},{3,2},{4,5},{5,4},{6,7},{7,6},{8,9},{9,8},{10,11... | collective-permute-start | bytes 1572872 | tf_op jit(solution)/shard_map/ppermute | solution.py:514
  187.8 30.8 %collective-permute-start.31 = (bf16[512,1024]{1,0:T(8,128)(2,1)}, bf16[512,1024]{1,0:T(8,128)(2,1)S(1)}, u32[]{:S(2)}, u32[]{:S(2)}) collective-permute-start(bf16[512,1024]{1,0:T(8,128)(2,1)} %bitcast.288), channel_id=1, source_target_pairs={{0,4},{4,0},{8,12},{12,8},{16,20},{20,16},{24,28},{28,24},{1,5},{5... | collective-permute-start | bytes 3145736 | tf_op jit(solution)/shard_map/ppermute | solution.py:514
  219.9 10.3 %collective-permute-start.28 = (bf16[2,32,1024]{2,1,0:T(8,128)(2,1)S(1)}, bf16[2,32,1024]{2,1,0:T(8,128)(2,1)S(1)}, u32[]{:S(2)}, u32[]{:S(2)}) collective-permute-start(bf16[2,32,1024]{2,1,0:T(8,128)(2,1)S(1)} %shard_map.222), channel_id=1, source_target_pairs={{0,4},{4,8},{8,12},{12,16},{16,20},{20,24},{24,28},{1,5},{5,9},{9,... | collective-permute-start | bytes 393224 | tf_op jit(solution)/shard_map/ppermute | solution.py:509
  246.3 31.7 %collective-permute-start.34 = (bf16[2,16,1024]{2,1,0:T(8,128)(2,1)}, bf16[2,16,1024]{2,1,0:T(8,128)(2,1)}, u32[]{:S(2)}, u32[]{:S(2)}) collective-permute-start(bf16[2,16,1024]{2,1,0:T(8,128)(2,1)} %get-tuple-element.323), channel_id=1, source_target_pairs={{16,0},{20,4},{24,8},{28,12},{17,1},{21,5},{25,9},{29,13},{18,2},{... | collective-permute-start | bytes 196616 | tf_op jit(solution)/shard_map/ppermute | solution.py:509
  279.9 289.3 %reduce-scatter.8.cloned.1.call-start = ((), (), s32[]{:S(2)}) async-start(), calls=%async_computation.5 | async-start | bytes 2621440 | tf_op jit(solution)/shard_map/reduce_scatter | solution.py:710
  281.9 38.8 %collective-permute-start.35 = (bf16[512,1024]{1,0:T(8,128)(2,1)S(1)}, bf16[512,1024]{1,0:T(8,128)(2,1)S(1)}, u32[]{:S(2)}, u32[]{:S(2)}) collective-permute-start(bf16[512,1024]{1,0:T(8,128)(2,1)S(1)} %pad_maximum_fusion.6), channel_id=1, source_target_pairs={{0,4},{4,0},{8,12},{12,8},{16,20},{20,16},{24,28},{28,24},{1,5},{5... | collective-permute-start | bytes 3145736 | tf_op jit(solution)/shard_map/ppermute | solution.py:514
  351.3 25.5 %collective-permute-start.42 = (bf16[256,1024]{1,0:T(8,128)(2,1)S(1)}, bf16[256,1024]{1,0:T(8,128)(2,1)S(1)}, u32[]{:S(2)}, u32[]{:S(2)}) collective-permute-start(bf16[256,1024]{1,0:T(8,128)(2,1)S(1)} %get-tuple-element.303), channel_id=1, source_target_pairs={{0,4},{4,0},{8,12},{12,8},{16,20},{20,16},{24,28},{28,24},{1,5},{5... | collective-permute-start | bytes 1572872 | tf_op jit(solution)/shard_map/ppermute | solution.py:514
  355.4 21.4 %collective-permute-start.41 = (bf16[2,256,512]{2,1,0:T(8,128)(2,1)S(1)}, bf16[2,256,512]{2,1,0:T(8,128)(2,1)S(1)}, u32[]{:S(2)}, u32[]{:S(2)}) collective-permute-start(bf16[2,256,512]{2,1,0:T(8,128)(2,1)S(1)} %select_convert_fusion.3), channel_id=1, source_target_pairs={{0,2},{1,3},{2,0},{3,1},{4,6},{5,7},{6,4},{7,5},{8,10},{9,11},{10,... | collective-permute-start | bytes 1572872 | tf_op jit(solution)/shard_map/ppermute | solution.py:514
  358.1 11.0 %collective-permute-start.44 = (f32[2,256]{1,0:T(2,128)S(1)}, f32[2,256]{1,0:T(2,128)S(1)}, u32[]{:S(2)}, u32[]{:S(2)}) collective-permute-start(f32[2,256]{1,0:T(2,128)S(1)} %add.582), channel_id=1, source_target_pairs={{0,2},{1,3},{2,0},{3,1},{4,6},{5,7},{6,4},{7,5},{8,10},{9,11},{10,... | collective-permute-start | bytes 6152 | tf_op jit(solution)/shard_map/ppermute | solution.py:514
  358.6 35.0 %collective-permute-start.46 = (bf16[256,1024]{1,0:T(8,128)(2,1)S(1)}, bf16[256,1024]{1,0:T(8,128)(2,1)S(1)}, u32[]{:S(2)}, u32[]{:S(2)}) collective-permute-start(bf16[256,1024]{1,0:T(8,128)(2,1)S(1)} %get-tuple-element.302), channel_id=1, source_target_pairs={{0,4},{4,0},{8,12},{12,8},{16,20},{20,16},{24,28},{28,24},{1,5},{5... | collective-permute-start | bytes 1572872 | tf_op jit(solution)/shard_map/ppermute | solution.py:514
  378.2 15.4 %collective-permute-start.45 = (bf16[2,256,512]{2,1,0:T(8,128)(2,1)S(1)}, bf16[2,256,512]{2,1,0:T(8,128)(2,1)S(1)}, u32[]{:S(2)}, u32[]{:S(2)}) collective-permute-start(bf16[2,256,512]{2,1,0:T(8,128)(2,1)S(1)} %multiply_convert_fusion.4), channel_id=1, source_target_pairs={{0,2},{1,3},{2,0},{3,1},{4,6},{5,7},{6,4},{7,5},{8,10},{9,11},{10,... | collective-permute-start | bytes 1572872 | tf_op jit(solution)/shard_map/ppermute | solution.py:514
  380.0 14.7 %collective-permute-start.48 = (bf16[2,256,512]{2,1,0:T(8,128)(2,1)S(1)}, bf16[2,256,512]{2,1,0:T(8,128)(2,1)S(1)}, u32[]{:S(2)}, u32[]{:S(2)}) collective-permute-start(bf16[2,256,512]{2,1,0:T(8,128)(2,1)S(1)} %multiply_convert_fusion.4), channel_id=1, source_target_pairs={{0,1},{1,0},{2,3},{3,2},{4,5},{5,4},{6,7},{7,6},{8,9},{9,8},{10,11... | collective-permute-start | bytes 1572872 | tf_op jit(solution)/shard_map/ppermute | solution.py:514
  397.6 67.8 %collective-permute-start.52 = (bf16[512,1024]{1,0:T(8,128)(2,1)}, bf16[512,1024]{1,0:T(8,128)(2,1)}, u32[]{:S(2)}, u32[]{:S(2)}) collective-permute-start(bf16[512,1024]{1,0:T(8,128)(2,1)} %pad_maximum_fusion.8), channel_id=1, source_target_pairs={{0,4},{4,0},{8,12},{12,8},{16,20},{20,16},{24,28},{28,24},{1,5},{5... | collective-permute-start | bytes 3145736 | tf_op jit(solution)/shard_map/ppermute | solution.py:514
  415.2 22.7 %collective-permute-start.49 = (bf16[2,32,1024]{2,1,0:T(8,128)(2,1)}, bf16[2,32,1024]{2,1,0:T(8,128)(2,1)}, u32[]{:S(2)}, u32[]{:S(2)}) collective-permute-start(bf16[2,32,1024]{2,1,0:T(8,128)(2,1)} %pad_maximum_fusion.17), channel_id=1, source_target_pairs={{4,0},{8,4},{12,8},{16,12},{20,16},{24,20},{28,24},{5,1},{9,5},{13... | collective-permute-start | bytes 393224 | tf_op jit(solution)/shard_map/ppermute | solution.py:509
  439.8 16.2 %collective-permute-start.50 = (bf16[2,32,1024]{2,1,0:T(8,128)(2,1)S(1)}, bf16[2,32,1024]{2,1,0:T(8,128)(2,1)S(1)}, u32[]{:S(2)}, u32[]{:S(2)}) collective-permute-start(bf16[2,32,1024]{2,1,0:T(8,128)(2,1)S(1)} %pad_maximum_fusion.18), channel_id=1, source_target_pairs={{8,0},{12,4},{16,8},{20,12},{24,16},{28,20},{9,1},{13,5},{17,9},{2... | collective-permute-start | bytes 393224 | tf_op jit(solution)/shard_map/ppermute | solution.py:509
  466.2 46.1 %collective-permute-start.53 = (bf16[512,1024]{1,0:T(8,128)(2,1)}, bf16[512,1024]{1,0:T(8,128)(2,1)}, u32[]{:S(2)}, u32[]{:S(2)}) collective-permute-start(bf16[512,1024]{1,0:T(8,128)(2,1)} %bitcast.331), channel_id=1, source_target_pairs={{0,4},{4,0},{8,12},{12,8},{16,20},{20,16},{24,28},{28,24},{1,5},{5... | collective-permute-start | bytes 3145736 | tf_op jit(solution)/shard_map/ppermute | solution.py:514
  472.4 210.6 %reduce-scatter.6.cloned.1.call-start = ((), (), s32[]{:S(2)}) async-start(), calls=%async_computation.4 | async-start | bytes 5242880 | tf_op jit(solution)/shard_map/reduce_scatter | solution.py:710
  518.8 10.8 %collective-permute-start.55 = (bf16[2,256,160]{2,1,0:T(8,128)(2,1)S(1)}, bf16[2,256,160]{2,1,0:T(8,128)(2,1)}, u32[]{:S(2)}, u32[]{:S(2)}) collective-permute-start(bf16[2,256,160]{2,1,0:T(8,128)(2,1)S(1)} %fusion.98), channel_id=1, source_target_pairs={{0,2},{1,3},{2,0},{3,1},{4,6},{5,7},{6,4},{7,5},{8,10},{9,11},{10,... | collective-permute-start | bytes 491528 | tf_op jit(solution)/shard_map/ppermute | solution.py:514
  554.5 12.2 %collective-permute-start.57 = (bf16[256,1024]{1,0:T(8,128)(2,1)S(1)}, bf16[256,1024]{1,0:T(8,128)(2,1)S(1)}, u32[]{:S(2)}, u32[]{:S(2)}) collective-permute-start(bf16[256,1024]{1,0:T(8,128)(2,1)S(1)} %get-tuple-element.301), channel_id=1, source_target_pairs={{0,4},{4,0},{8,12},{12,8},{16,20},{20,16},{24,28},{28,24},{1,5},{5... | collective-permute-start | bytes 1572872 | tf_op jit(solution)/shard_map/ppermute | solution.py:514
  572.4 17.1 %collective-permute-start.61 = (bf16[256,1024]{1,0:T(8,128)(2,1)S(1)}, bf16[256,1024]{1,0:T(8,128)(2,1)S(1)}, u32[]{:S(2)}, u32[]{:S(2)}) collective-permute-start(bf16[256,1024]{1,0:T(8,128)(2,1)S(1)} %copy-done.100), channel_id=1, source_target_pairs={{0,4},{4,0},{8,12},{12,8},{16,20},{20,16},{24,28},{28,24},{1,5},{5... | collective-permute-start | bytes 1572872 | tf_op jit(solution)/shard_map/ppermute | solution.py:514
  575.1 15.2 %collective-permute-start.60 = (bf16[2,256,512]{2,1,0:T(8,128)(2,1)S(1)}, bf16[2,256,512]{2,1,0:T(8,128)(2,1)S(1)}, u32[]{:S(2)}, u32[]{:S(2)}) collective-permute-start(bf16[2,256,512]{2,1,0:T(8,128)(2,1)S(1)} %select_convert_fusion.2), channel_id=1, source_target_pairs={{0,2},{1,3},{2,0},{3,1},{4,6},{5,7},{6,4},{7,5},{8,10},{9,11},{10,... | collective-permute-start | bytes 1572872 | tf_op jit(solution)/shard_map/ppermute | solution.py:514
  575.8 13.6 %collective-permute-start.63 = (f32[2,256]{1,0:T(2,128)S(1)}, f32[2,256]{1,0:T(2,128)S(1)}, u32[]{:S(2)}, u32[]{:S(2)}) collective-permute-start(f32[2,256]{1,0:T(2,128)S(1)} %add.606), channel_id=1, source_target_pairs={{0,2},{1,3},{2,0},{3,1},{4,6},{5,7},{6,4},{7,5},{8,10},{9,11},{10,... | collective-permute-start | bytes 6152 | tf_op jit(solution)/shard_map/ppermute | solution.py:514
  596.1 40.7 %collective-permute-start.67 = (bf16[336,1024]{1,0:T(8,128)(2,1)S(1)}, bf16[336,1024]{1,0:T(8,128)(2,1)S(1)}, u32[]{:S(2)}, u32[]{:S(2)}) collective-permute-start(bf16[336,1024]{1,0:T(8,128)(2,1)S(1)} %pad_maximum_fusion.10), channel_id=1, source_target_pairs={{0,4},{4,0},{8,12},{12,8},{16,20},{20,16},{24,28},{28,24},{1,5},{5... | collective-permute-start | bytes 2064392 | tf_op jit(solution)/shard_map/ppermute | solution.py:514
  605.7 25.5 %collective-permute-start.68 = (bf16[256,1024]{1,0:T(8,128)(2,1)S(1)}, bf16[256,1024]{1,0:T(8,128)(2,1)S(1)}, u32[]{:S(2)}, u32[]{:S(2)}) collective-permute-start(bf16[256,1024]{1,0:T(8,128)(2,1)S(1)} %get-tuple-element.250), channel_id=1, source_target_pairs={{0,8},{4,12},{1,9},{5,13},{2,10},{6,14},{3,11},{7,15}} | collective-permute-start | bytes 1572872 | tf_op jit(solution)/shard_map/ppermute | solution.py:732
  608.1 23.2 %collective-permute-start.69 = (bf16[256,1024]{1,0:T(8,128)(2,1)S(1)}, bf16[256,1024]{1,0:T(8,128)(2,1)S(1)}, u32[]{:S(2)}, u32[]{:S(2)}) collective-permute-start(bf16[256,1024]{1,0:T(8,128)(2,1)S(1)} %get-tuple-element.249), channel_id=1, source_target_pairs={{24,16},{28,20},{25,17},{29,21},{26,18},{30,22},{27,19},{31,23}} | collective-permute-start | bytes 1572872 | tf_op jit(solution)/shard_map/ppermute | solution.py:733
  613.7 24.7 %collective-permute-start.64 = (bf16[2,256,512]{2,1,0:T(8,128)(2,1)S(1)}, bf16[2,256,512]{2,1,0:T(8,128)(2,1)S(1)}, u32[]{:S(2)}, u32[]{:S(2)}) collective-permute-start(bf16[2,256,512]{2,1,0:T(8,128)(2,1)S(1)} %get-tuple-element.252), channel_id=1, source_target_pairs={{0,1},{1,0},{2,3},{3,2},{4,5},{5,4},{6,7},{7,6},{8,9},{9,8},{10,11... | collective-permute-start | bytes 1572872 | tf_op jit(solution)/shard_map/ppermute | solution.py:514
  613.8 24.6 %collective-permute-start.65 = (bf16[2,256,512]{2,1,0:T(8,128)(2,1)S(1)}, bf16[2,256,512]{2,1,0:T(8,128)(2,1)S(1)}, u32[]{:S(2)}, u32[]{:S(2)}) collective-permute-start(bf16[2,256,512]{2,1,0:T(8,128)(2,1)S(1)} %get-tuple-element.251), channel_id=1, source_target_pairs={{0,1},{1,0},{2,3},{3,2},{4,5},{5,4},{6,7},{7,6},{8,9},{9,8},{10,11... | collective-permute-start | bytes 1572872 | tf_op jit(solution)/shard_map/ppermute | solution.py:514
  631.7 16.8 %collective-permute-start.71 = (bf16[256,1024]{1,0:T(8,128)(2,1)S(1)}, bf16[256,1024]{1,0:T(8,128)(2,1)S(1)}, u32[]{:S(2)}, u32[]{:S(2)}) collective-permute-start(bf16[256,1024]{1,0:T(8,128)(2,1)S(1)} %get-tuple-element.248), channel_id=1, source_target_pairs={{0,8},{4,12},{8,16},{12,20},{1,9},{5,13},{9,17},{13,21},{2,10},{6,... | collective-permute-start | bytes 1572872 | tf_op jit(solution)/shard_map/ppermute | solution.py:732
  636.1 12.3 %collective-permute-start.72 = (bf16[256,1024]{1,0:T(8,128)(2,1)S(1)}, bf16[256,1024]{1,0:T(8,128)(2,1)S(1)}, u32[]{:S(2)}, u32[]{:S(2)}) collective-permute-start(bf16[256,1024]{1,0:T(8,128)(2,1)S(1)} %get-tuple-element.247), channel_id=1, source_target_pairs={{16,8},{20,12},{24,16},{28,20},{17,9},{21,13},{25,17},{29,21},{18,... | collective-permute-start | bytes 1572872 | tf_op jit(solution)/shard_map/ppermute | solution.py:733
  637.1 20.4 %collective-permute-start.70 = (bf16[208,1024]{1,0:T(8,128)(2,1)S(1)}, bf16[208,1024]{1,0:T(8,128)(2,1)S(1)}, u32[]{:S(2)}, u32[]{:S(2)}) collective-permute-start(bf16[208,1024]{1,0:T(8,128)(2,1)S(1)} %pad_maximum_fusion.11), channel_id=1, source_target_pairs={{0,8},{4,12},{8,0},{12,4},{16,24},{20,28},{24,16},{28,20},{1,9},{5... | collective-permute-start | bytes 1277960 | tf_op jit(solution)/shard_map/ppermute | solution.py:514
  638.8 22.9 %collective-permute-start.66 = (bf16[2,256,512]{2,1,0:T(8,128)(2,1)S(1)}, bf16[2,256,512]{2,1,0:T(8,128)(2,1)S(1)}, u32[]{:S(2)}, u32[]{:S(2)}) collective-permute-start(bf16[2,256,512]{2,1,0:T(8,128)(2,1)S(1)} %select_convert_fusion.1), channel_id=1, source_target_pairs={{0,2},{1,3},{2,0},{3,1},{4,6},{5,7},{6,4},{7,5},{8,10},{9,11},{10,... | collective-permute-start | bytes 1572872 | tf_op jit(solution)/shard_map/ppermute | solution.py:514
  648.8 19.9 %collective-permute-start.74 = (bf16[256,1024]{1,0:T(8,128)(2,1)S(1)}, bf16[256,1024]{1,0:T(8,128)(2,1)S(1)}, u32[]{:S(2)}, u32[]{:S(2)}) collective-permute-start(bf16[256,1024]{1,0:T(8,128)(2,1)S(1)} %get-tuple-element.246), channel_id=1, source_target_pairs={{0,8},{4,12},{8,16},{12,20},{16,24},{20,28},{1,9},{5,13},{9,17},{1... | collective-permute-start | bytes 1572872 | tf_op jit(solution)/shard_map/ppermute | solution.py:732
  653.3 15.8 %collective-permute-start.75 = (bf16[256,1024]{1,0:T(8,128)(2,1)S(1)}, bf16[256,1024]{1,0:T(8,128)(2,1)S(1)}, u32[]{:S(2)}, u32[]{:S(2)}) collective-permute-start(bf16[256,1024]{1,0:T(8,128)(2,1)S(1)} %get-tuple-element.245), channel_id=1, source_target_pairs={{8,0},{12,4},{16,8},{20,12},{24,16},{28,20},{9,1},{13,5},{17,9},{2... | collective-permute-start | bytes 1572872 | tf_op jit(solution)/shard_map/ppermute | solution.py:733
  657.8 20.5 %collective-permute-start.73 = (bf16[144,1024]{1,0:T(8,128)(2,1)S(1)}, bf16[144,1024]{1,0:T(8,128)(2,1)S(1)}, u32[]{:S(2)}, u32[]{:S(2)}) collective-permute-start(bf16[144,1024]{1,0:T(8,128)(2,1)S(1)} %pad_maximum_fusion.12), channel_id=1, source_target_pairs={{0,16},{4,20},{8,24},{12,28},{16,0},{20,4},{24,8},{28,12},{1,17},{... | collective-permute-start | bytes 884744 | tf_op jit(solution)/shard_map/ppermute | solution.py:514
  (223 other events, 1985.0 us)
Sparse Core Ops, SparseCore 0:
  280.0 178.1 reduce-scatter.3
Sparse Core Ops, SparseCore 1:
  472.4 41.4 reduce-scatter.7
  547.8 86.9 reduce-scatter.5

commit v4 on v3

--- a/solution.py
+++ b/solution.py
@@ -9,7 +9,7 @@
 
 CH = 16
 LANES = 128
-VMEM_BYTES = 20 * 1024 * 1024
+VMEM_BYTES = 27 * 1024 * 1024
 BLOCK = 128
 norm_epsilon = 1e-05
 F32 = jnp.float32

time: 712 us -> 709 us (level)
  local copies, waits for them, and re-layouts: 63.5 us -> 50.7 us
  Pallas kernels: 177 us -> 187 us
    unnamed x390 -> x326, local copies, waits for them, and re-layouts: 28.8 us -> 20.3 us
  transfers between devices with their start and end apart: 79 -> 79, of which waited for: 40 -> 40; matrix products, arithmetic and copies ran while one was open for 18% -> 17% of each run, Pallas kernels for 25% -> 27%
where the time goes in v4:
time: 709 us; the launch traced here: 699 us
  waiting for transfers between devices  196 us (28%)
  Pallas kernels  187 us (26%)
  starting transfers between devices  115 us (16%)
  other arithmetic  77.1 us (11%)
  matrix products  53.5 us (8%)
  local copies, waits for them, and re-layouts  50.7 us (7%)
  between operations  19 us (3%)
    ppermute x54, waiting for transfers between devices, swapped(): lax.ppermute(value, axis, [(source, source ^ bit) for source in range(cou...  111 us
    pallas_call x2, Pallas kernels, run_backward(): pl.pallas_call(functools.partial(backward_kernel, states), grid=grid, in_...  79.2 us
    ppermute x16, waiting for transfers between devices, shifted(): lax.ppermute(value, axis, [(source, source + steps) for source in range(l...  53.6 us
    dot_general x20, matrix products, matmul(): return jnp.einsum(dims, left, right, preferred_element_type=F32)  53.5 us
    ppermute x54, starting transfers between devices, swapped(): lax.ppermute(value, axis, [(source, source ^ bit) for source in range(cou...  53 us
    ppermute x16, starting transfers between devices, shifted(): lax.ppermute(value, axis, [(source, source + steps) for source in range(l...  47.9 us
    pallas_call x2, Pallas kernels, run_forward(): pl.pallas_call(functools.partial(forward_kernel, states), grid=grid, in_s...  37.3 us
    ppermute x3, waiting for transfers between devices, line_task(): right = lax.ppermute(ahead, 'seq', pairs(range(min(step, long - 1)), 1))  30.1 us
  transfers between devices with their start and end apart: 79, of which 40 were waited for; matrix products, arithmetic and copies ran while one was open for 17% of the time, Pallas kernels for 27%

profile of v4, /device:TPU:0, one launch (start us, length us, event | category | flops | bytes accessed | tf_op | source)
XLA Modules:
  0.0 699.2 jit_solution(377135518874436015)
XLA Ops:
  14.0 14.2 %slice_bitcast_fusion = (bf16[2048,2,1024]{2,1,0:T(2,128)(2,1)}, bf16[2048,2,1024]{2,1,0:T(2,128)(2,1)}) fusion(bf16[2,2048,2,1024]{3,2,1,0:T(2,128)(2,1)} %param.15), kind=kLoop, calls=%fused_computation | loop fusion | bytes 33554432 | tf_op jit(solution)/shard_map/squeeze | solution.py:1080
  35.9 4.9 multiply_convert_fusion.1
  60.0 4.8 collective-permute-done.8
  68.4 10.2 %shard_map.220 = bf16[2,32,1024]{2,1,0:T(8,128)(2,1)S(1)} custom-call(f32[2,256,1024]{2,1,0:T(8,128)S(1)} %fusion.71.r_ref, bf16[2,256,1024]{2,1,0:T(8,128)(2,1)S(1)} %get-tuple-element.238.act_ref, f32[2,256,160]{2,1,0:T(8,128)S(1)} %convert_add_fusion.21.sel_ref, f32[2,256,128]{2,1,0:T(8,128)S(1)} %broadcast_in_dim.26.keep_ref), custom_call_target="tpu_custom_call" | custom-call | flops 50331648 | bytes 16777216 | tf_op jit(solution)/shard_map/pallas_call | solution.py:402
  85.6 6.3 collective-permute-start.10
  94.4 5.8 collective-permute-start.11
  106.4 18.6 %shard_map.221 = (bf16[2,4096,1024]{2,1,0:T(8,128)(2,1)}, bf16[2,256,1024]{2,1,0:T(8,128)(2,1)}, bf16[2,256,1024]{2,1,0:T(8,128)(2,1)}) custom-call(f32[2,256,1024]{2,1,0:T(8,128)} %copy-done, bf16[2,256,1024]{2,1,0:T(8,128)(2,1)} %copy-done.3, f32[2,256,160]{2,1,0:T(8,128)} %copy-done.6, f32[2,256,128]{2,1,0:T(8,128)} %copy-done.15, ...), custom_call_target="tpu_custom_call" | custom-call | flops 67108864 | bytes 16777216 | tf_op jit(solution)/shard_map/pallas_call | solution.py:421
  126.4 4.5 fusion.24
  135.9 12.7 %collective-permute-done.21 = bf16[2,256,512]{2,1,0:T(8,128)(2,1)S(1)} collective-permute-done((bf16[2,256,512]{2,1,0:T(8,128)(2,1)S(1)}, bf16[2,256,512]{2,1,0:T(8,128)(2,1)S(1)}, u32[]{:S(2)}, u32[]{:S(2)}) %collective-permute-start.21) | collective-permute-done | bytes 524320 | tf_op jit(solution)/shard_map/ppermute | solution.py:514
  150.8 11.9 %collective-permute-done.22 = bf16[2,256,512]{2,1,0:T(8,128)(2,1)S(1)} collective-permute-done((bf16[2,256,512]{2,1,0:T(8,128)(2,1)S(1)}, bf16[2,256,512]{2,1,0:T(8,128)(2,1)S(1)}, u32[]{:S(2)}, u32[]{:S(2)}) %collective-permute-start.22) | collective-permute-done | bytes 524320 | tf_op jit(solution)/shard_map/ppermute | solution.py:514
  165.6 4.9 multiply_convert_fusion
  175.5 7.5 %multiply_reduce_fusion.2 = (f32[1024]{0:T(1024)}, f32[2,256,1024]{2,1,0:T(8,128)}, bf16[2,256,1024]{2,1,0:T(8,128)(2,1)S(1)}, f32[2,256,1024]{2,1,0:T(8,128)}, f32[2,256,1024]{2,1,0:T(8,128)}) fusion(bf16[2,256,2,1024]{3,1,0,2:T(8,128)(2,1)S(1)} %multiply_convert_fusion, f32[2,256]{1,0:T(2,128)S(1)} %get-tuple-element.349, ...), kind=kOutput, calls=%fused_computation.92 | convolution fusion | flops 2161114112 | bytes 23101440 | tf_op jit(solution)/shard_map/mrd,id->mri/dot_general | solution.py:799
  198.2 9.0 %shard_map.224 = bf16[2,16,1024]{2,1,0:T(8,128)(2,1)S(1)} custom-call(f32[2,256,1024]{2,1,0:T(8,128)S(1)} %fusion.70.r_ref, f32[2,256,1024]{2,1,0:T(8,128)S(1)} %copy-done.19, f32[2,256,160]{2,1,0:T(8,128)S(1)} %convert_add_fusion.19.sel_ref, f32[2,256,128]{2,1,0:T(8,128)S(1)} %copy-done.16), custom_call_target="tpu_custom_call" | custom-call | flops 41943040 | bytes 16777216 | tf_op jit(solution)/shard_map/pallas_call | solution.py:450
  207.2 10.2 %shard_map.222 = bf16[2,32,1024]{2,1,0:T(8,128)(2,1)S(1)} custom-call(f32[2,256,1024]{2,1,0:T(8,128)S(1)} %fusion.70.r_ref, bf16[2,256,1024]{2,1,0:T(8,128)(2,1)S(1)} %copy-done.13, f32[2,256,160]{2,1,0:T(8,128)S(1)} %convert_add_fusion.19.sel_ref, f32[2,256,128]{2,1,0:T(8,128)S(1)} %copy-done.16), custom_call_target="tpu_custom_call" | custom-call | flops 50331648 | bytes 16777216 | tf_op jit(solution)/shard_map/pallas_call | solution.py:402
  218.8 5.8 collective-permute-start.28
  229.3 4.9 collective-permute-start.29
  236.7 4.4 collective-permute-done.33
  247.9 18.7 %shard_map.223 = (bf16[2,4096,1024]{2,1,0:T(8,128)(2,1)}, bf16[2,256,1024]{2,1,0:T(8,128)(2,1)}, bf16[2,256,1024]{2,1,0:T(8,128)(2,1)}) custom-call(f32[2,256,1024]{2,1,0:T(8,128)} %copy-done.2, bf16[2,256,1024]{2,1,0:T(8,128)(2,1)} %copy-done.12, f32[2,256,160]{2,1,0:T(8,128)} %copy-done.9, f32[2,256,128]{2,1,0:T(8,128)} %copy-done.15, ...), custom_call_target="tpu_custom_call" | custom-call | flops 67108864 | bytes 16777216 | tf_op jit(solution)/shard_map/pallas_call | solution.py:421
  269.9 10.7 %shard_map.225 = bf16[8,256,2048]{2,1,0:T(8,128)(2,1)} custom-call(bf16[512,2048]{1,0:T(8,128)(2,1)} %bitcast.290, bf16[512,1024]{1,0:T(8,128)(2,1)} %bitcast.303, bf16[512,2048]{1,0:T(8,128)(2,1)} %bitcast.311, bf16[512,1024]{1,0:T(8,128)(2,1)} %bitcast.391), custom_call_target="tpu_custom_call" | custom-call | flops 4294967296 | bytes 4194304 | tf_op jit(solution)/shard_map/pallas_call | solution.py:697
  284.9 39.5 %shard_map.226 = (f32[2,256,1024]{2,1,0:T(8,128)}, f32[2,256,1024]{2,1,0:T(8,128)}, f32[2,256,160]{2,1,0:T(8,128)}) custom-call(f32[2,256,1024]{2,1,0:T(8,128)} %copy-done.2, bf16[2,256,1024]{2,1,0:T(8,128)(2,1)} %copy-done.12, f32[2,256,1024]{2,1,0:T(8,128)} %get-tuple-element.216.gm_ref, f32[2,256,160]{2,1,0:T(8,128)} %copy-done.9, ...), custom_call_target="tpu_custom_call" | custom-call | flops 134217728 | bytes 16777216 | tf_op jit(solution)/shard_map/pallas_call | solution.py:471
  324.5 5.0 fusion.152
  333.4 6.8 collective-permute-done.37
  350.7 5.2 bitcast_convert_fusion.1
  366.0 8.5 %collective-permute-done.44 = f32[2,256]{1,0:T(2,128)S(1)} collective-permute-done((f32[2,256]{1,0:T(2,128)S(1)}, f32[2,256]{1,0:T(2,128)S(1)}, u32[]{:S(2)}, u32[]{:S(2)}) %collective-permute-start.44) | collective-permute-done | bytes 2080 | tf_op jit(solution)/shard_map/ppermute | solution.py:514
  374.6 8.7 %collective-permute-done.42 = bf16[256,1024]{1,0:T(8,128)(2,1)S(1)} collective-permute-done((bf16[256,1024]{1,0:T(8,128)(2,1)S(1)}, bf16[256,1024]{1,0:T(8,128)(2,1)S(1)}, u32[]{:S(2)}, u32[]{:S(2)}) %collective-permute-start.42) | collective-permute-done | bytes 524320 | tf_op jit(solution)/shard_map/ppermute | solution.py:514
  386.0 15.7 %collective-permute-done.46 = bf16[256,1024]{1,0:T(8,128)(2,1)S(1)} collective-permute-done((bf16[256,1024]{1,0:T(8,128)(2,1)S(1)}, bf16[256,1024]{1,0:T(8,128)(2,1)S(1)}, u32[]{:S(2)}, u32[]{:S(2)}) %collective-permute-start.46) | collective-permute-done | bytes 524320 | tf_op jit(solution)/shard_map/ppermute | solution.py:514
  408.3 4.9 multiply_reduce_fusion.7
  413.2 9.4 %shard_map.227 = bf16[2,16,1024]{2,1,0:T(8,128)(2,1)S(1)} custom-call(f32[2,256,1024]{2,1,0:T(8,128)S(1)} %copy-done.1, f32[2,256,1024]{2,1,0:T(8,128)S(1)} %get-tuple-element.224.gm_ref, f32[2,256,160]{2,1,0:T(8,128)S(1)} %copy-done.7, f32[2,256,128]{2,1,0:T(8,128)S(1)} %copy-done.17), custom_call_target="tpu_custom_call" | custom-call | flops 41943040 | bytes 16777216 | tf_op jit(solution)/shard_map/pallas_call | solution.py:450
  424.0 6.1 shard_map.228
  430.1 15.8 %collective-permute-done.49 = bf16[2,32,1024]{2,1,0:T(8,128)(2,1)S(1)} collective-permute-done((bf16[2,32,1024]{2,1,0:T(8,128)(2,1)S(1)}, bf16[2,32,1024]{2,1,0:T(8,128)(2,1)S(1)}, u32[]{:S(2)}, u32[]{:S(2)}) %collective-permute-start.49) | collective-permute-done | bytes 131104 | tf_op jit(solution)/shard_map/ppermute | solution.py:509
  447.5 11.5 %collective-permute-done.50 = bf16[2,32,1024]{2,1,0:T(8,128)(2,1)S(1)} collective-permute-done((bf16[2,32,1024]{2,1,0:T(8,128)(2,1)S(1)}, bf16[2,32,1024]{2,1,0:T(8,128)(2,1)S(1)}, u32[]{:S(2)}, u32[]{:S(2)}) %collective-permute-start.50) | collective-permute-done | bytes 131104 | tf_op jit(solution)/shard_map/ppermute | solution.py:509
  460.5 5.8 collective-permute-done.51
  470.8 39.6 %shard_map.229 = (f32[2,256,1024]{2,1,0:T(8,128)}, f32[2,256,1024]{2,1,0:T(8,128)}, f32[2,256,160]{2,1,0:T(8,128)}) custom-call(f32[2,256,1024]{2,1,0:T(8,128)} %copy-done, bf16[2,256,1024]{2,1,0:T(8,128)(2,1)} %copy-done.3, f32[2,256,1024]{2,1,0:T(8,128)} %copy-done.18, f32[2,256,160]{2,1,0:T(8,128)} %copy-done.6, f32[2,256,128]{2,1,0:T(8,128)} %copy-done.15, ...), custom_call_target="tpu_custom_call" | custom-call | flops 134217728 | bytes 16777216 | tf_op jit(solution)/shard_map/pallas_call | solution.py:471
  510.6 4.6 fusion.154
  520.8 9.1 %shard_map.230 = bf16[4,256,2048]{2,1,0:T(8,128)(2,1)} custom-call(s32[1]{0:T(128)} %bitcast.51.side_ref, bf16[512,2048]{1,0:T(8,128)(2,1)} %bitcast.315, bf16[512,1024]{1,0:T(8,128)(2,1)} %pad_maximum_fusion.5.refs_1_, bf16[512,1024]{1,0:T(8,128)(2,1)} %bitcast.329, bf16[512,1024]{1,0:T(8,128)(2,1)} %collective-permute-done.53.refs_3_, ...), custom_call_target="tpu_custom_call" | custom-call | flops 4294967296 | bytes 4194304 | tf_op jit(solution)/shard_map/pallas_call | solution.py:673
  532.7 8.6 %multiply_reduce_fusion.8 = (f32[1024]{0:T(1024)S(1)}, f32[1024]{0:T(1024)S(1)}, f32[1024]{0:T(1024)S(1)}, f32[1024]{0:T(1024)S(1)}, f32[1024]{0:T(1024)S(1)}, /...) fusion(f32[2,259,1024]{2,1,0:T(8,128)S(1)} %copy-done.21, ...), kind=kLoop, calls=%fused_computation.98 | loop fusion | flops 18339840 | bytes 27312128 | tf_op jit(solution)/shard_map/reduce_sum | solution.py:996
  553.8 9.2 %bitcast_convert_fusion = bf16[2,256,2048]{2,1,0:T(8,128)(2,1)S(1)} fusion(bf16[2048,2,1024,1]{2,1,0,3:T(2,128)(2,1)} %bitcast.295, bf16[2,256,1,1024]{3,1,0,2:T(8,128)(2,1)S(1)} %bitcast.330, bf16[2,256,1,1024]{3,1,0,2:T(8,128)(2,1)S(1)} %bitcast.306), kind=kOutput, calls=%fused_computation.10 | convolution fusion | flops 4297064448 | bytes 12582912 | tf_op jit(solution)/shard_map/bptg,htg->bph/dot_general | solution.py:799
  575.2 11.2 %collective-permute-done.63 = f32[2,256]{1,0:T(2,128)S(1)} collective-permute-done((f32[2,256]{1,0:T(2,128)S(1)}, f32[2,256]{1,0:T(2,128)S(1)}, u32[]{:S(2)}, u32[]{:S(2)}) %collective-permute-start.63) | collective-permute-done | bytes 2080 | tf_op jit(solution)/shard_map/ppermute | solution.py:514
  595.0 6.1 shard_map.231
  605.8 4.5 fusion.27
  611.2 16.8 %collective-permute-done.68 = bf16[256,1024]{1,0:T(8,128)(2,1)S(1)} collective-permute-done((bf16[256,1024]{1,0:T(8,128)(2,1)S(1)}, bf16[256,1024]{1,0:T(8,128)(2,1)S(1)}, u32[]{:S(2)}, u32[]{:S(2)}) %collective-permute-start.68) | collective-permute-done | bytes 524320 | tf_op jit(solution)/shard_map/ppermute | solution.py:732
  628.4 4.4 collective-permute-start.71
  637.1 8.1 %collective-permute-done.71 = bf16[256,1024]{1,0:T(8,128)(2,1)S(1)} collective-permute-done((bf16[256,1024]{1,0:T(8,128)(2,1)S(1)}, bf16[256,1024]{1,0:T(8,128)(2,1)S(1)}, u32[]{:S(2)}, u32[]{:S(2)}) %collective-permute-start.71) | collective-permute-done | bytes 524320 | tf_op jit(solution)/shard_map/ppermute | solution.py:732
  645.6 4.8 collective-permute-start.74
  654.6 4.5 collective-permute-start.73
  660.4 5.1 collective-permute-done.74
  666.3 9.2 %collective-permute-done.73 = bf16[144,1024]{1,0:T(8,128)(2,1)S(1)} collective-permute-done((bf16[144,1024]{1,0:T(8,128)(2,1)S(1)}, bf16[144,1024]{1,0:T(8,128)(2,1)S(1)}, u32[]{:S(2)}, u32[]{:S(2)}) %collective-permute-start.73) | collective-permute-done | bytes 294944 | tf_op jit(solution)/shard_map/ppermute | solution.py:514
  684.1 5.2 copy.141
  (641 shorter events, 215.9 us)
Async XLA Ops:
  8.0 459.1 %reduce-scatter.4.cloned.1.call-start = ((), (), s32[]{:S(2)}) async-start(), calls=%async_computation.3 | async-start | bytes 9437184 | tf_op jit(solution)/shard_map/reduce_scatter | solution.py:940
  8.7 20.2 %collective-permute-start.5 = (f32[2,512]{1,0:T(2,128)S(1)}, f32[2,512]{1,0:T(2,128)S(1)}, u32[]{:S(2)}, u32[]{:S(2)}) collective-permute-start(f32[2,512]{1,0:T(2,128)S(1)} %convert_element_type.575), channel_id=1, source_target_pairs={{0,1},{1,0},{2,3},{3,2},{4,5},{5,4},{6,7},{7,6},{8,9},{9,8},{10,11... | collective-permute-start | bytes 12296 | tf_op jit(solution)/shard_map/ppermute | solution.py:514
  9.2 19.3 %collective-permute-start.3 = (f32[2,512]{1,0:T(2,128)S(1)}, f32[2,512]{1,0:T(2,128)S(1)}, u32[]{:S(2)}, u32[]{:S(2)}) collective-permute-start(f32[2,512]{1,0:T(2,128)S(1)} %convert_element_type.575), channel_id=1, source_target_pairs={{0,2},{1,3},{2,0},{3,1},{4,6},{5,7},{6,4},{7,5},{8,10},{9,11},{10,... | collective-permute-start | bytes 12296 | tf_op jit(solution)/shard_map/ppermute | solution.py:514
  13.6 16.2 %collective-permute-start = (bf16[2,256,512]{2,1,0:T(8,128)(2,1)S(1)}, bf16[2,256,512]{2,1,0:T(8,128)(2,1)S(1)}, u32[]{:S(2)}, u32[]{:S(2)}) collective-permute-start(bf16[2,256,512]{2,1,0:T(8,128)(2,1)S(1)} %multiply_convert_fusion.6), channel_id=1, source_target_pairs={{0,2},{1,3},{2,0},{3,1},{4,6},{5,7},{6,4},{7,5},{8,10},{9,11},{10,... | collective-permute-start | bytes 1572872 | tf_op jit(solution)/shard_map/ppermute | solution.py:514
  13.7 16.5 %collective-permute-start.2 = (bf16[2,256,512]{2,1,0:T(8,128)(2,1)S(1)}, bf16[2,256,512]{2,1,0:T(8,128)(2,1)S(1)}, u32[]{:S(2)}, u32[]{:S(2)}) collective-permute-start(bf16[2,256,512]{2,1,0:T(8,128)(2,1)S(1)} %multiply_convert_fusion.6), channel_id=1, source_target_pairs={{0,1},{1,0},{2,3},{3,2},{4,5},{5,4},{6,7},{7,6},{8,9},{9,8},{10,11... | collective-permute-start | bytes 1572872 | tf_op jit(solution)/shard_map/ppermute | solution.py:514
  57.6 25.3 %collective-permute-start.12 = (bf16[512,256]{1,0:T(8,128)(2,1)}, bf16[512,256]{1,0:T(8,128)(2,1)S(1)}, u32[]{:S(2)}, u32[]{:S(2)}) collective-permute-start(bf16[512,256]{1,0:T(8,128)(2,1)} %bitcast.332), channel_id=1, source_target_pairs={{0,4},{4,0},{8,12},{12,8},{16,20},{20,16},{24,28},{28,24},{1,5},{5... | collective-permute-start | bytes 786440 | tf_op jit(solution)/shard_map/ppermute | solution.py:514
  82.9 10.7 %collective-permute-start.13 = (bf16[512,256]{1,0:T(8,128)(2,1)S(1)}, bf16[512,256]{1,0:T(8,128)(2,1)S(1)}, u32[]{:S(2)}, u32[]{:S(2)}) collective-permute-start(bf16[512,256]{1,0:T(8,128)(2,1)S(1)} %collective-permute-done.12), channel_id=1, source_target_pairs={{0,2},{1,3},{2,0},{3,1},{4,6},{5,7},{6,4},{7,5},{8,10},{9,11},{10,... | collective-permute-start | bytes 786440 | tf_op jit(solution)/shard_map/ppermute | solution.py:514
  92.0 12.5 %collective-permute-start.16 = (bf16[2,256,512]{2,1,0:T(8,128)(2,1)S(1)}, bf16[2,256,512]{2,1,0:T(8,128)(2,1)S(1)}, u32[]{:S(2)}, u32[]{:S(2)}) collective-permute-start(bf16[2,256,512]{2,1,0:T(8,128)(2,1)S(1)} %fusion.72), channel_id=1, source_target_pairs={{0,2},{1,3},{2,0},{3,1},{4,6},{5,7},{6,4},{7,5},{8,10},{9,11},{10,... | collective-permute-start | bytes 1572872 | tf_op jit(solution)/shard_map/ppermute | solution.py:514
  93.6 11.6 %collective-permute-start.15 = (bf16[512,256]{1,0:T(8,128)(2,1)S(1)}, bf16[512,256]{1,0:T(8,128)(2,1)S(1)}, u32[]{:S(2)}, u32[]{:S(2)}) collective-permute-start(bf16[512,256]{1,0:T(8,128)(2,1)S(1)} %collective-permute-done.12), channel_id=1, source_target_pairs={{0,1},{1,0},{2,3},{3,2},{4,5},{5,4},{6,7},{7,6},{8,9},{9,8},{10,11... | collective-permute-start | bytes 786440 | tf_op jit(solution)/shard_map/ppermute | solution.py:514
  93.6 11.6 %collective-permute-start.14 = (bf16[512,256]{1,0:T(8,128)(2,1)S(1)}, bf16[512,256]{1,0:T(8,128)(2,1)S(1)}, u32[]{:S(2)}, u32[]{:S(2)}) collective-permute-start(bf16[512,256]{1,0:T(8,128)(2,1)S(1)} %collective-permute-done.13), channel_id=1, source_target_pairs={{0,1},{1,0},{2,3},{3,2},{4,5},{5,4},{6,7},{7,6},{8,9},{9,8},{10,11... | collective-permute-start | bytes 786440 | tf_op jit(solution)/shard_map/ppermute | solution.py:514
  100.8 24.1 %collective-permute-start.18 = (bf16[2,256,512]{2,1,0:T(8,128)(2,1)S(1)}, bf16[2,256,512]{2,1,0:T(8,128)(2,1)S(1)}, u32[]{:S(2)}, u32[]{:S(2)}) collective-permute-start(bf16[2,256,512]{2,1,0:T(8,128)(2,1)S(1)} %fusion.72), channel_id=1, source_target_pairs={{0,1},{1,0},{2,3},{3,2},{4,5},{5,4},{6,7},{7,6},{8,9},{9,8},{10,11... | collective-permute-start | bytes 1572872 | tf_op jit(solution)/shard_map/ppermute | solution.py:514
  104.5 20.5 %collective-permute-start.17 = (bf16[2,256,512]{2,1,0:T(8,128)(2,1)S(1)}, bf16[2,256,512]{2,1,0:T(8,128)(2,1)S(1)}, u32[]{:S(2)}, u32[]{:S(2)}) collective-permute-start(bf16[2,256,512]{2,1,0:T(8,128)(2,1)S(1)} %collective-permute-done.16), channel_id=1, source_target_pairs={{0,1},{1,0},{2,3},{3,2},{4,5},{5,4},{6,7},{7,6},{8,9},{9,8},{10,11... | collective-permute-start | bytes 1572872 | tf_op jit(solution)/shard_map/ppermute | solution.py:514
  134.3 14.3 %collective-permute-start.21 = (bf16[2,256,512]{2,1,0:T(8,128)(2,1)S(1)}, bf16[2,256,512]{2,1,0:T(8,128)(2,1)S(1)}, u32[]{:S(2)}, u32[]{:S(2)}) collective-permute-start(bf16[2,256,512]{2,1,0:T(8,128)(2,1)S(1)} %select_convert_fusion.4), channel_id=1, source_target_pairs={{0,2},{1,3},{2,0},{3,1},{4,6},{5,7},{6,4},{7,5},{8,10},{9,11},{10,... | collective-permute-start | bytes 1572872 | tf_op jit(solution)/shard_map/ppermute | solution.py:514
  149.2 13.4 %collective-permute-start.22 = (bf16[2,256,512]{2,1,0:T(8,128)(2,1)S(1)}, bf16[2,256,512]{2,1,0:T(8,128)(2,1)S(1)}, u32[]{:S(2)}, u32[]{:S(2)}) collective-permute-start(bf16[2,256,512]{2,1,0:T(8,128)(2,1)S(1)} %get-tuple-element.236), channel_id=1, source_target_pairs={{0,2},{1,3},{2,0},{3,1},{4,6},{5,7},{6,4},{7,5},{8,10},{9,11},{10,... | collective-permute-start | bytes 1572872 | tf_op jit(solution)/shard_map/ppermute | solution.py:514
  150.8 11.9 %collective-permute-start.24 = (bf16[2,256,512]{2,1,0:T(8,128)(2,1)S(1)}, bf16[2,256,512]{2,1,0:T(8,128)(2,1)S(1)}, u32[]{:S(2)}, u32[]{:S(2)}) collective-permute-start(bf16[2,256,512]{2,1,0:T(8,128)(2,1)S(1)} %get-tuple-element.236), channel_id=1, source_target_pairs={{0,1},{1,0},{2,3},{3,2},{4,5},{5,4},{6,7},{7,6},{8,9},{9,8},{10,11... | collective-permute-start | bytes 1572872 | tf_op jit(solution)/shard_map/ppermute | solution.py:514
  187.8 29.6 %collective-permute-start.31 = (bf16[512,1024]{1,0:T(8,128)(2,1)}, bf16[512,1024]{1,0:T(8,128)(2,1)S(1)}, u32[]{:S(2)}, u32[]{:S(2)}) collective-permute-start(bf16[512,1024]{1,0:T(8,128)(2,1)} %bitcast.389), channel_id=1, source_target_pairs={{0,4},{4,0},{8,12},{12,8},{16,20},{20,16},{24,28},{28,24},{1,5},{5... | collective-permute-start | bytes 3145736 | tf_op jit(solution)/shard_map/ppermute | solution.py:514
  218.8 10.3 %collective-permute-start.28 = (bf16[2,32,1024]{2,1,0:T(8,128)(2,1)S(1)}, bf16[2,32,1024]{2,1,0:T(8,128)(2,1)S(1)}, u32[]{:S(2)}, u32[]{:S(2)}) collective-permute-start(bf16[2,32,1024]{2,1,0:T(8,128)(2,1)S(1)} %shard_map.222), channel_id=1, source_target_pairs={{0,4},{4,8},{8,12},{12,16},{16,20},{20,24},{24,28},{1,5},{5,9},{9,... | collective-permute-start | bytes 393224 | tf_op jit(solution)/shard_map/ppermute | solution.py:509
  245.3 35.3 %collective-permute-start.34 = (bf16[2,16,1024]{2,1,0:T(8,128)(2,1)}, bf16[2,16,1024]{2,1,0:T(8,128)(2,1)}, u32[]{:S(2)}, u32[]{:S(2)}) collective-permute-start(bf16[2,16,1024]{2,1,0:T(8,128)(2,1)} %get-tuple-element.323), channel_id=1, source_target_pairs={{16,0},{20,4},{24,8},{28,12},{17,1},{21,5},{25,9},{29,13},{18,2},{... | collective-permute-start | bytes 196616 | tf_op jit(solution)/shard_map/ppermute | solution.py:509
  282.3 283.6 %reduce-scatter.8.cloned.1.call-start = ((), (), s32[]{:S(2)}) async-start(), calls=%async_computation.5 | async-start | bytes 2621440 | tf_op jit(solution)/shard_map/reduce_scatter | solution.py:710
  284.2 40.3 %collective-permute-start.35 = (bf16[512,1024]{1,0:T(8,128)(2,1)S(1)}, bf16[512,1024]{1,0:T(8,128)(2,1)S(1)}, u32[]{:S(2)}, u32[]{:S(2)}) collective-permute-start(bf16[512,1024]{1,0:T(8,128)(2,1)S(1)} %pad_maximum_fusion.6), channel_id=1, source_target_pairs={{0,4},{4,0},{8,12},{12,8},{16,20},{20,16},{24,28},{28,24},{1,5},{5... | collective-permute-start | bytes 3145736 | tf_op jit(solution)/shard_map/ppermute | solution.py:514
  356.7 26.6 %collective-permute-start.42 = (bf16[256,1024]{1,0:T(8,128)(2,1)S(1)}, bf16[256,1024]{1,0:T(8,128)(2,1)S(1)}, u32[]{:S(2)}, u32[]{:S(2)}) collective-permute-start(bf16[256,1024]{1,0:T(8,128)(2,1)S(1)} %get-tuple-element.303), channel_id=1, source_target_pairs={{0,4},{4,0},{8,12},{12,8},{16,20},{20,16},{24,28},{28,24},{1,5},{5... | collective-permute-start | bytes 1572872 | tf_op jit(solution)/shard_map/ppermute | solution.py:514
  360.8 22.5 %collective-permute-start.41 = (bf16[2,256,512]{2,1,0:T(8,128)(2,1)S(1)}, bf16[2,256,512]{2,1,0:T(8,128)(2,1)S(1)}, u32[]{:S(2)}, u32[]{:S(2)}) collective-permute-start(bf16[2,256,512]{2,1,0:T(8,128)(2,1)S(1)} %select_convert_fusion.3), channel_id=1, source_target_pairs={{0,2},{1,3},{2,0},{3,1},{4,6},{5,7},{6,4},{7,5},{8,10},{9,11},{10,... | collective-permute-start | bytes 1572872 | tf_op jit(solution)/shard_map/ppermute | solution.py:514
  363.6 10.9 %collective-permute-start.44 = (f32[2,256]{1,0:T(2,128)S(1)}, f32[2,256]{1,0:T(2,128)S(1)}, u32[]{:S(2)}, u32[]{:S(2)}) collective-permute-start(f32[2,256]{1,0:T(2,128)S(1)} %add.582), channel_id=1, source_target_pairs={{0,2},{1,3},{2,0},{3,1},{4,6},{5,7},{6,4},{7,5},{8,10},{9,11},{10,... | collective-permute-start | bytes 6152 | tf_op jit(solution)/shard_map/ppermute | solution.py:514
  364.0 37.7 %collective-permute-start.46 = (bf16[256,1024]{1,0:T(8,128)(2,1)S(1)}, bf16[256,1024]{1,0:T(8,128)(2,1)S(1)}, u32[]{:S(2)}, u32[]{:S(2)}) collective-permute-start(bf16[256,1024]{1,0:T(8,128)(2,1)S(1)} %get-tuple-element.302), channel_id=1, source_target_pairs={{0,4},{4,0},{8,12},{12,8},{16,20},{20,16},{24,28},{28,24},{1,5},{5... | collective-permute-start | bytes 1572872 | tf_op jit(solution)/shard_map/ppermute | solution.py:514
  384.8 17.0 %collective-permute-start.45 = (bf16[2,256,512]{2,1,0:T(8,128)(2,1)S(1)}, bf16[2,256,512]{2,1,0:T(8,128)(2,1)S(1)}, u32[]{:S(2)}, u32[]{:S(2)}) collective-permute-start(bf16[2,256,512]{2,1,0:T(8,128)(2,1)S(1)} %multiply_convert_fusion.4), channel_id=1, source_target_pairs={{0,2},{1,3},{2,0},{3,1},{4,6},{5,7},{6,4},{7,5},{8,10},{9,11},{10,... | collective-permute-start | bytes 1572872 | tf_op jit(solution)/shard_map/ppermute | solution.py:514
  386.0 16.8 %collective-permute-start.48 = (bf16[2,256,512]{2,1,0:T(8,128)(2,1)S(1)}, bf16[2,256,512]{2,1,0:T(8,128)(2,1)S(1)}, u32[]{:S(2)}, u32[]{:S(2)}) collective-permute-start(bf16[2,256,512]{2,1,0:T(8,128)(2,1)S(1)} %multiply_convert_fusion.4), channel_id=1, source_target_pairs={{0,1},{1,0},{2,3},{3,2},{4,5},{5,4},{6,7},{7,6},{8,9},{9,8},{10,11... | collective-permute-start | bytes 1572872 | tf_op jit(solution)/shard_map/ppermute | solution.py:514
  405.7 60.6 %collective-permute-start.52 = (bf16[512,1024]{1,0:T(8,128)(2,1)}, bf16[512,1024]{1,0:T(8,128)(2,1)}, u32[]{:S(2)}, u32[]{:S(2)}) collective-permute-start(bf16[512,1024]{1,0:T(8,128)(2,1)} %pad_maximum_fusion.8), channel_id=1, source_target_pairs={{0,4},{4,0},{8,12},{12,8},{16,20},{20,16},{24,28},{28,24},{1,5},{5... | collective-permute-start | bytes 3145736 | tf_op jit(solution)/shard_map/ppermute | solution.py:514
  422.7 23.2 %collective-permute-start.49 = (bf16[2,32,1024]{2,1,0:T(8,128)(2,1)S(1)}, bf16[2,32,1024]{2,1,0:T(8,128)(2,1)S(1)}, u32[]{:S(2)}, u32[]{:S(2)}) collective-permute-start(bf16[2,32,1024]{2,1,0:T(8,128)(2,1)S(1)} %pad_maximum_fusion.17), channel_id=1, source_target_pairs={{4,0},{8,4},{12,8},{16,12},{20,16},{24,20},{28,24},{5,1},{9,5},{13... | collective-permute-start | bytes 393224 | tf_op jit(solution)/shard_map/ppermute | solution.py:509
  446.0 13.0 %collective-permute-start.50 = (bf16[2,32,1024]{2,1,0:T(8,128)(2,1)S(1)}, bf16[2,32,1024]{2,1,0:T(8,128)(2,1)S(1)}, u32[]{:S(2)}, u32[]{:S(2)}) collective-permute-start(bf16[2,32,1024]{2,1,0:T(8,128)(2,1)S(1)} %pad_maximum_fusion.18), channel_id=1, source_target_pairs={{8,0},{12,4},{16,8},{20,12},{24,16},{28,20},{9,1},{13,5},{17,9},{2... | collective-permute-start | bytes 393224 | tf_op jit(solution)/shard_map/ppermute | solution.py:509
  467.1 43.4 %collective-permute-start.53 = (bf16[512,1024]{1,0:T(8,128)(2,1)}, bf16[512,1024]{1,0:T(8,128)(2,1)}, u32[]{:S(2)}, u32[]{:S(2)}) collective-permute-start(bf16[512,1024]{1,0:T(8,128)(2,1)} %bitcast.328), channel_id=1, source_target_pairs={{0,4},{4,0},{8,12},{12,8},{16,20},{20,16},{24,28},{28,24},{1,5},{5... | collective-permute-start | bytes 3145736 | tf_op jit(solution)/shard_map/ppermute | solution.py:514
  470.7 209.4 %reduce-scatter.6.cloned.1.call-start = ((), (), s32[]{:S(2)}) async-start(), calls=%async_computation.4 | async-start | bytes 5242880 | tf_op jit(solution)/shard_map/reduce_scatter | solution.py:710
  517.9 12.0 %collective-permute-start.55 = (bf16[2,256,160]{2,1,0:T(8,128)(2,1)S(1)}, bf16[2,256,160]{2,1,0:T(8,128)(2,1)}, u32[]{:S(2)}, u32[]{:S(2)}) collective-permute-start(bf16[2,256,160]{2,1,0:T(8,128)(2,1)S(1)} %fusion.98), channel_id=1, source_target_pairs={{0,2},{1,3},{2,0},{3,1},{4,6},{5,7},{6,4},{7,5},{8,10},{9,11},{10,... | collective-permute-start | bytes 491528 | tf_op jit(solution)/shard_map/ppermute | solution.py:514
  551.6 12.1 %collective-permute-start.57 = (bf16[256,1024]{1,0:T(8,128)(2,1)S(1)}, bf16[256,1024]{1,0:T(8,128)(2,1)S(1)}, u32[]{:S(2)}, u32[]{:S(2)}) collective-permute-start(bf16[256,1024]{1,0:T(8,128)(2,1)S(1)} %get-tuple-element.301), channel_id=1, source_target_pairs={{0,4},{4,0},{8,12},{12,8},{16,20},{20,16},{24,28},{28,24},{1,5},{5... | collective-permute-start | bytes 1572872 | tf_op jit(solution)/shard_map/ppermute | solution.py:514
  569.1 17.4 %collective-permute-start.61 = (bf16[256,1024]{1,0:T(8,128)(2,1)S(1)}, bf16[256,1024]{1,0:T(8,128)(2,1)S(1)}, u32[]{:S(2)}, u32[]{:S(2)}) collective-permute-start(bf16[256,1024]{1,0:T(8,128)(2,1)S(1)} %copy-done.86), channel_id=1, source_target_pairs={{0,4},{4,0},{8,12},{12,8},{16,20},{20,16},{24,28},{28,24},{1,5},{5... | collective-permute-start | bytes 1572872 | tf_op jit(solution)/shard_map/ppermute | solution.py:514
  572.0 15.3 %collective-permute-start.60 = (bf16[2,256,512]{2,1,0:T(8,128)(2,1)S(1)}, bf16[2,256,512]{2,1,0:T(8,128)(2,1)S(1)}, u32[]{:S(2)}, u32[]{:S(2)}) collective-permute-start(bf16[2,256,512]{2,1,0:T(8,128)(2,1)S(1)} %select_convert_fusion.2), channel_id=1, source_target_pairs={{0,2},{1,3},{2,0},{3,1},{4,6},{5,7},{6,4},{7,5},{8,10},{9,11},{10,... | collective-permute-start | bytes 1572872 | tf_op jit(solution)/shard_map/ppermute | solution.py:514
  573.1 13.3 %collective-permute-start.63 = (f32[2,256]{1,0:T(2,128)S(1)}, f32[2,256]{1,0:T(2,128)S(1)}, u32[]{:S(2)}, u32[]{:S(2)}) collective-permute-start(f32[2,256]{1,0:T(2,128)S(1)} %add.606), channel_id=1, source_target_pairs={{0,2},{1,3},{2,0},{3,1},{4,6},{5,7},{6,4},{7,5},{8,10},{9,11},{10,... | collective-permute-start | bytes 6152 | tf_op jit(solution)/shard_map/ppermute | solution.py:514
  592.9 40.6 %collective-permute-start.67 = (bf16[336,1024]{1,0:T(8,128)(2,1)S(1)}, bf16[336,1024]{1,0:T(8,128)(2,1)S(1)}, u32[]{:S(2)}, u32[]{:S(2)}) collective-permute-start(bf16[336,1024]{1,0:T(8,128)(2,1)S(1)} %pad_maximum_fusion.10), channel_id=1, source_target_pairs={{0,4},{4,0},{8,12},{12,8},{16,20},{20,16},{24,28},{28,24},{1,5},{5... | collective-permute-start | bytes 2064392 | tf_op jit(solution)/shard_map/ppermute | solution.py:514
  602.4 25.6 %collective-permute-start.68 = (bf16[256,1024]{1,0:T(8,128)(2,1)S(1)}, bf16[256,1024]{1,0:T(8,128)(2,1)S(1)}, u32[]{:S(2)}, u32[]{:S(2)}) collective-permute-start(bf16[256,1024]{1,0:T(8,128)(2,1)S(1)} %get-tuple-element.250), channel_id=1, source_target_pairs={{0,8},{4,12},{1,9},{5,13},{2,10},{6,14},{3,11},{7,15}} | collective-permute-start | bytes 1572872 | tf_op jit(solution)/shard_map/ppermute | solution.py:732
  604.8 23.2 %collective-permute-start.69 = (bf16[256,1024]{1,0:T(8,128)(2,1)S(1)}, bf16[256,1024]{1,0:T(8,128)(2,1)S(1)}, u32[]{:S(2)}, u32[]{:S(2)}) collective-permute-start(bf16[256,1024]{1,0:T(8,128)(2,1)S(1)} %get-tuple-element.249), channel_id=1, source_target_pairs={{24,16},{28,20},{25,17},{29,21},{26,18},{30,22},{27,19},{31,23}} | collective-permute-start | bytes 1572872 | tf_op jit(solution)/shard_map/ppermute | solution.py:733
  610.4 25.3 %collective-permute-start.64 = (bf16[2,256,512]{2,1,0:T(8,128)(2,1)S(1)}, bf16[2,256,512]{2,1,0:T(8,128)(2,1)S(1)}, u32[]{:S(2)}, u32[]{:S(2)}) collective-permute-start(bf16[2,256,512]{2,1,0:T(8,128)(2,1)S(1)} %get-tuple-element.252), channel_id=1, source_target_pairs={{0,1},{1,0},{2,3},{3,2},{4,5},{5,4},{6,7},{7,6},{8,9},{9,8},{10,11... | collective-permute-start | bytes 1572872 | tf_op jit(solution)/shard_map/ppermute | solution.py:514
  610.5 25.2 %collective-permute-start.65 = (bf16[2,256,512]{2,1,0:T(8,128)(2,1)S(1)}, bf16[2,256,512]{2,1,0:T(8,128)(2,1)S(1)}, u32[]{:S(2)}, u32[]{:S(2)}) collective-permute-start(bf16[2,256,512]{2,1,0:T(8,128)(2,1)S(1)} %get-tuple-element.251), channel_id=1, source_target_pairs={{0,1},{1,0},{2,3},{3,2},{4,5},{5,4},{6,7},{7,6},{8,9},{9,8},{10,11... | collective-permute-start | bytes 1572872 | tf_op jit(solution)/shard_map/ppermute | solution.py:514
  628.4 16.8 %collective-permute-start.71 = (bf16[256,1024]{1,0:T(8,128)(2,1)S(1)}, bf16[256,1024]{1,0:T(8,128)(2,1)S(1)}, u32[]{:S(2)}, u32[]{:S(2)}) collective-permute-start(bf16[256,1024]{1,0:T(8,128)(2,1)S(1)} %get-tuple-element.248), channel_id=1, source_target_pairs={{0,8},{4,12},{8,16},{12,20},{1,9},{5,13},{9,17},{13,21},{2,10},{6,... | collective-permute-start | bytes 1572872 | tf_op jit(solution)/shard_map/ppermute | solution.py:732
  632.8 12.3 %collective-permute-start.72 = (bf16[256,1024]{1,0:T(8,128)(2,1)S(1)}, bf16[256,1024]{1,0:T(8,128)(2,1)S(1)}, u32[]{:S(2)}, u32[]{:S(2)}) collective-permute-start(bf16[256,1024]{1,0:T(8,128)(2,1)S(1)} %get-tuple-element.247), channel_id=1, source_target_pairs={{16,8},{20,12},{24,16},{28,20},{17,9},{21,13},{25,17},{29,21},{18,... | collective-permute-start | bytes 1572872 | tf_op jit(solution)/shard_map/ppermute | solution.py:733
  633.9 20.4 %collective-permute-start.70 = (bf16[208,1024]{1,0:T(8,128)(2,1)S(1)}, bf16[208,1024]{1,0:T(8,128)(2,1)S(1)}, u32[]{:S(2)}, u32[]{:S(2)}) collective-permute-start(bf16[208,1024]{1,0:T(8,128)(2,1)S(1)} %pad_maximum_fusion.11), channel_id=1, source_target_pairs={{0,8},{4,12},{8,0},{12,4},{16,24},{20,28},{24,16},{28,20},{1,9},{5... | collective-permute-start | bytes 1277960 | tf_op jit(solution)/shard_map/ppermute | solution.py:514
  636.1 22.9 %collective-permute-start.66 = (bf16[2,256,512]{2,1,0:T(8,128)(2,1)S(1)}, bf16[2,256,512]{2,1,0:T(8,128)(2,1)S(1)}, u32[]{:S(2)}, u32[]{:S(2)}) collective-permute-start(bf16[2,256,512]{2,1,0:T(8,128)(2,1)S(1)} %select_convert_fusion.1), channel_id=1, source_target_pairs={{0,2},{1,3},{2,0},{3,1},{4,6},{5,7},{6,4},{7,5},{8,10},{9,11},{10,... | collective-permute-start | bytes 1572872 | tf_op jit(solution)/shard_map/ppermute | solution.py:514
  645.6 19.9 %collective-permute-start.74 = (bf16[256,1024]{1,0:T(8,128)(2,1)S(1)}, bf16[256,1024]{1,0:T(8,128)(2,1)S(1)}, u32[]{:S(2)}, u32[]{:S(2)}) collective-permute-start(bf16[256,1024]{1,0:T(8,128)(2,1)S(1)} %get-tuple-element.246), channel_id=1, source_target_pairs={{0,8},{4,12},{8,16},{12,20},{16,24},{20,28},{1,9},{5,13},{9,17},{1... | collective-permute-start | bytes 1572872 | tf_op jit(solution)/shard_map/ppermute | solution.py:732
  650.4 16.0 %collective-permute-start.75 = (bf16[256,1024]{1,0:T(8,128)(2,1)S(1)}, bf16[256,1024]{1,0:T(8,128)(2,1)S(1)}, u32[]{:S(2)}, u32[]{:S(2)}) collective-permute-start(bf16[256,1024]{1,0:T(8,128)(2,1)S(1)} %get-tuple-element.245), channel_id=1, source_target_pairs={{8,0},{12,4},{16,8},{20,12},{24,16},{28,20},{9,1},{13,5},{17,9},{2... | collective-permute-start | bytes 1572872 | tf_op jit(solution)/shard_map/ppermute | solution.py:733
  654.6 21.0 %collective-permute-start.73 = (bf16[144,1024]{1,0:T(8,128)(2,1)S(1)}, bf16[144,1024]{1,0:T(8,128)(2,1)S(1)}, u32[]{:S(2)}, u32[]{:S(2)}) collective-permute-start(bf16[144,1024]{1,0:T(8,128)(2,1)S(1)} %pad_maximum_fusion.12), channel_id=1, source_target_pairs={{0,16},{4,20},{8,24},{12,28},{16,0},{20,4},{24,8},{28,12},{1,17},{... | collective-permute-start | bytes 884744 | tf_op jit(solution)/shard_map/ppermute | solution.py:514
  (191 other events, 2991.3 us)
Sparse Core Ops, SparseCore 0:
  282.4 178.8 reduce-scatter.3
Sparse Core Ops, SparseCore 1:
  470.8 42.6 reduce-scatter.7
  544.8 86.4 reduce-scatter.5
